TPU v7x, 512 devices: a whole 4x4x16 slice. The times are simulated.
512 devices in a mesh: ctx: 32 (over x_lo, z), kv: 8 (over x_hi, y), pb: 2 (over core).
Axes of the slice: x: 4 (x_hi: 2, x_lo: 2; x = x_hi * 2 + x_lo), y: 4, z: 16, core: 2. Of those that a mesh axis runs over, the one named last changes fastest.
Arguments:
- queries: bfloat16 [8, 8, 256, 128], P('kv', None, 'pb'), may hold values from -24 to 24
- cache_keys: bfloat16 [8, 131072, 128], P('kv', 'ctx'), may hold values from -6 to 6
- cache_values: bfloat16 [8, 131072, 128], P('kv', 'ctx'), may hold values from -6 to 6
- sel_index: int32 [8, 2048], P('kv', 'ctx'), may hold values from 0 to 131071, as said below
Outputs:
- gram: float32 [8, 2048, 2048], P('kv', ('ctx', 'pb'))
- value_rhs: float32 [8, 2048, 128], P('kv', ('ctx', 'pb'))
- mass_gap: float32 [8, 8, 256], P('kv', None, 'pb')
Inputs may be any that keep to these rules, and one draw needn't show every extreme that they name: `sel_index`: for every KV head, entries k * 64 to (k + 1) * 64 - 1 are distinct positions of context block k (from k * 4096 to (k + 1) * 4096 - 1), in increasing order.
All inputs are finite; a program needn't handle non-finite values.
Results may differ from a plain program's by a relative error of at most 0.0016.
Values may be sent and summed in bfloat16 or wider, within the bound.
No kernel may reach another device: no remote copies, remote signals or barrier semaphores. Data moves between devices by JAX's collectives and lax.ppermute only.
A program may use at most 64 MiB of HBM per device.

v0:
```python
import math

import jax
import jax.numpy as jnp
from jax import lax
from jax.sharding import PartitionSpec as P

eps = 1e-06


def sent_to_all(x, axis):
    peers = lax.axis_size(axis)
    return lax.all_to_all(jnp.broadcast_to(x[None], (peers, *x.shape)), axis, 0, 0, tiled=True)


def of_everyone(x, axis):
    return sent_to_all(x, axis).max(axis=0)


def in_blocks(x, dim, peers):
    before, after = (x.shape[:dim], x.shape[dim + 1 :])
    return jnp.moveaxis(x.reshape(*before, peers, -1, *after), dim, 0)


def sum_at_owner(x, axis, dim):
    pieces = in_blocks(x, dim, lax.axis_size(axis))
    arrived = lax.all_to_all(pieces, axis, split_axis=0, concat_axis=0, tiled=True)
    return arrived.sum(axis=0)


def sent_together(arrays, axis, dim, along):
    widths = [math.prod(a.shape[along:]) for a in arrays]
    both = jnp.concatenate(
        [a.reshape(*a.shape[:along], w) for a, w in zip(arrays, widths)], axis=along
    )
    out = sum_at_owner(both, axis, dim)
    pieces = jnp.split(out, [sum(widths[:k]) for k in range(1, len(widths))], axis=along)
    return tuple((b.reshape(*out.shape[:along], *a.shape[along:]) for a, b in zip(arrays, pieces)))


def joined_along(pieces, dim):
    shape = list(pieces.shape[1:])
    shape[dim] *= pieces.shape[0]
    return jnp.moveaxis(pieces, 0, dim).reshape(shape)


def gathered_copies(x, axis, dim):
    return joined_along(sent_to_all(x, axis), dim)


def in_one_piece(arrays, axis, dim, along):
    ends, at = ([], 0)
    for a in arrays[:-1]:
        at += a.shape[along]
        ends.append(at)
    both = jnp.concatenate(arrays, axis=along)
    return tuple(jnp.split(sum_at_owner(both, axis, dim), ends, axis=along))


def normalize(summed, total):
    target = summed / total[:, None]
    return (target * lax.rsqrt(jnp.mean(target * target, axis=1, keepdims=True) + eps)).astype(
        jnp.bfloat16
    )


def shards(queries, cache_keys, cache_values, sel_index):
    heads = queries.shape[1]
    rows_dev = queries.shape[2]
    width = queries.shape[3]
    scale = width ** (-0.5)
    rows = queries[0].reshape(-1, width)
    row_count = rows.shape[0]
    keys = cache_keys[0]
    values = cache_values[0]
    ctx_rows = keys.shape[0]
    sel_dev = sel_index.shape[1]
    ctx_count = lax.axis_size("ctx")
    position = lax.axis_index("ctx")
    sel_all = sel_dev * ctx_count
    total_rows = heads * rows_dev * lax.axis_size("pb")
    block_len = 512

    def attend(block_rows):
        scores = (
            jnp.einsum("rd,kd->rk", block_rows, keys, preferred_element_type=jnp.float32) * scale
        )
        block_max = jnp.max(scores, axis=1)
        expo = jnp.exp(scores - block_max[:, None])
        block_total = jnp.sum(expo, axis=1)
        block_out = jnp.dot(expo.astype(jnp.bfloat16), values, preferred_element_type=jnp.float32)
        return (block_max, block_total, block_out)

    local_max, local_total, local_out = lax.map(attend, rows.reshape(-1, block_len, width))
    local_max = local_max.reshape(row_count)
    local_total = local_total.reshape(row_count)
    local_out = local_out.reshape(row_count, width)
    top = of_everyone(local_max, "ctx")
    weight = jnp.exp(local_max - top)
    share_total, share_summed = sent_together(
        (weight * local_total, weight[:, None] * local_out), "ctx", 0, 1
    )
    share_len = row_count // ctx_count
    share_top = lax.dynamic_slice_in_dim(top, position * share_len, share_len, 0)
    share_y = normalize(share_summed, share_total)
    share_lse = share_top + jnp.log(share_total)
    target_y = gathered_copies(share_y, "ctx", 0)
    full_mass = gathered_copies(share_lse, "ctx", 0)
    local_pos = sel_index[0] - position * ctx_rows
    compact_local = jnp.take(keys, local_pos, axis=0)
    compact = gathered_copies(compact_local, "ctx", 0)
    cscores = jnp.einsum("rd,kd->rk", rows, compact, preferred_element_type=jnp.float32) * scale
    cmax = jnp.max(cscores, axis=1)
    cexp = jnp.exp(cscores - cmax[:, None])
    ctotal = jnp.sum(cexp, axis=1)
    feat = (sel_all * cexp / ctotal[:, None]).astype(jnp.bfloat16)
    own = lax.dynamic_slice_in_dim(feat, position * sel_dev, sel_dev, 1)
    gram_part = jnp.einsum("rk,rj->kj", own, feat, preferred_element_type=jnp.float32)
    rhs_part = jnp.einsum("rk,rd->kd", own, target_y, preferred_element_type=jnp.float32)
    inverse = 1.0 / total_rows
    gram, value_rhs = in_one_piece((gram_part * inverse, rhs_part * inverse), "pb", 0, 1)
    mass_gap = (full_mass - (cmax + jnp.log(ctotal))).reshape(heads, rows_dev)
    return (gram[None], value_rhs[None], mass_gap[None])


def solution(mesh):
    in_specs = (
        P("kv", None, "pb", None),
        P("kv", "ctx", None),
        P("kv", "ctx", None),
        P("kv", "ctx"),
    )
    out_specs = (P("kv", ("ctx", "pb"), None), P("kv", ("ctx", "pb"), None), P("kv", None, "pb"))
    return jax.shard_map(shards, mesh=mesh, in_specs=in_specs, out_specs=out_specs, check_vma=False)
```

profile of v0, /device:TPU:1, one launch (start us, length us, event | category | flops | bytes accessed | tf_op | source)
XLA Modules:
  0.0 191.2 jit_solution(3135404709743869900)
XLA Ops:
  0.7 11.6 %while.14 = (s32[]{:T(128)}, f32[2,512]{1,0:T(2,128)S(1)}, f32[2,512]{1,0:T(2,128)S(1)}, f32[2,512,128]{2,1,0:T(8,128)S(1)}, bf16[2,512,128]{2,1,0:T(8,128)(2,1)...) while((s32[]{:T(128)}, f32[2,512]{1,0:T(2,128)S(1)}, ...), condition=%wide.region_5.6_spmd, body=%wide.region_2.5_spmd.sunk | while | flops 1090518016 | bytes 31867024 | solution.py:94
  0.7 2.7 %multiply_reduce_fusion.4 = (f32[512]{0:T(512)S(1)}, f32[512,4096]{1,0:T(8,128)S(1)}) fusion(bf16[4096,128]{1,0:T(8,128)(2,1)} %get-tuple-element.133, bf16[2,512,128]{2,1,0:T(8,128)(2,1)} %get-tuple-element.132, s32[]{:T(128)S(6)} %copy.26), kind=kOutput, calls=%fused_computation.2.clone.1 | convolution fusion | flops 541064704 | bytes 9570308 | tf_op jit(solution)/shard_map/while/body/eval_jaxpr/rd,kd->rk/dot_general | solution.py:86
  3.4 1.5 fusion.35
  4.9 1.5 fusion.36
  6.5 2.7 %multiply_reduce_fusion.4 = (f32[512]{0:T(512)S(1)}, f32[512,4096]{1,0:T(8,128)S(1)}) fusion(bf16[4096,128]{1,0:T(8,128)(2,1)} %get-tuple-element.133, bf16[2,512,128]{2,1,0:T(8,128)(2,1)} %get-tuple-element.132, s32[]{:T(128)S(6)} %copy.26), kind=kOutput, calls=%fused_computation.2.clone.1 | convolution fusion | flops 541064704 | bytes 9570308 | tf_op jit(solution)/shard_map/while/body/eval_jaxpr/rd,kd->rk/dot_general | solution.py:86
  9.2 1.5 fusion.35
  10.7 1.5 fusion.36
  13.0 17.0 %all-to-all-start.1 = ((f32[32,1,1024]{2,1,0:T(1,128)}), f32[32,1,1024]{2,1,0:T(1,128)S(1)}, u32[]{:S(2)}, u32[]{:S(2)}) async-start(f32[32,1,1024]{2,1,0:T(1,128)} %broadcast_in_dim.65), calls=%async_computation.1 | async-start | bytes 262144 | tf_op jit(solution)/shard_map/all_to_all | solution.py:13
  30.0 2.0 %gather_fusion = bf16[64,128]{1,0:T(8,128)(2,1)S(1)} fusion(bf16[4096,128]{1,0:T(8,128)(2,1)} %get-tuple-element.137, s32[1024]{0:T(1024)S(1)} %pad_clamp_fusion), kind=kCustom, calls=%fused_computation | custom fusion | bytes 33024 | tf_op jit(solution)/shard_map/jit(_take)/gather | solution.py:110
  32.1 12.5 %all-to-all-done.1 = f32[32,1,1024]{2,1,0:T(1,128)S(1)} async-done(((f32[32,1,1024]{2,1,0:T(1,128)}), f32[32,1,1024]{2,1,0:T(1,128)S(1)}, u32[]{:S(2)}, u32[]{:S(2)}) %all-to-all-start.1) | async-done | bytes 131104 | tf_op jit(solution)/shard_map/all_to_all | solution.py:13
  45.5 4.7 %all-to-all-start = ((bf16[32,64,128]{2,1,0:T(8,128)(2,1)}), bf16[32,64,128]{2,1,0:T(8,128)(2,1)S(1)}, u32[]{:S(2)}, u32[]{:S(2)}) async-start(bf16[32,64,128]{2,1,0:T(8,128)(2,1)} %broadcast_in_dim.62), calls=%async_computation | async-start | bytes 1048576 | tf_op jit(solution)/shard_map/all_to_all | solution.py:13
  51.2 1.4 pad_maximum_fusion
  52.6 25.8 %all-to-all-done = bf16[32,64,128]{2,1,0:T(8,128)(2,1)S(1)} async-done(((bf16[32,64,128]{2,1,0:T(8,128)(2,1)}), bf16[32,64,128]{2,1,0:T(8,128)(2,1)S(1)}, u32[]{:S(2)}, u32[]{:S(2)}) %all-to-all-start) | async-done | bytes 524320 | tf_op jit(solution)/shard_map/all_to_all | solution.py:13
  78.5 6.9 %all-to-all-start.2 = ((f32[32,32,129]{2,1,0:T(8,128)}), f32[32,32,129]{2,1,0:T(8,128)S(1)}, u32[]{:S(2)}, u32[]{:S(2)}) async-start(f32[32,32,129]{2,1,0:T(8,128)} %pad_maximum_fusion), calls=%async_computation.2 | async-start | bytes 2097152 | tf_op jit(solution)/shard_map/all_to_all | solution.py:27
  86.7 3.2 %copy-done = f32[2048,1024]{1,0:T(8,128)} copy-done((f32[2048,1024]{1,0:T(8,128)}, f32[2048,1024]{1,0:T(8,128)S(1)}, u32[]{:S(2)}) %copy-start) | copy-done | bytes 8388632
  89.9 1.4 fusion.15
  91.3 44.0 %all-to-all-done.2 = f32[32,32,129]{2,1,0:T(8,128)S(1)} async-done(((f32[32,32,129]{2,1,0:T(8,128)}), f32[32,32,129]{2,1,0:T(8,128)S(1)}, u32[]{:S(2)}, u32[]{:S(2)}) %all-to-all-start.2) | async-done | bytes 528416 | tf_op jit(solution)/shard_map/all_to_all | solution.py:27
  136.4 8.4 %all-to-all-start.5 = ((f32[32,1,32]{2,1,0:T(1,128)}), f32[32,1,32]{2,1,0:T(1,128)S(1)}, u32[]{:S(2)}, u32[]{:S(2)}) async-start(f32[32,1,32]{2,1,0:T(1,128)} %broadcast_in_dim.69), calls=%async_computation.5 | async-start | bytes 32768 | tf_op jit(solution)/shard_map/all_to_all | solution.py:13
  144.9 12.1 %all-to-all-done.5 = f32[32,1,32]{2,1,0:T(1,128)S(1)} async-done(((f32[32,1,32]{2,1,0:T(1,128)}), f32[32,1,32]{2,1,0:T(1,128)S(1)}, u32[]{:S(2)}, u32[]{:S(2)}) %all-to-all-start.5) | async-done | bytes 4128 | tf_op jit(solution)/shard_map/all_to_all | solution.py:13
  157.7 3.9 %all-to-all-start.3 = ((bf16[32,32,128]{2,1,0:T(8,128)(2,1)}), bf16[32,32,128]{2,1,0:T(8,128)(2,1)S(1)}, u32[]{:S(2)}, u32[]{:S(2)}) async-start(bf16[32,32,128]{2,1,0:T(8,128)(2,1)} %broadcast_in_dim.66), calls=%async_computation.3 | async-start | bytes 524288 | tf_op jit(solution)/shard_map/all_to_all | solution.py:13
  161.6 4.4 %divide_convert_fusion = bf16[2048,1024]{1,0:T(8,128)(2,1)S(1)} fusion(f32[2048,1024]{1,0:T(8,128)} %copy-done, f32[1024]{0:T(1024)S(1)} %fusion.15, f32[1024]{0:T(1024)S(1)} %get-tuple-element.61), kind=kLoop, calls=%fused_computation.13 | loop fusion | flops 10485760 | bytes 12591104 | tf_op jit(solution)/shard_map/convert_element_type | solution.py:116
  166.0 1.9 %copy-done.2 = bf16[2048,1024]{1,0:T(8,128)(2,1)} copy-done((bf16[2048,1024]{1,0:T(8,128)(2,1)}, bf16[2048,1024]{1,0:T(8,128)(2,1)S(1)}, u32[]{:S(2)}) %copy-start.2) | copy-done | bytes 4194328
  171.2 8.4 %all-to-all-done.3 = bf16[32,32,128]{2,1,0:T(8,128)(2,1)S(1)} async-done(((bf16[32,32,128]{2,1,0:T(8,128)(2,1)}), bf16[32,32,128]{2,1,0:T(8,128)(2,1)S(1)}, u32[]{:S(2)}, u32[]{:S(2)}) %all-to-all-start.3) | async-done | bytes 262176 | tf_op jit(solution)/shard_map/all_to_all | solution.py:13
  180.7 9.1 %all_to_all.32 = f32[2,32,2176]{2,1,0:T(8,128)S(1)} all-to-all(f32[2,32,2176]{2,1,0:T(8,128)S(1)} %bitcast.57), channel_id=1, replica_groups=mesh['ctx'=32,'kv'=8,'pb'=2] {'pb'}, dimensions={0} | all-to-all | bytes 1114112 | tf_op jit(solution)/shard_map/all_to_all | solution.py:27
  (53 shorter events, 11.8 us)
Async XLA Ops:
  0.7 29.3 %copy-start.4 = (s32[1,64]{1,0:T(1,128)S(1)}, s32[1,64]{1,0:T(1,128)}, u32[]{:S(2)}) copy-start(s32[1,64]{1,0:T(1,128)} %param.9) | copy-start | bytes 772
  0.7 4.2 %copy-start.1 = (bf16[4096,128]{1,0:T(8,128)(2,1)S(1)}, bf16[4096,128]{1,0:T(8,128)(2,1)}, u32[]{:S(2)}) copy-start(bf16[4096,128]{1,0:T(8,128)(2,1)} %get-tuple-element.134) | copy-start | bytes 3145732 | tf_op jit(solution)/shard_map/while
  6.5 4.2 %copy-start.1 = (bf16[4096,128]{1,0:T(8,128)(2,1)S(1)}, bf16[4096,128]{1,0:T(8,128)(2,1)}, u32[]{:S(2)}) copy-start(bf16[4096,128]{1,0:T(8,128)(2,1)} %get-tuple-element.134) | copy-start | bytes 3145732 | tf_op jit(solution)/shard_map/while
  12.3 73.1 %copy-start.3 = (bf16[2,512,128]{2,1,0:T(8,128)(2,1)S(1)}, bf16[2,512,128]{2,1,0:T(8,128)(2,1)}, u32[]{:S(2)}) copy-start(bf16[2,512,128]{2,1,0:T(8,128)(2,1)} %get-tuple-element.140) | copy-start | bytes 786436
  13.0 31.6 %all-to-all-start.1 = ((f32[32,1,1024]{2,1,0:T(1,128)}), f32[32,1,1024]{2,1,0:T(1,128)S(1)}, u32[]{:S(2)}, u32[]{:S(2)}) async-start(f32[32,1,1024]{2,1,0:T(1,128)} %broadcast_in_dim.65), calls=%async_computation.1 | async-start | bytes 262144 | tf_op jit(solution)/shard_map/all_to_all | solution.py:13
  45.5 33.0 %all-to-all-start = ((bf16[32,64,128]{2,1,0:T(8,128)(2,1)}), bf16[32,64,128]{2,1,0:T(8,128)(2,1)S(1)}, u32[]{:S(2)}, u32[]{:S(2)}) async-start(bf16[32,64,128]{2,1,0:T(8,128)(2,1)} %broadcast_in_dim.62), calls=%async_computation | async-start | bytes 1048576 | tf_op jit(solution)/shard_map/all_to_all | solution.py:13
  78.5 56.9 %all-to-all-start.2 = ((f32[32,32,129]{2,1,0:T(8,128)}), f32[32,32,129]{2,1,0:T(8,128)S(1)}, u32[]{:S(2)}, u32[]{:S(2)}) async-start(f32[32,32,129]{2,1,0:T(8,128)} %pad_maximum_fusion), calls=%async_computation.2 | async-start | bytes 2097152 | tf_op jit(solution)/shard_map/all_to_all | solution.py:27
  86.7 3.2 %copy-start = (f32[2048,1024]{1,0:T(8,128)}, f32[2048,1024]{1,0:T(8,128)S(1)}, u32[]{:S(2)}) copy-start(f32[2048,1024]{1,0:T(8,128)S(1)} %get-tuple-element.62) | copy-start | bytes 25165828
  136.4 20.6 %all-to-all-start.5 = ((f32[32,1,32]{2,1,0:T(1,128)}), f32[32,1,32]{2,1,0:T(1,128)S(1)}, u32[]{:S(2)}, u32[]{:S(2)}) async-start(f32[32,1,32]{2,1,0:T(1,128)} %broadcast_in_dim.69), calls=%async_computation.5 | async-start | bytes 32768 | tf_op jit(solution)/shard_map/all_to_all | solution.py:13
  157.7 21.9 %all-to-all-start.3 = ((bf16[32,32,128]{2,1,0:T(8,128)(2,1)}), bf16[32,32,128]{2,1,0:T(8,128)(2,1)S(1)}, u32[]{:S(2)}, u32[]{:S(2)}) async-start(bf16[32,32,128]{2,1,0:T(8,128)(2,1)} %broadcast_in_dim.66), calls=%async_computation.3 | async-start | bytes 524288 | tf_op jit(solution)/shard_map/all_to_all | solution.py:13
  166.0 1.9 %copy-start.2 = (bf16[2048,1024]{1,0:T(8,128)(2,1)}, bf16[2048,1024]{1,0:T(8,128)(2,1)S(1)}, u32[]{:S(2)}) copy-start(bf16[2048,1024]{1,0:T(8,128)(2,1)S(1)} %divide_convert_fusion) | copy-start | bytes 12582916
where the time goes:
time: 192 us; the launch traced here: 191 us
  waiting for transfers between devices  103 us (54%)
  starting transfers between devices  40.9 us (21%)
  local copies, waits for them, and re-layouts  13 us (7%)
  other arithmetic  12.5 us (7%)
  matrix products  12.1 us (6%)
  blocking collectives  9.12 us (5%)
    all_to_all x4, waiting for transfers between devices, sent_to_all(): lax.all_to_all(jnp.broadcast_to(x[None], (peers, *x.shape)), axis, 0, 0,...  58.8 us
    all_to_all x1, waiting for transfers between devices, sum_at_owner(): lax.all_to_all(pieces, axis, split_axis=0, concat_axis=0, tiled=True)  44 us
    all_to_all x4, starting transfers between devices, sent_to_all(): lax.all_to_all(jnp.broadcast_to(x[None], (peers, *x.shape)), axis, 0, 0,...  33.9 us
    all_to_all x1, blocking collectives, sum_at_owner(): lax.all_to_all(pieces, axis, split_axis=0, concat_axis=0, tiled=True)  9.12 us
    all_to_all x1, starting transfers between devices, sum_at_owner(): lax.all_to_all(pieces, axis, split_axis=0, concat_axis=0, tiled=True)  6.95 us
    dot_general x2, matrix products, attend(): jnp.einsum('rd,kd->rk', block_rows, keys, preferred_element_type=jnp.floa...  5.42 us
    unnamed x9, local copies, waits for them, and re-layouts  5.15 us
    convert_element_type x1, other arithmetic, shards(): feat = (sel_all * cexp / ctotal[:, None]).astype(jnp.bfloat16)  4.39 us
  transfers between devices with their start and end apart: 5, of which 5 were waited for; matrix products, arithmetic and copies ran while one was open for 8% of the time, Pallas kernels for 0%

commit v1 on v0

v1 whole, which is shorter than its diff:
```python
import functools
import math

import jax
import jax.numpy as jnp
from jax import lax
from jax.experimental import pallas as pl
from jax.experimental.pallas import tpu as pltpu
from jax.sharding import PartitionSpec as P

eps = 1e-06
LOG2E = math.log2(math.e)
F32, BF16 = jnp.float32, jnp.bfloat16
VMEM = pl.BlockSpec(memory_space=pltpu.VMEM)
NT = (((1,), (1,)), ((), ()))


def call(name, body, outs, ins, scratch=(), after=(), flops=0, exps=0, moved=0, limit=48):
    count, skip = len(ins), len(after)

    def ordered(*refs):
        body(*refs[:count], *refs[count + skip :])

    return pl.pallas_call(
        ordered,
        name=name,
        out_shape=[jax.ShapeDtypeStruct(s, d) for s, d in outs],
        in_specs=[VMEM] * count + [pl.BlockSpec(memory_space=pl.ANY)] * skip,
        out_specs=[VMEM] * len(outs),
        scratch_shapes=list(scratch),
        compiler_params=pltpu.CompilerParams(vmem_limit_bytes=limit << 20),
        cost_estimate=pl.CostEstimate(flops=flops, transcendentals=exps, bytes_accessed=moved),
    )(*ins, *after)


def split3(x):
    hi = x.astype(BF16)
    rest = x - hi.astype(F32)
    mid = rest.astype(BF16)
    low = (rest - mid.astype(F32)).astype(BF16)
    return hi, mid, low


def joined3(a, b, c):
    return (a.astype(F32) + b.astype(F32)) + c.astype(F32)


def pick_body(sel_ref, keys_ref, out_ref):
    peers, half, _ = out_ref.shape
    count = sel_ref.shape[1]
    tokens = keys_ref.shape[0]
    base = lax.axis_index("ctx") * tokens
    first = lax.axis_index("pb") * half
    row = lax.broadcasted_iota(jnp.int32, (half, count), 0) + first
    lane = lax.broadcasted_iota(jnp.int32, (half, count), 1)
    sel = jnp.broadcast_to((sel_ref[...] - base).astype(F32), (half, count))
    col = jnp.sum(jnp.where(row == lane, sel, 0.0), axis=1, keepdims=True).astype(jnp.int32)
    step = 512
    acc = jnp.zeros((half, keys_ref.shape[1]), F32)
    for k in range(0, tokens, step):
        at = lax.broadcasted_iota(jnp.int32, (half, step), 1) + k
        hot = (at == col).astype(F32).astype(BF16)
        acc += jnp.dot(hot, keys_ref[k : k + step, :], preferred_element_type=F32)
    mine = acc.astype(BF16)
    for p in range(peers):
        out_ref[p] = mine


def attend_body(rt, q_ref, k_ref, v_ref, out_ref, s_ref, m_ref):
    rows, width = q_ref.shape
    tokens = k_ref.shape[0]
    tiles = rows // rt
    step = 512
    c = LOG2E * width**-0.5
    share = rows // out_ref.shape[0]

    def scores(t, slot, k):
        q = q_ref[pl.ds(pl.multiple_of(t * rt, rt), rt), :]
        s = lax.dot_general(q, k_ref[k : k + step, :], NT, preferred_element_type=F32)
        s_ref[slot, :, k : k + step] = s
        mx = s[:, :128]
        for j in range(128, step, 128):
            mx = jnp.maximum(mx, s[:, j : j + 128])
        return mx

    def weighed(slot, k, mc, acc):
        l, o = acc
        p = jnp.exp2(s_ref[slot, :, k : k + step] * c - mc)
        for j in range(0, step, 128):
            l = l + p[:, j : j + 128]
        o = o + jnp.dot(p.astype(BF16), v_ref[k : k + step, :], preferred_element_type=F32)
        return l, o

    def close(t, mc, acc):
        l, o = acc
        total = jnp.sum(l, axis=1, keepdims=True)
        o = (o / total).astype(BF16)
        lse = (mc + jnp.log2(total)) * (1.0 / LOG2E)
        lanes = jnp.broadcast_to(lse, (rt, 128))
        for g in range(rt // 128):
            line = lanes[g * 128 : (g + 1) * 128, :].T[:16, :]
            hi, mid, low = split3(line)
            r = lax.broadcasted_iota(jnp.int32, (16, 128), 0)
            three = jnp.where(r == 0, hi.astype(F32), jnp.where(r == 1, mid.astype(F32), low.astype(F32)))
            three = three.astype(BF16)
            for j in range(128 // share):
                p = t * (rt // share) + g * (128 // share) + j
                out_ref[p, 0:share, :] = o[g * 128 + j * share : g * 128 + (j + 1) * share, :]
                out_ref[p, share : share + 16, :] = three

    def maxed(mx):
        return jnp.max(mx, axis=1, keepdims=True) * c

    def zero():
        return jnp.zeros((rt, 128), F32), jnp.zeros((rt, width), F32)

    mx = scores(0, 0, 0)
    for k in range(step, tokens, step):
        mx = jnp.maximum(mx, scores(0, 0, k))
    m_ref[...] = jnp.broadcast_to(maxed(mx), (rt, 128))

    def loop(t, carry):
        slot = t % 2
        mc = m_ref[:, :1]
        acc, mx = zero(), None
        for k in range(0, tokens, step):
            new = scores(t + 1, 1 - slot, k)
            mx = new if mx is None else jnp.maximum(mx, new)
            acc = weighed(slot, k, mc, acc)
        close(t, mc, acc)
        m_ref[...] = jnp.broadcast_to(maxed(mx), (rt, 128))
        return carry

    lax.fori_loop(0, tiles - 1, loop, 0)
    last = tiles - 1
    mc = m_ref[:, :1]
    acc = zero()
    for k in range(0, tokens, step):
        acc = weighed(last % 2, k, mc, acc)
    close(last, mc, acc)


def features_body(rt, q_ref, mine_ref, other_ref, keep_ref, send_ref, own_ref, stat_ref, c_ref, f_ref):
    rows, width = q_ref.shape
    peers, half, _ = mine_ref.shape
    count = 2 * half
    sel = peers * count
    c = LOG2E * width**-0.5
    pb = lax.axis_index("pb")
    at = lax.axis_index("ctx")
    for j in range(peers):
        c_ref[pl.ds(pl.multiple_of(j * count + pb * half, half), half), :] = mine_ref[j]
        c_ref[pl.ds(pl.multiple_of(j * count + (1 - pb) * half, half), half), :] = other_ref[j]
    for t in range(rows // rt):
        s = lax.dot_general(c_ref[...], q_ref[t * rt : (t + 1) * rt, :], NT, preferred_element_type=F32)
        mx = jnp.max(s, axis=0, keepdims=True) * c
        e = jnp.exp2(s * c - mx)
        total = jnp.sum(e, axis=0, keepdims=True)
        f_ref[:, t * rt : (t + 1) * rt] = (e * (sel / total)).astype(BF16)
        stat = (mx + jnp.log2(total)) * (1.0 / LOG2E)
        for g in range(rt // 128):
            r = t * (rt // 128) + g
            stat_ref[r : r + 1, :] = stat[:, g * 128 : (g + 1) * 128]
    own_ref[:half, :] = f_ref[pl.ds(pl.multiple_of(at * count + pb * half, half), half), :]
    own_ref[half:, :] = f_ref[pl.ds(pl.multiple_of(at * count + (1 - pb) * half, half), half), :]
    step = 512
    for k in range(0, sel, step):
        g = lax.dot_general(own_ref[...], f_ref[k : k + step, :], NT, preferred_element_type=F32)
        g = g * (1.0 / (2 * rows))
        keep_ref[:, k : k + step] = g[:half]
        send_ref[:, k : k + step] = g[half:]


def settle_body(in_ref, out_ref, w_ref):
    peers = in_ref.shape[0]
    share = in_ref.shape[1] - 16
    at = lax.axis_index("ctx")
    first = (at % (128 // share)) * share
    lines = in_ref[:, share : share + 16, :].astype(F32)
    lse = (lines[:, 0, :] + lines[:, 1, :]) + lines[:, 2, :]
    top = jnp.max(lse, axis=0, keepdims=True)
    w = jnp.exp(lse - top)
    total = jnp.sum(w, axis=0, keepdims=True)
    w = w / total
    pad = jnp.concatenate([w, jnp.zeros((128 - peers, 128), F32)], axis=0) if peers < 128 else w
    w_ref[...] = pad.T
    mine = w_ref[pl.ds(pl.multiple_of(first, share), share), :]
    acc = jnp.zeros((share, 128), F32)
    for b in range(peers):
        acc = acc + mine[:, b : b + 1] * in_ref[b, :share, :].astype(F32)
    y = (acc * lax.rsqrt(jnp.mean(acc * acc, axis=1, keepdims=True) + eps)).astype(BF16)
    full = jnp.broadcast_to(top + jnp.log(total), (16, 128))
    hi, mid, low = split3(full)
    r = lax.broadcasted_iota(jnp.int32, (16, 128), 0)
    three = jnp.where(r == 0, hi.astype(F32), jnp.where(r == 1, mid.astype(F32), low.astype(F32))).astype(BF16)
    for p in range(peers):
        out_ref[p, :share, :] = y
        out_ref[p, share : share + 16, :] = three


def rhs_body(in_ref, own_ref, stat_ref, keep_ref, send_ref, gap_ref, y_ref):
    peers = in_ref.shape[0]
    share = in_ref.shape[1] - 16
    half = keep_ref.shape[0]
    rows = peers * share
    for p in range(peers):
        y_ref[p * share : (p + 1) * share, :] = in_ref[p, :share, :]
    g = jnp.dot(own_ref[...], y_ref[...], preferred_element_type=F32) * (1.0 / (2 * rows))
    keep_ref[...] = g[:half]
    send_ref[...] = g[half:]
    per = 128 // share
    lane = lax.broadcasted_iota(jnp.int32, (1, 128), 1)
    for h in range(rows // 128):
        line = jnp.zeros((1, 128), F32)
        for j in range(per):
            x = in_ref[h * per + j, share : share + 16, :].astype(F32)
            v = (x[0:1] + x[1:2]) + x[2:3]
            line = jnp.where((lane >= j * share) & (lane < (j + 1) * share), v, line)
        gap_ref[h : h + 1, :] = line - stat_ref[h : h + 1, :]


def shards(queries, cache_keys, cache_values, sel_index):
    heads, rows_dev, width = queries.shape[1:]
    q = queries[0].reshape(-1, width)
    keys, values = cache_keys[0], cache_values[0]
    rows, tokens = q.shape[0], keys.shape[0]
    peers = lax.axis_size("ctx")
    share = rows // peers
    count = sel_index.shape[1]
    half = count // 2
    sel = count * peers
    swap = [(0, 1), (1, 0)]

    def exchange(x):
        return lax.all_to_all(x, "ctx", 0, 0, tiled=True)

    (picked,) = call(
        "pick", pick_body, [((peers, half, width), BF16)], (sel_index, keys), flops=2 * half * tokens * width, moved=tokens * width * 2
    )
    mine = exchange(picked)
    rt = 256
    (parts,) = call(
        "attend",
        functools.partial(attend_body, rt),
        [((peers, share + 16, width), BF16)],
        (q, keys, values),
        after=(picked,),
        scratch=[pltpu.VMEM((2, rt, tokens), F32), pltpu.VMEM((rt, 128), F32)],
        flops=4 * rows * tokens * width,
        exps=rows * tokens,
        moved=tokens * width * 4,
    )
    arrived = exchange(parts)
    other = lax.ppermute(mine, "pb", swap)
    keep, send, own, stat = call(
        "features",
        functools.partial(features_body, rt),
        [((half, sel), F32), ((half, sel), F32), ((count, rows), BF16), ((rows // 128, 128), F32)],
        (q, mine, other),
        after=(parts,),
        scratch=[pltpu.VMEM((sel, width), BF16), pltpu.VMEM((sel, rows), BF16)],
        flops=2 * rows * sel * width + 2 * count * rows * sel,
        exps=rows * sel,
        moved=sel * width * 4,
    )
    (told,) = call(
        "settle",
        settle_body,
        [((peers, share + 16, width), BF16)],
        (arrived,),
        after=(stat,),
        scratch=[pltpu.VMEM((128, 128), F32)],
        flops=4 * rows * width,
        moved=2 * rows * width * 2,
    )
    heard = exchange(told)
    gram = keep + lax.ppermute(send, "pb", swap)
    rkeep, rsend, gap = call(
        "rhs",
        rhs_body,
        [((half, width), F32), ((half, width), F32), ((rows // 128, 128), F32)],
        (heard, own, stat),
        scratch=[pltpu.VMEM((rows, width), BF16)],
        flops=2 * count * rows * width,
        moved=rows * width * 2,
    )
    rhs = rkeep + lax.ppermute(rsend, "pb", swap)
    return (gram[None], rhs[None], gap.reshape(1, heads, rows_dev))


def solution(mesh):
    in_specs = (
        P("kv", None, "pb", None),
        P("kv", "ctx", None),
        P("kv", "ctx", None),
        P("kv", "ctx"),
    )
    out_specs = (P("kv", ("ctx", "pb"), None), P("kv", ("ctx", "pb"), None), P("kv", None, "pb"))
    return jax.shard_map(shards, mesh=mesh, in_specs=in_specs, out_specs=out_specs, check_vma=False)
```

time: 192 us -> 112 us (0.58)
  waiting for transfers between devices: 103 us -> 43.4 us
  Pallas kernels: 0 us -> 21.4 us
  matrix products: 12.1 us -> 0 us
  other arithmetic: 12.5 us -> 1.35 us
  local copies, waits for them, and re-layouts: 13 us -> 3.1 us
  blocking collectives: 9.12 us -> 0 us
    all_to_all x5 -> x3, waiting for transfers between devices: 103 us -> 42.2 us  [exchange(): return lax.all_to_all(x, 'ctx', 0, 0, tiled=True)]
    pallas_call x0 -> x5, Pallas kernels: none -> 21.4 us  [call(): pl.pallas_call(ordered, name=name, out_shape=[jax.ShapeDtypeStruct(s, d)...]
    dot_general x7 -> x0, matrix products: 12.1 us -> none  [the longest x2 5.42 us: attend(): jnp.einsum('rd,kd->rk', block_rows, keys, preferred_element_type=jnp.floa...]
    ppermute x0 -> x3, starting transfers between devices: none -> 11 us  [the longest x1 4.82 us: shards(): rhs = rkeep + lax.ppermute(rsend, 'pb', swap)]
    all_to_all x5 -> x3, starting transfers between devices: 40.9 us -> 30.5 us  [exchange(): return lax.all_to_all(x, 'ctx', 0, 0, tiled=True)]
    all_to_all x1 -> x0, blocking collectives: 9.12 us -> none  [sum_at_owner(): lax.all_to_all(pieces, axis, split_axis=0, concat_axis=0, tiled=True)]
    reduce_sum x6 -> x0, other arithmetic: 4.75 us -> none  [the longest x2 3.02 us: attend(): block_total = jnp.sum(expo, axis=1)]
    convert_element_type x2 -> x0, other arithmetic: 4.47 us -> none  [the longest x1 4.39 us: shards(): feat = (sel_all * cexp / ctotal[:, None]).astype(jnp.bfloat16)]
  transfers between devices with their start and end apart: 5 -> 6, of which waited for: 5 -> 5; matrix products, arithmetic and copies ran while one was open for 8% -> 1% of each run, Pallas kernels for 0% -> 17%
where the time goes in v1:
time: 112 us
  waiting for transfers between devices  43.4 us (39%)
  starting transfers between devices  41.6 us (37%)
  Pallas kernels  21.4 us (19%)
  local copies, waits for them, and re-layouts  3.1 us (3%)
  other arithmetic  1.35 us (1%)
    all_to_all x3, waiting for transfers between devices, exchange(): return lax.all_to_all(x, 'ctx', 0, 0, tiled=True)  42.2 us
    all_to_all x3, starting transfers between devices, exchange(): return lax.all_to_all(x, 'ctx', 0, 0, tiled=True)  30.5 us
    pallas_call x5, Pallas kernels, call(): pl.pallas_call(ordered, name=name, out_shape=[jax.ShapeDtypeStruct(s, d)...  21.4 us
    ppermute x1, starting transfers between devices, shards(): rhs = rkeep + lax.ppermute(rsend, 'pb', swap)  4.82 us
    ppermute x1, starting transfers between devices, shards(): other = lax.ppermute(mine, 'pb', swap)  3.41 us
    unnamed x10, local copies, waits for them, and re-layouts  3.1 us
    ppermute x1, starting transfers between devices, shards(): gram = keep + lax.ppermute(send, 'pb', swap)  2.81 us
  transfers between devices with their start and end apart: 6, of which 5 were waited for; matrix products, arithmetic and copies ran while one was open for 1% of the time, Pallas kernels for 17%

profile of v1, /device:TPU:1, one launch (start us, length us, event | category | flops | bytes accessed | tf_op | source)
XLA Modules:
  0.0 111.6 jit_solution(4710389162449940658)
XLA Ops:
  0.6 0.0 copy-start.2
  0.6 0.6 copy-done.2
  1.3 1.2 %copy-done = bf16[1,4096,128]{2,1,0:T(8,128)(2,1)S(1)} copy-done((bf16[1,4096,128]{2,1,0:T(8,128)(2,1)S(1)}, bf16[1,4096,128]{2,1,0:T(8,128)(2,1)}, u32[]{:S(2)}) %copy-start) | copy-done | bytes 1048600
  2.5 1.1 pick.1.refs_3_
  3.6 17.1 %all-to-all-start = ((bf16[32,32,128]{2,1,0:T(8,128)(2,1)}), bf16[32,32,128]{2,1,0:T(8,128)(2,1)S(1)}, u32[]{:S(2)}, u32[]{:S(2)}) async-start(bf16[32,32,128]{2,1,0:T(8,128)(2,1)} %pick.1.refs_3_), calls=%async_computation | async-start | bytes 524288 | tf_op jit(solution)/shard_map/all_to_all | solution.py:235
  20.7 0.0 copy-start.3
  20.7 1.2 %copy-done.3 = bf16[1,4096,128]{2,1,0:T(8,128)(2,1)S(1)} copy-done((bf16[1,4096,128]{2,1,0:T(8,128)(2,1)S(1)}, bf16[1,4096,128]{2,1,0:T(8,128)(2,1)}, u32[]{:S(2)}) %copy-start.3) | copy-done | bytes 1048600
  21.9 12.9 %attend.1.refs_3_ = bf16[32,48,128]{2,1,0:T(8,128)(2,1)} custom-call(bf16[1024,128]{1,0:T(8,128)(2,1)S(1)} %bitcast.11, bf16[4096,128]{1,0:T(8,128)(2,1)S(1)} %bitcast.9, bf16[4096,128]{1,0:T(8,128)(2,1)S(1)} %bitcast.10, bf16[32,32,128]{2,1,0:T(8,128)(2,1)} %pick.1.refs_3_), custom_call_target="tpu_custom_call" | custom-call | flops 2147483648 | bytes 2097152 | tf_op jit(solution)/shard_map/attend/pallas_call | solution.py:24
  34.8 5.9 %all-to-all-done.refs_1_ = bf16[32,32,128]{2,1,0:T(8,128)(2,1)S(1)} async-done(((bf16[32,32,128]{2,1,0:T(8,128)(2,1)}), bf16[32,32,128]{2,1,0:T(8,128)(2,1)S(1)}, u32[]{:S(2)}, u32[]{:S(2)}) %all-to-all-start) | async-done | bytes 262176 | tf_op jit(solution)/shard_map/all_to_all | solution.py:235
  40.7 6.7 %all-to-all-start.1 = ((bf16[32,48,128]{2,1,0:T(8,128)(2,1)}), bf16[32,48,128]{2,1,0:T(8,128)(2,1)S(1)}, u32[]{:S(2)}, u32[]{:S(2)}) async-start(bf16[32,48,128]{2,1,0:T(8,128)(2,1)} %attend.1.refs_3_), calls=%async_computation.1 | async-start | bytes 786432 | tf_op jit(solution)/shard_map/all_to_all | solution.py:235
  47.4 3.4 %collective-permute-start = (bf16[32,32,128]{2,1,0:T(8,128)(2,1)S(1)}, bf16[32,32,128]{2,1,0:T(8,128)(2,1)S(1)}, u32[]{:S(2)}, u32[]{:S(2)}) collective-permute-start(bf16[32,32,128]{2,1,0:T(8,128)(2,1)S(1)} %all-to-all-done.refs_1_), channel_id=1, source_target_pairs={{0,1},{1,0},{2,3},{3,2},{4,5},{5,4},{6,7},{7,6},{8,9},{9,8},{10,11... | collective-permute-start | bytes 786440 | tf_op jit(solution)/shard_map/ppermute | solution.py:254
  50.8 1.1 %collective-permute-done.refs_2_ = bf16[32,32,128]{2,1,0:T(8,128)(2,1)S(1)} collective-permute-done((bf16[32,32,128]{2,1,0:T(8,128)(2,1)S(1)}, bf16[32,32,128]{2,1,0:T(8,128)(2,1)S(1)}, u32[]{:S(2)}, u32[]{:S(2)}) %collective-permute-start) | collective-permute-done | bytes 262176 | tf_op jit(solution)/shard_map/ppermute | solution.py:254
  52.0 5.4 %features.1 = (f32[32,2048]{1,0:T(8,128)S(1)}, f32[32,2048]{1,0:T(8,128)S(1)}, bf16[64,1024]{1,0:T(8,128)(2,1)S(1)}, f32[8,128]{1,0:T(8,128)S(1)}) custom-call(bf16[1024,128]{1,0:T(8,128)(2,1)S(1)} %bitcast.12, bf16[32,32,128]{2,1,0:T(8,128)(2,1)S(1)} %all-to-all-done.refs_1_, bf16[32,32,128]{2,1,0:T(8,128)(2,1)S(1)} %collective-permute-done.refs_2_, ...), custom_call_target="tpu_custom_call" | custom-call | flops 805306368 | bytes 1048576 | tf_op jit(solution)/shard_map/features/pallas_call | solution.py:24
  57.4 14.1 %all-to-all-done.1.refs_0_ = bf16[32,48,128]{2,1,0:T(8,128)(2,1)S(1)} async-done(((bf16[32,48,128]{2,1,0:T(8,128)(2,1)}), bf16[32,48,128]{2,1,0:T(8,128)(2,1)S(1)}, u32[]{:S(2)}, u32[]{:S(2)}) %all-to-all-start.1) | async-done | bytes 393248 | tf_op jit(solution)/shard_map/all_to_all | solution.py:235
  71.5 1.3 %settle.1 = bf16[32,48,128]{2,1,0:T(8,128)(2,1)} custom-call(bf16[32,48,128]{2,1,0:T(8,128)(2,1)S(1)} %all-to-all-done.1.refs_0_, f32[8,128]{1,0:T(8,128)S(1)} %get-tuple-element.12.refs_1_.refs_2_), custom_call_target="tpu_custom_call" | custom-call | flops 524288 | bytes 524288 | tf_op jit(solution)/shard_map/settle/pallas_call | solution.py:24
  72.8 6.8 %all-to-all-start.2 = ((bf16[32,48,128]{2,1,0:T(8,128)(2,1)}), bf16[32,48,128]{2,1,0:T(8,128)(2,1)S(1)}, u32[]{:S(2)}, u32[]{:S(2)}) async-start(bf16[32,48,128]{2,1,0:T(8,128)(2,1)} %settle.1), calls=%async_computation.2 | async-start | bytes 786432 | tf_op jit(solution)/shard_map/all_to_all | solution.py:235
  79.5 2.8 %collective-permute-start.1 = (f32[32,2048]{1,0:T(8,128)S(1)}, f32[32,2048]{1,0:T(8,128)S(1)}, u32[]{:S(2)}, u32[]{:S(2)}) collective-permute-start(f32[32,2048]{1,0:T(8,128)S(1)} %get-tuple-element.11), channel_id=1, source_target_pairs={{0,1},{1,0},{2,3},{3,2},{4,5},{5,4},{6,7},{7,6},{8,9},{9,8},{10,11... | collective-permute-start | bytes 786440 | tf_op jit(solution)/shard_map/ppermute | solution.py:277
  82.3 22.3 %all-to-all-done.2.refs_0_ = bf16[32,48,128]{2,1,0:T(8,128)(2,1)S(1)} async-done(((bf16[32,48,128]{2,1,0:T(8,128)(2,1)}), bf16[32,48,128]{2,1,0:T(8,128)(2,1)S(1)}, u32[]{:S(2)}, u32[]{:S(2)}) %all-to-all-start.2) | async-done | bytes 393248 | tf_op jit(solution)/shard_map/all_to_all | solution.py:235
  104.6 0.7 rhs.1
  105.3 4.8 %collective-permute-start.2 = (f32[32,128]{1,0:T(8,128)S(1)}, f32[32,128]{1,0:T(8,128)S(1)}, u32[]{:S(2)}, u32[]{:S(2)}) collective-permute-start(f32[32,128]{1,0:T(8,128)S(1)} %get-tuple-element.15), channel_id=1, source_target_pairs={{0,1},{1,0},{2,3},{3,2},{4,5},{5,4},{6,7},{7,6},{8,9},{9,8},{10,11... | collective-permute-start | bytes 49160 | tf_op jit(solution)/shard_map/ppermute | solution.py:287
  110.1 0.0 collective-permute-done.1
  110.1 0.7 add_bitcast_fusion
  110.9 0.1 collective-permute-done.2
  111.0 0.6 add_bitcast_fusion.1
  (5 shorter events, 0.0 us)
Async XLA Ops:
  0.6 0.7 copy-start.2
  1.3 1.2 %copy-start = (bf16[1,4096,128]{2,1,0:T(8,128)(2,1)S(1)}, bf16[1,4096,128]{2,1,0:T(8,128)(2,1)}, u32[]{:S(2)}) copy-start(bf16[1,4096,128]{2,1,0:T(8,128)(2,1)} %param.5) | copy-start | bytes 3145732
  2.5 18.2 %copy-start.1 = (bf16[1,4096,128]{2,1,0:T(8,128)(2,1)S(1)}, bf16[1,4096,128]{2,1,0:T(8,128)(2,1)}, u32[]{:S(2)}) copy-start(bf16[1,4096,128]{2,1,0:T(8,128)(2,1)} %param.5) | copy-start | bytes 3145732
  3.6 17.1 %copy-start.4 = (bf16[1,8,128,128]{3,2,1,0:T(8,128)(2,1)S(1)}, bf16[1,8,128,128]{3,2,1,0:T(8,128)(2,1)}, u32[]{:S(2)}) copy-start(bf16[1,8,128,128]{3,2,1,0:T(8,128)(2,1)} %param.4) | copy-start | bytes 786436
  3.6 37.1 %all-to-all-start = ((bf16[32,32,128]{2,1,0:T(8,128)(2,1)}), bf16[32,32,128]{2,1,0:T(8,128)(2,1)S(1)}, u32[]{:S(2)}, u32[]{:S(2)}) async-start(bf16[32,32,128]{2,1,0:T(8,128)(2,1)} %pick.1.refs_3_), calls=%async_computation | async-start | bytes 524288 | tf_op jit(solution)/shard_map/all_to_all | solution.py:235
  20.7 1.2 %copy-start.3 = (bf16[1,4096,128]{2,1,0:T(8,128)(2,1)S(1)}, bf16[1,4096,128]{2,1,0:T(8,128)(2,1)}, u32[]{:S(2)}) copy-start(bf16[1,4096,128]{2,1,0:T(8,128)(2,1)} %param.6) | copy-start | bytes 3145732
  40.7 30.8 %all-to-all-start.1 = ((bf16[32,48,128]{2,1,0:T(8,128)(2,1)}), bf16[32,48,128]{2,1,0:T(8,128)(2,1)S(1)}, u32[]{:S(2)}, u32[]{:S(2)}) async-start(bf16[32,48,128]{2,1,0:T(8,128)(2,1)} %attend.1.refs_3_), calls=%async_computation.1 | async-start | bytes 786432 | tf_op jit(solution)/shard_map/all_to_all | solution.py:235
  47.4 4.6 %collective-permute-start = (bf16[32,32,128]{2,1,0:T(8,128)(2,1)S(1)}, bf16[32,32,128]{2,1,0:T(8,128)(2,1)S(1)}, u32[]{:S(2)}, u32[]{:S(2)}) collective-permute-start(bf16[32,32,128]{2,1,0:T(8,128)(2,1)S(1)} %all-to-all-done.refs_1_), channel_id=1, source_target_pairs={{0,1},{1,0},{2,3},{3,2},{4,5},{5,4},{6,7},{7,6},{8,9},{9,8},{10,11... | collective-permute-start | bytes 786440 | tf_op jit(solution)/shard_map/ppermute | solution.py:254
  72.8 31.8 %all-to-all-start.2 = ((bf16[32,48,128]{2,1,0:T(8,128)(2,1)}), bf16[32,48,128]{2,1,0:T(8,128)(2,1)S(1)}, u32[]{:S(2)}, u32[]{:S(2)}) async-start(bf16[32,48,128]{2,1,0:T(8,128)(2,1)} %settle.1), calls=%async_computation.2 | async-start | bytes 786432 | tf_op jit(solution)/shard_map/all_to_all | solution.py:235
  79.5 30.6 %collective-permute-start.1 = (f32[32,2048]{1,0:T(8,128)S(1)}, f32[32,2048]{1,0:T(8,128)S(1)}, u32[]{:S(2)}, u32[]{:S(2)}) collective-permute-start(f32[32,2048]{1,0:T(8,128)S(1)} %get-tuple-element.11), channel_id=1, source_target_pairs={{0,1},{1,0},{2,3},{3,2},{4,5},{5,4},{6,7},{7,6},{8,9},{9,8},{10,11... | collective-permute-start | bytes 786440 | tf_op jit(solution)/shard_map/ppermute | solution.py:277
  105.3 5.6 %collective-permute-start.2 = (f32[32,128]{1,0:T(8,128)S(1)}, f32[32,128]{1,0:T(8,128)S(1)}, u32[]{:S(2)}, u32[]{:S(2)}) collective-permute-start(f32[32,128]{1,0:T(8,128)S(1)} %get-tuple-element.15), channel_id=1, source_target_pairs={{0,1},{1,0},{2,3},{3,2},{4,5},{5,4},{6,7},{7,6},{8,9},{9,8},{10,11... | collective-permute-start | bytes 49160 | tf_op jit(solution)/shard_map/ppermute | solution.py:287

commit v2 on v1

v2 whole, which is shorter than its diff:
```python
import functools
import math

import jax
import jax.numpy as jnp
from jax import lax
from jax.experimental import pallas as pl
from jax.experimental.pallas import tpu as pltpu
from jax.sharding import PartitionSpec as P

eps = 1e-06
LOG2E = math.log2(math.e)
F32, BF16 = jnp.float32, jnp.bfloat16
VMEM = pl.BlockSpec(memory_space=pltpu.VMEM)
ANY = pl.BlockSpec(memory_space=pl.ANY)
NT = (((1,), (1,)), ((), ()))
TT = (((0,), (0,)), ((), ()))
STAT = 16


def call(name, body, outs, ins, scratch=(), after=(), held=None, specs=(), flops=0, exps=0, moved=0, limit=20):
    count, skip, here = len(ins), len(after) + (held is not None), len(outs)
    more = [held] if held is not None else []

    def ordered(*refs):
        body(*refs[:count], *refs[count + skip : count + skip + here], *refs[count + skip + here + len(more) :])

    return pl.pallas_call(
        ordered,
        name=name,
        out_shape=[jax.ShapeDtypeStruct(s, d) for s, d in outs] + [jax.ShapeDtypeStruct(m.shape, m.dtype) for m in more],
        in_specs=(list(specs) or [VMEM] * count) + [ANY] * skip,
        out_specs=[VMEM] * here + [ANY] * len(more),
        input_output_aliases={count + skip - 1: here} if more else {},
        scratch_shapes=list(scratch),
        compiler_params=pltpu.CompilerParams(vmem_limit_bytes=limit << 20),
        cost_estimate=pl.CostEstimate(flops=flops, transcendentals=exps, bytes_accessed=moved),
    )(*ins, *after, *more)


def split3(x):
    hi = x.astype(BF16)
    rest = x - hi.astype(F32)
    mid = rest.astype(BF16)
    low = (rest - mid.astype(F32)).astype(BF16)
    return hi, mid, low


def joined3(a, b, c):
    return (a.astype(F32) + b.astype(F32)) + c.astype(F32)


def packed3(line):
    hi, mid, low = split3(jnp.broadcast_to(line, (STAT, 128)))
    r = lax.broadcasted_iota(jnp.int32, (STAT, 128), 0)
    return jnp.where(r == 0, hi.astype(F32), jnp.where(r == 1, mid.astype(F32), low.astype(F32))).astype(BF16)


def column(line):
    return jnp.broadcast_to(line, (128, 128)).T


def place(ring):
    at = lax.axis_index("ctx")
    return at // ring, at % ring


def attend(ring, away, q_hbm, k_hbm, v_hbm, q_ref, k_ref, v_ref, s_ref, sem):
    rows, width = q_ref.shape
    tokens = k_ref.shape[0]
    step = 512
    c = LOG2E * width**-0.5
    x, _ = place(ring)
    part = 1 - x if away else x
    copies = [pltpu.make_async_copy(q_hbm.at[pl.ds(pl.multiple_of(part * rows, rows), rows)], q_ref, sem.at[0])]
    for ref, hbm in ((k_ref, k_hbm), (v_ref, v_hbm)):
        for a in range(0, tokens, step):
            cut = pl.ds(a, step)
            copies.append(pltpu.make_async_copy(hbm.at[cut], ref.at[cut], sem.at[len(copies)]))
    for copy in copies:
        copy.start()
    copies[0].wait()
    q = q_ref[...]
    chunks = tokens // step
    mx = None
    for n in range(chunks):
        copies[1 + n].wait()
        a = n * step
        s = lax.dot_general(k_ref[a : a + step, :], q, NT, preferred_element_type=F32)
        s_ref[a : a + step, :] = s
        top = jnp.max(s.reshape(step // 8, 8, rows), axis=0)
        mx = top if mx is None else jnp.maximum(mx, top)
    mc = jnp.max(mx, axis=0, keepdims=True) * c
    total, out = jnp.zeros((8, rows), F32), jnp.zeros((width, rows), F32)
    for n in range(chunks):
        copies[1 + chunks + n].wait()
        a = n * step
        p = jnp.exp2(s_ref[a : a + step, :] * c - mc)
        total = total + jnp.sum(p.reshape(step // 8, 8, rows), axis=0)
        out = out + lax.dot_general(v_ref[a : a + step, :], p.astype(BF16), TT, preferred_element_type=F32)
    total = jnp.sum(total, axis=0, keepdims=True)
    return (out * (1.0 / total)).T, (mc + jnp.log2(total)) * (1.0 / LOG2E)


def away_body(ring, sel_hbm, q_hbm, k_hbm, v_hbm, out_ref, pick_ref, sel_ref, q_ref, k_ref, v_ref, s_ref, sem, sel_sem):
    fetch = pltpu.make_async_copy(sel_hbm, sel_ref, sel_sem)
    fetch.start()
    o, lse = attend(ring, True, q_hbm, k_hbm, v_hbm, q_ref, k_ref, v_ref, s_ref, sem)
    rows, width = q_ref.shape
    tokens = k_ref.shape[0]
    share = rows // ring
    per = 128 // share
    o = o.astype(BF16)
    block = share + STAT
    for g in range(rows // 128):
        three = packed3(lse[:, g * 128 : (g + 1) * 128])
        for j in range(g * per, (g + 1) * per):
            out_ref[j * block : j * block + share, :] = o[j * share : (j + 1) * share, :]
            out_ref[j * block + share : (j + 1) * block, :] = three
    fetch.wait()
    half = pick_ref.shape[0]
    count = sel_ref.shape[1]
    base = lax.axis_index("ctx") * tokens
    first = lax.axis_index("pb") * half
    row = lax.broadcasted_iota(jnp.int32, (half, count), 0) + first
    lane = lax.broadcasted_iota(jnp.int32, (half, count), 1)
    sel = jnp.broadcast_to((sel_ref[...] - base).astype(F32), (half, count))
    col = jnp.sum(jnp.where(row == lane, sel, 0.0), axis=1, keepdims=True).astype(jnp.int32)
    step = 512
    acc = jnp.zeros((half, width), F32)
    for k in range(0, tokens, step):
        at = lax.broadcasted_iota(jnp.int32, (half, step), 1) + k
        hot = (at == col).astype(F32).astype(BF16)
        acc += jnp.dot(hot, k_ref[k : k + step, :], preferred_element_type=F32)
    mine = acc.astype(BF16)
    pick_ref[...] = mine
    out_ref[ring * block : ring * block + half, :] = mine


def home_body(ring, q_hbm, k_hbm, v_hbm, out_ref, lse_ref, q_ref, k_ref, v_ref, s_ref, sem):
    o, lse = attend(ring, False, q_hbm, k_hbm, v_hbm, q_ref, k_ref, v_ref, s_ref, sem)
    out_ref[...] = o
    lse_ref[...] = jnp.zeros_like(lse_ref)
    for g in range(o.shape[0] // 128):
        lse_ref[g : g + 1, :] = lse[:, g * 128 : (g + 1) * 128]


def pair_body(o_ref, lse_ref, in_ref, pick_ref, out_ref):
    ring = out_ref.shape[0]
    rows = o_ref.shape[0]
    half = pick_ref.shape[0]
    share = rows // ring
    per = 128 // share
    block = share + STAT
    mine, theirs = pick_ref[...], in_ref[ring * block : ring * block + half, :]
    for g in range(rows // 128):
        at = g * per * block
        three = in_ref[at + share : at + block, :].astype(F32)
        other = (three[0:1] + three[1:2]) + three[2:3]
        here = lse_ref[g : g + 1, :]
        top = jnp.maximum(other, here)
        wo, wh = jnp.exp(other - top), jnp.exp(here - top)
        total = wo + wh
        lines = packed3(top + jnp.log(total))
        share_of = column(wh / total)
        for j in range(g * per, (g + 1) * per):
            w = share_of[(j % per) * share : (j % per + 1) * share, :]
            a = in_ref[j * block : j * block + share, :].astype(F32)
            h = o_ref[j * share : (j + 1) * share, :]
            out_ref[j, :share, :] = (a + w * (h - a)).astype(BF16)
            out_ref[j, share:block, :] = lines
            out_ref[j, block : block + half, :] = mine
            out_ref[j, block + half :, :] = theirs


def settle_body(share, in_ref, out_ref, keys_ref, w_ref):
    ring = in_ref.shape[0]
    block = share + STAT
    _, z = place(ring)
    lines = in_ref[:, share:block, :].astype(F32)
    lse = (lines[:, 0, :] + lines[:, 1, :]) + lines[:, 2, :]
    top = jnp.max(lse, axis=0, keepdims=True)
    w = jnp.exp(lse - top)
    total = jnp.sum(w, axis=0, keepdims=True)
    w = w / total
    w_ref[...] = jnp.concatenate([w, jnp.zeros((128 - ring, 128), F32)], axis=0).T
    mine = w_ref[pl.ds(pl.multiple_of((z % (128 // share)) * share, share), share), :]
    acc = jnp.zeros((share, 128), F32)
    for b in range(ring):
        acc = acc + mine[:, b : b + 1] * in_ref[b, :share, :].astype(F32)
    y = (acc * lax.rsqrt(jnp.mean(acc * acc, axis=1, keepdims=True) + eps)).astype(BF16)
    three = packed3(top + jnp.log(total))
    for p in range(ring):
        out_ref[p, :share, :] = y
        out_ref[p, share:, :] = three
        keys_ref[p] = in_ref[p, block:, :]


def features_body(rt, q_ref, mine_ref, other_ref, own_ref, stat_ref, keep_ref, send_ref, c_ref, f_ref, g_ref):
    rows, width = q_ref.shape
    ring, count, _ = mine_ref.shape
    half = count // 2
    sel = 2 * ring * count
    c = LOG2E * width**-0.5
    pb = lax.axis_index("pb")
    x, z = place(ring)
    for j in range(ring):
        for ref, core in ((mine_ref, pb), (other_ref, 1 - pb)):
            for k, side in ((0, x), (1, 1 - x)):
                at = pl.multiple_of((side * ring + j) * count + core * half, half)
                c_ref[pl.ds(at, half), :] = ref[j, k * half : (k + 1) * half, :]
    for t in range(rows // rt):
        s = lax.dot_general(c_ref[...], q_ref[t * rt : (t + 1) * rt, :], NT, preferred_element_type=F32)
        mx = jnp.max(s, axis=0, keepdims=True) * c
        e = jnp.exp2(s * c - mx)
        total = jnp.sum(e, axis=0, keepdims=True)
        f_ref[:, t * rt : (t + 1) * rt] = (e * (sel / total)).astype(BF16)
        stat = (mx + jnp.log2(total)) * (1.0 / LOG2E)
        for g in range(rt // 128):
            r = t * (rt // 128) + g
            stat_ref[r : r + 1, :] = stat[:, g * 128 : (g + 1) * 128]
    there = rows // 2
    lanes = pl.ds(pl.multiple_of(x * there, there), there)
    for k, side in ((0, x), (1, 1 - x)):
        at = pl.multiple_of((side * ring + z) * count, count)
        own_ref[k * count : (k + 1) * count, :] = f_ref[pl.ds(at, count), lanes]
    at = lax.axis_index("ctx") * count
    g_ref[:half, :] = f_ref[pl.ds(pl.multiple_of(at + pb * half, half), half), :]
    g_ref[half:, :] = f_ref[pl.ds(pl.multiple_of(at + (1 - pb) * half, half), half), :]
    step = 512
    for k in range(0, sel, step):
        g = lax.dot_general(g_ref[...], f_ref[k : k + step, :], NT, preferred_element_type=F32)
        g = g * (1.0 / (2 * rows))
        keep_ref[:, k : k + step] = g[:half]
        send_ref[:, k : k + step] = g[half:]


def rhs_body(total_rows, in_ref, own_ref, keep_ref, send_ref, y_ref):
    ring, block, _ = in_ref.shape
    share = block - STAT
    count = keep_ref.shape[0]
    rows = ring * share
    for p in range(ring):
        y_ref[p * share : (p + 1) * share, :] = in_ref[p, :share, :]
    g = jnp.dot(own_ref[...], y_ref[...], preferred_element_type=F32) * (1.0 / total_rows)
    keep_ref[...] = g[:count]
    send_ref[:count, :] = g[count:]
    send_ref[count:, :] = jnp.zeros((8, 128), F32)
    per = 128 // share
    lane = lax.broadcasted_iota(jnp.int32, (1, 128), 1)
    for h in range(rows // 128):
        line = jnp.zeros((1, 128), F32)
        for j in range(per):
            v = in_ref[h * per + j, share:block, :].astype(F32)
            v = (v[0:1] + v[1:2]) + v[2:3]
            line = jnp.where((lane >= j * share) & (lane < (j + 1) * share), v, line)
        send_ref[count + h : count + h + 1, :] = line


def sides_body(ring, keep_ref, sent_ref, got_ref, stat_ref, mine_ref, other_ref, gap_ref, sum_ref):
    count = keep_ref.shape[0]
    half = count // 2
    pb = lax.axis_index("pb")
    x, _ = place(ring)
    sum_ref[...] = keep_ref[...] + got_ref[:count, :]
    mine_ref[...] = sum_ref[pl.ds(pl.multiple_of(pb * half, half), half), :]
    other_ref[...] = sum_ref[pl.ds(pl.multiple_of((1 - pb) * half, half), half), :]
    lines = gap_ref.shape[0] // 2
    here, there = sent_ref[count : count + lines, :], got_ref[count : count + lines, :]
    low = jnp.where(x == 0, here, there)
    high = jnp.where(x == 0, there, here)
    gap_ref[:lines, :] = low - stat_ref[:lines, :]
    gap_ref[lines:, :] = high - stat_ref[lines:, :]


def last_body(a_ref, b_ref, out_ref):
    out_ref[...] = a_ref[...] + b_ref[...]


def shards(queries, cache_keys, cache_values, sel_index):
    heads, rows_dev, width = queries.shape[1:]
    q = queries[0].reshape(-1, width)
    keys, values = cache_keys[0], cache_values[0]
    rows, tokens = q.shape[0], keys.shape[0]
    blocks = lax.axis_size("ctx")
    ring = blocks // 2
    part = rows // 2
    share = part // ring
    block = share + STAT
    count = sel_index.shape[1]
    half = count // 2
    sel = count * blocks
    total_rows = 2 * rows
    swap = [(0, 1), (1, 0)]
    across = [(i, (i + ring) % blocks) for i in range(blocks)]
    rings = [list(range(ring)), list(range(ring, blocks))]

    def exchange(x):
        return lax.all_to_all(x, "ctx", 0, 0, axis_index_groups=rings, tiled=True)

    held = [
        pltpu.VMEM((part, width), BF16),
        pltpu.VMEM((tokens, width), BF16),
        pltpu.VMEM((tokens, width), BF16),
        pltpu.VMEM((tokens, part), F32),
        pltpu.SemaphoreType.DMA((1 + 2 * (tokens // 512),)),
    ]
    work = dict(flops=4 * part * tokens * width, exps=part * tokens, moved=tokens * width * 4, limit=60)
    away, picked = call(
        "away",
        functools.partial(away_body, ring),
        [((ring * block + half, width), BF16), ((half, width), BF16)],
        (sel_index, q, keys, values),
        specs=[ANY] * 4,
        scratch=[pltpu.VMEM((1, count), jnp.int32), *held, pltpu.SemaphoreType.DMA],
        **work,
    )
    came = lax.ppermute(away, "ctx", across)
    home, lse = call(
        "home",
        functools.partial(home_body, ring),
        [((part, width), F32), ((8, 128), F32)],
        (q, keys, values),
        specs=[ANY] * 3,
        after=(picked,),
        scratch=held,
        **work,
    )
    (parts,) = call("pair", pair_body, [((ring, block + count, width), BF16)], (home, lse, came, picked), moved=part * width * 12)
    told, mine = call(
        "settle",
        functools.partial(settle_body, share),
        [((ring, block, width), BF16), ((ring, count, width), BF16)],
        (exchange(parts),),
        scratch=[pltpu.VMEM((128, 128), F32)],
        moved=part * width * 8,
    )
    heard = exchange(told)
    other = lax.ppermute(mine, "pb", swap)
    own, stat, gkeep, gsend = call(
        "features",
        functools.partial(features_body, 256),
        [((2 * count, part), BF16), ((rows // 128, 128), F32), ((half, sel), F32), ((half, sel), F32)],
        (q, mine, other),
        after=(told,),
        scratch=[pltpu.VMEM((sel, width), BF16), pltpu.VMEM((sel, rows), BF16), pltpu.VMEM((count, rows), BF16)],
        flops=2 * rows * sel * (width + count),
        exps=rows * sel,
        moved=sel * width * 4,
    )
    rkeep, rsend, gsend = call(
        "rhs",
        functools.partial(rhs_body, total_rows),
        [((count, width), F32), ((count + 8, width), F32)],
        (heard, own),
        held=gsend,
        scratch=[pltpu.VMEM((part, width), BF16)],
        flops=4 * count * part * width,
        moved=part * width * 2,
    )
    rmine, rother, gap = call(
        "sides",
        functools.partial(sides_body, ring),
        [((half, width), F32), ((half, width), F32), ((rows // 128, 128), F32)],
        (rkeep, rsend, lax.ppermute(rsend, "ctx", across), stat),
        scratch=[pltpu.VMEM((count, width), F32)],
        moved=count * width * 16,
    )
    gram = gkeep + lax.ppermute(gsend, "pb", swap)
    rgot = lax.ppermute(rother, "pb", swap)
    (rhs,) = call("last", last_body, [((half, width), F32)], (rmine, rgot), after=(gram,), moved=half * width * 12)
    return (gram[None], rhs[None], gap.reshape(1, heads, rows_dev))


def solution(mesh):
    in_specs = (
        P("kv", None, "pb", None),
        P("kv", "ctx", None),
        P("kv", "ctx", None),
        P("kv", "ctx"),
    )
    out_specs = (P("kv", ("ctx", "pb"), None), P("kv", ("ctx", "pb"), None), P("kv", None, "pb"))
    return jax.shard_map(shards, mesh=mesh, in_specs=in_specs, out_specs=out_specs, check_vma=False)
```

time: 112 us -> 97.8 us (0.87)
  waiting for transfers between devices: 43.4 us -> 6.61 us
  blocking collectives: 0 us -> 35.6 us
  starting transfers between devices: 41.6 us -> 31.1 us
  local copies, waits for them, and re-layouts: 3.1 us -> 1.65 us
  other arithmetic: 1.35 us -> 0.03 us
    all_to_all x3 -> x1, waiting for transfers between devices: 42.2 us -> 2.42 us  [exchange(): return lax.all_to_all(x, 'ctx', 0, 0, axis_index_groups=rings, tiled=True)]
    all_to_all x0 -> x1, blocking collectives: none -> 35.6 us  [exchange(): return lax.all_to_all(x, 'ctx', 0, 0, axis_index_groups=rings, tiled=True)]
    all_to_all x3 -> x1, starting transfers between devices: 30.5 us -> 11.5 us  [exchange(): return lax.all_to_all(x, 'ctx', 0, 0, axis_index_groups=rings, tiled=True)]
    ppermute x2 -> x4, starting transfers between devices: 7.62 us -> 16.2 us  [the longest x1 7.01 us: shards(): gram = gkeep + lax.ppermute(gsend, 'pb', swap)]
    ppermute x2 -> x4, waiting for transfers between devices: 0.06 us -> 3.23 us  [the longest x1 2.47 us: shards(): lax.ppermute(rsend, 'ctx', across)]
    unnamed x10, local copies, waits for them, and re-layouts: 3.1 us -> 1.65 us
    broadcast_in_dim x2 -> x0, other arithmetic: 1.35 us -> none  [shards(): return (gram[None], rhs[None], gap.reshape(1, heads, rows_dev))]
    pallas_call x5 -> x8, Pallas kernels: 21.4 us -> 21.6 us  [call(): pl.pallas_call(ordered, name=name, out_shape=[jax.ShapeDtypeStruct(s, d)...]
  transfers between devices with their start and end apart: 6 -> 6, of which waited for: 5 -> 4; matrix products, arithmetic and copies ran while one was open for 1% -> 0% of each run, Pallas kernels for 17% -> 13%
where the time goes in v2:
time: 97.8 us; the launch traced here: 97.3 us
  blocking collectives  35.6 us (36%)
  starting transfers between devices  31.1 us (32%)
  Pallas kernels  21.6 us (22%)
  waiting for transfers between devices  6.61 us (7%)
  local copies, waits for them, and re-layouts  1.65 us (2%)
    all_to_all x1, blocking collectives, exchange(): return lax.all_to_all(x, 'ctx', 0, 0, axis_index_groups=rings, tiled=True)  35.6 us
    pallas_call x8, Pallas kernels, call(): pl.pallas_call(ordered, name=name, out_shape=[jax.ShapeDtypeStruct(s, d)...  21.6 us
    all_to_all x1, starting transfers between devices, exchange(): return lax.all_to_all(x, 'ctx', 0, 0, axis_index_groups=rings, tiled=True)  11.5 us
    ppermute x1, starting transfers between devices, shards(): gram = gkeep + lax.ppermute(gsend, 'pb', swap)  7.01 us
    ppermute x1, starting transfers between devices, shards(): came = lax.ppermute(away, 'ctx', across)  3.92 us
    ppermute x1, starting transfers between devices, shards(): other = lax.ppermute(mine, 'pb', swap)  3.47 us
    ppermute x1, starting transfers between devices, shards(): rgot = lax.ppermute(rother, 'pb', swap)  3.06 us
    ppermute x1, waiting for transfers between devices, shards(): lax.ppermute(rsend, 'ctx', across)  2.47 us
  transfers between devices with their start and end apart: 6, of which 4 were waited for; matrix products, arithmetic and copies ran while one was open for 0% of the time, Pallas kernels for 13%

profile of v2, /device:TPU:1, one launch (start us, length us, event | category | flops | bytes accessed | tf_op | source)
XLA Modules:
  0.0 97.3 jit_solution(132308326679152670)
XLA Ops:
  0.6 6.9 %away.1 = (bf16[800,128]{1,0:T(8,128)(2,1)}, bf16[32,128]{1,0:T(8,128)(2,1)}) custom-call(s32[1,64]{1,0:T(1,128)} %refs_0_.1, bf16[1024,128]{1,0:T(8,128)(2,1)} %bitcast.7, bf16[4096,128]{1,0:T(8,128)(2,1)} %bitcast.11, bf16[4096,128]{1,0:T(8,128)(2,1)} %bitcast.13), custom_call_target="tpu_custom_call" | custom-call | flops 1073741824 | bytes 2097152 | tf_op jit(solution)/shard_map/away/pallas_call | solution.py:28
  7.5 3.9 %collective-permute-start = (bf16[800,128]{1,0:T(8,128)(2,1)}, bf16[800,128]{1,0:T(8,128)(2,1)S(1)}, u32[]{:S(2)}, u32[]{:S(2)}) collective-permute-start(bf16[800,128]{1,0:T(8,128)(2,1)} %get-tuple-element.22), channel_id=1, source_target_pairs={{0,256},{16,272},{32,288},{48,304},{64,320},{80,336},{96,352},{112... | collective-permute-start | bytes 614408 | tf_op jit(solution)/shard_map/ppermute | solution.py:318
  11.4 0.0 copy-start.2
  11.5 6.6 %home.1 = (f32[512,128]{1,0:T(8,128)}, f32[8,128]{1,0:T(8,128)}) custom-call(bf16[1024,128]{1,0:T(8,128)(2,1)} %bitcast.8, bf16[4096,128]{1,0:T(8,128)(2,1)} %bitcast.12, bf16[4096,128]{1,0:T(8,128)(2,1)} %bitcast.14, bf16[32,128]{1,0:T(8,128)(2,1)} %get-tuple-element.19.refs_3_), custom_call_target="tpu_custom_call" | custom-call | flops 1073741824 | bytes 2097152 | tf_op jit(solution)/shard_map/home/pallas_call | solution.py:28
  18.0 0.0 copy-start.1
  18.1 0.9 copy-done.1
  19.0 0.7 copy-done.3
  19.7 0.2 pair.1
  19.8 35.6 %all_to_all.10.refs_0_ = bf16[16,112,128]{2,1,0:T(8,128)(2,1)S(1)} all-to-all(bf16[16,112,128]{2,1,0:T(8,128)(2,1)S(1)} %pair.1), channel_id=1, replica_groups={{0,16,32,48,64,80,96,112,128,144,160,176,192,208,224,240},{256,272,288,..., dimensions={0} | all-to-all | bytes 917504 | tf_op jit(solution)/shard_map/all_to_all | solution.py:299
  55.4 1.1 %settle.1 = (bf16[16,48,128]{2,1,0:T(8,128)(2,1)}, bf16[16,64,128]{2,1,0:T(8,128)(2,1)S(1)}) custom-call(bf16[16,112,128]{2,1,0:T(8,128)(2,1)S(1)} %all_to_all.10.refs_0_), custom_call_target="tpu_custom_call" | custom-call | bytes 524288 | tf_op jit(solution)/shard_map/settle/pallas_call | solution.py:28
  56.5 11.5 %all-to-all-start.1 = ((bf16[16,48,128]{2,1,0:T(8,128)(2,1)}), bf16[16,48,128]{2,1,0:T(8,128)(2,1)S(1)}, u32[]{:S(2)}, u32[]{:S(2)}) async-start(bf16[16,48,128]{2,1,0:T(8,128)(2,1)} %get-tuple-element.24.refs_3_), calls=%async_computation.1 | async-start | bytes 393216 | tf_op jit(solution)/shard_map/all_to_all | solution.py:299
  68.0 3.5 %collective-permute-start.1 = (bf16[16,64,128]{2,1,0:T(8,128)(2,1)S(1)}, bf16[16,64,128]{2,1,0:T(8,128)(2,1)S(1)}, u32[]{:S(2)}, u32[]{:S(2)}) collective-permute-start(bf16[16,64,128]{2,1,0:T(8,128)(2,1)S(1)} %get-tuple-element.23.refs_1_), channel_id=1, source_target_pairs={{0,1},{1,0},{2,3},{3,2},{4,5},{5,4},{6,7},{7,6},{8,9},{9,8},{10,11... | collective-permute-start | bytes 786440 | tf_op jit(solution)/shard_map/ppermute | solution.py:339
  71.5 1.0 collective-permute-done.1.refs_2_
  72.4 5.5 %features.1 = (bf16[128,512]{1,0:T(8,128)(2,1)S(1)}, f32[8,128]{1,0:T(8,128)S(1)}, f32[32,2048]{1,0:T(8,128)S(1)}, f32[32,2048]{1,0:T(8,128)S(1)}) custom-call(bf16[1024,128]{1,0:T(8,128)(2,1)S(1)} %bitcast.9, bf16[16,64,128]{2,1,0:T(8,128)(2,1)S(1)} %get-tuple-element.23.refs_1_, bf16[16,64,128]{2,1,0:T(8,128)(2,1)S(1)} %collective-permute-done.1.refs_2_, ...), custom_call_target="tpu_custom_call" | custom-call | flops 805306368 | bytes 1048576 | tf_op jit(solution)/shard_map/features/pallas_call | solution.py:28
  77.9 2.4 %all-to-all-done.1.refs_0_ = bf16[16,48,128]{2,1,0:T(8,128)(2,1)S(1)} async-done(((bf16[16,48,128]{2,1,0:T(8,128)(2,1)}), bf16[16,48,128]{2,1,0:T(8,128)(2,1)S(1)}, u32[]{:S(2)}, u32[]{:S(2)}) %all-to-all-start.1) | async-done | bytes 196640 | tf_op jit(solution)/shard_map/all_to_all | solution.py:299
  80.3 0.2 rhs.1
  80.5 7.0 %collective-permute-start.2 = (f32[32,2048]{1,0:T(8,128)S(1)}, f32[32,2048]{1,0:T(8,128)S(1)}, u32[]{:S(2)}, u32[]{:S(2)}) collective-permute-start(f32[32,2048]{1,0:T(8,128)S(1)} %get-tuple-element.28), channel_id=1, source_target_pairs={{0,1},{1,0},{2,3},{3,2},{4,5},{5,4},{6,7},{7,6},{8,9},{9,8},{10,11... | collective-permute-start | bytes 786440 | tf_op jit(solution)/shard_map/ppermute | solution.py:369
  87.5 2.2 %collective-permute-start.3 = (f32[72,128]{1,0:T(8,128)S(1)}, f32[72,128]{1,0:T(8,128)S(1)}, u32[]{:S(2)}, u32[]{:S(2)}) collective-permute-start(f32[72,128]{1,0:T(8,128)S(1)} %get-tuple-element.30.refs_1_), channel_id=1, source_target_pairs={{0,256},{16,272},{32,288},{48,304},{64,320},{80,336},{96,352},{112... | collective-permute-start | bytes 110600 | tf_op jit(solution)/shard_map/ppermute | solution.py:365
  89.8 2.5 %collective-permute-done.3.refs_2_ = f32[72,128]{1,0:T(8,128)S(1)} collective-permute-done((f32[72,128]{1,0:T(8,128)S(1)}, f32[72,128]{1,0:T(8,128)S(1)}, u32[]{:S(2)}, u32[]{:S(2)}) %collective-permute-start.3) | collective-permute-done | bytes 36896 | tf_op jit(solution)/shard_map/ppermute | solution.py:365
  92.2 0.6 sides.1
  92.8 3.1 %collective-permute-start.4 = (f32[32,128]{1,0:T(8,128)S(1)}, f32[32,128]{1,0:T(8,128)S(1)}, u32[]{:S(2)}, u32[]{:S(2)}) collective-permute-start(f32[32,128]{1,0:T(8,128)S(1)} %get-tuple-element.33), channel_id=1, source_target_pairs={{0,1},{1,0},{2,3},{3,2},{4,5},{5,4},{6,7},{7,6},{8,9},{9,8},{10,11... | collective-permute-start | bytes 49160 | tf_op jit(solution)/shard_map/ppermute | solution.py:370
  96.0 0.0 copy-start
  96.0 0.8 collective-permute-done.4.refs_1_
  96.7 0.6 last.1
  (8 shorter events, 0.0 us)
Async XLA Ops:
  7.5 10.5 %collective-permute-start = (bf16[800,128]{1,0:T(8,128)(2,1)}, bf16[800,128]{1,0:T(8,128)(2,1)S(1)}, u32[]{:S(2)}, u32[]{:S(2)}) collective-permute-start(bf16[800,128]{1,0:T(8,128)(2,1)} %get-tuple-element.22), channel_id=1, source_target_pairs={{0,256},{16,272},{32,288},{48,304},{64,320},{80,336},{96,352},{112... | collective-permute-start | bytes 614408 | tf_op jit(solution)/shard_map/ppermute | solution.py:318
  11.4 6.6 %copy-start.2 = (bf16[32,128]{1,0:T(8,128)(2,1)S(1)}, bf16[32,128]{1,0:T(8,128)(2,1)}, u32[]{:S(2)}) copy-start(bf16[32,128]{1,0:T(8,128)(2,1)} %get-tuple-element.19.refs_3_) | copy-start | bytes 24580
  18.0 1.0 copy-start.1
  19.0 0.7 copy-start.3
  56.5 15.9 %copy-start.4 = (bf16[1,8,128,128]{3,2,1,0:T(8,128)(2,1)S(1)}, bf16[1,8,128,128]{3,2,1,0:T(8,128)(2,1)}, u32[]{:S(2)}) copy-start(bf16[1,8,128,128]{3,2,1,0:T(8,128)(2,1)} %param.4) | copy-start | bytes 786436
  56.5 23.8 %all-to-all-start.1 = ((bf16[16,48,128]{2,1,0:T(8,128)(2,1)}), bf16[16,48,128]{2,1,0:T(8,128)(2,1)S(1)}, u32[]{:S(2)}, u32[]{:S(2)}) async-start(bf16[16,48,128]{2,1,0:T(8,128)(2,1)} %get-tuple-element.24.refs_3_), calls=%async_computation.1 | async-start | bytes 393216 | tf_op jit(solution)/shard_map/all_to_all | solution.py:299
  68.0 4.4 %collective-permute-start.1 = (bf16[16,64,128]{2,1,0:T(8,128)(2,1)S(1)}, bf16[16,64,128]{2,1,0:T(8,128)(2,1)S(1)}, u32[]{:S(2)}, u32[]{:S(2)}) collective-permute-start(bf16[16,64,128]{2,1,0:T(8,128)(2,1)S(1)} %get-tuple-element.23.refs_1_), channel_id=1, source_target_pairs={{0,1},{1,0},{2,3},{3,2},{4,5},{5,4},{6,7},{7,6},{8,9},{9,8},{10,11... | collective-permute-start | bytes 786440 | tf_op jit(solution)/shard_map/ppermute | solution.py:339
  80.5 15.4 %collective-permute-start.2 = (f32[32,2048]{1,0:T(8,128)S(1)}, f32[32,2048]{1,0:T(8,128)S(1)}, u32[]{:S(2)}, u32[]{:S(2)}) collective-permute-start(f32[32,2048]{1,0:T(8,128)S(1)} %get-tuple-element.28), channel_id=1, source_target_pairs={{0,1},{1,0},{2,3},{3,2},{4,5},{5,4},{6,7},{7,6},{8,9},{9,8},{10,11... | collective-permute-start | bytes 786440 | tf_op jit(solution)/shard_map/ppermute | solution.py:369
  87.5 4.7 %collective-permute-start.3 = (f32[72,128]{1,0:T(8,128)S(1)}, f32[72,128]{1,0:T(8,128)S(1)}, u32[]{:S(2)}, u32[]{:S(2)}) collective-permute-start(f32[72,128]{1,0:T(8,128)S(1)} %get-tuple-element.30.refs_1_), channel_id=1, source_target_pairs={{0,256},{16,272},{32,288},{48,304},{64,320},{80,336},{96,352},{112... | collective-permute-start | bytes 110600 | tf_op jit(solution)/shard_map/ppermute | solution.py:365
  92.8 3.9 %collective-permute-start.4 = (f32[32,128]{1,0:T(8,128)S(1)}, f32[32,128]{1,0:T(8,128)S(1)}, u32[]{:S(2)}, u32[]{:S(2)}) collective-permute-start(f32[32,128]{1,0:T(8,128)S(1)} %get-tuple-element.33), channel_id=1, source_target_pairs={{0,1},{1,0},{2,3},{3,2},{4,5},{5,4},{6,7},{7,6},{8,9},{9,8},{10,11... | collective-permute-start | bytes 49160 | tf_op jit(solution)/shard_map/ppermute | solution.py:370
  96.0 1.4 %copy-start = (f32[32,2048]{1,0:T(8,128)}, f32[32,2048]{1,0:T(8,128)S(1)}, u32[]{:S(2)}) copy-start(f32[32,2048]{1,0:T(8,128)S(1)} %add.3.refs_2_) | copy-start | bytes 786436

commit v3 on v2

v3 whole, which is shorter than its diff:
```python
import functools
import math

import jax
import jax.numpy as jnp
from jax import lax
from jax.experimental import pallas as pl
from jax.experimental.pallas import tpu as pltpu
from jax.sharding import PartitionSpec as P

eps = 1e-06
LOG2E = math.log2(math.e)
F32, BF16 = jnp.float32, jnp.bfloat16
VMEM = pl.BlockSpec(memory_space=pltpu.VMEM)
ANY = pl.BlockSpec(memory_space=pl.ANY)
NT = (((1,), (1,)), ((), ()))
TT = (((0,), (0,)), ((), ()))
STAT = 16


def call(name, body, outs, ins, scratch=(), after=(), flops=0, exps=0, moved=0, limit=20):
    count, skip = len(ins), len(after)

    def ordered(*refs):
        body(*refs[:count], *refs[count + skip :])

    return pl.pallas_call(
        ordered,
        name=name,
        out_shape=[jax.ShapeDtypeStruct(s, d) for s, d in outs],
        in_specs=[VMEM] * count + [ANY] * skip,
        out_specs=[VMEM] * len(outs),
        scratch_shapes=list(scratch),
        compiler_params=pltpu.CompilerParams(vmem_limit_bytes=limit << 20),
        cost_estimate=pl.CostEstimate(flops=flops, transcendentals=exps, bytes_accessed=moved),
    )(*ins, *after)


def split3(x):
    hi = x.astype(BF16)
    rest = x - hi.astype(F32)
    mid = rest.astype(BF16)
    low = (rest - mid.astype(F32)).astype(BF16)
    return hi, mid, low


def joined3(a, b, c):
    return (a.astype(F32) + b.astype(F32)) + c.astype(F32)


def packed3(line):
    hi, mid, low = split3(jnp.broadcast_to(line, (STAT, 128)))
    r = lax.broadcasted_iota(jnp.int32, (STAT, 128), 0)
    return jnp.where(r == 0, hi.astype(F32), jnp.where(r == 1, mid.astype(F32), low.astype(F32))).astype(BF16)


def column(line):
    return jnp.broadcast_to(line, (128, 128)).T


def place(ring):
    at = lax.axis_index("ctx")
    return at // ring, at % ring


def pick_body(sel_ref, keys_ref, out_ref):
    peers, half, width = out_ref.shape
    count = sel_ref.shape[1]
    tokens = keys_ref.shape[0]
    base = lax.axis_index("ctx") * tokens
    first = lax.axis_index("pb") * half
    row = lax.broadcasted_iota(jnp.int32, (half, count), 0) + first
    lane = lax.broadcasted_iota(jnp.int32, (half, count), 1)
    sel = jnp.broadcast_to((sel_ref[...] - base).astype(F32), (half, count))
    col = jnp.sum(jnp.where(row == lane, sel, 0.0), axis=1, keepdims=True).astype(jnp.int32)
    step = 512
    acc = jnp.zeros((half, width), F32)
    for k in range(0, tokens, step):
        at = lax.broadcasted_iota(jnp.int32, (half, step), 1) + k
        hot = (at == col).astype(F32).astype(BF16)
        acc += jnp.dot(hot, keys_ref[k : k + step, :], preferred_element_type=F32)
    mine = acc.astype(BF16)
    for p in range(peers):
        out_ref[p] = mine


def attend(ring, away, q_ref, k_ref, v_ref, s_ref):
    tokens, width = k_ref.shape
    rows = s_ref.shape[1]
    step = 512
    c = LOG2E * width**-0.5
    x, _ = place(ring)
    part = 1 - x if away else x
    q = q_ref[pl.ds(pl.multiple_of(part * rows, rows), rows), :]
    mx = None
    for a in range(0, tokens, step):
        s = lax.dot_general(k_ref[a : a + step, :], q, NT, preferred_element_type=F32)
        s_ref[a : a + step, :] = s
        top = jnp.max(s.reshape(step // 8, 8, rows), axis=0)
        mx = top if mx is None else jnp.maximum(mx, top)
    mc = jnp.max(mx, axis=0, keepdims=True) * c
    total, out = jnp.zeros((8, rows), F32), jnp.zeros((width, rows), F32)
    for a in range(0, tokens, step):
        p = jnp.exp2(s_ref[a : a + step, :] * c - mc)
        total = total + jnp.sum(p.reshape(step // 8, 8, rows), axis=0)
        out = out + lax.dot_general(v_ref[a : a + step, :], p.astype(BF16), TT, preferred_element_type=F32)
    total = jnp.sum(total, axis=0, keepdims=True)
    return (out * (1.0 / total)).T, (mc + jnp.log2(total)) * (1.0 / LOG2E)


def away_body(ring, q_ref, k_ref, v_ref, out_ref, s_ref):
    o, lse = attend(ring, True, q_ref, k_ref, v_ref, s_ref)
    rows = o.shape[0]
    share = rows // ring
    per = 128 // share
    o = o.astype(BF16)
    block = share + STAT
    for g in range(rows // 128):
        three = packed3(lse[:, g * 128 : (g + 1) * 128])
        for j in range(g * per, (g + 1) * per):
            out_ref[j, :share, :] = o[j * share : (j + 1) * share, :]
            out_ref[j, share:block, :] = three


def home_body(ring, q_ref, k_ref, v_ref, out_ref, lse_ref, s_ref):
    o, lse = attend(ring, False, q_ref, k_ref, v_ref, s_ref)
    out_ref[...] = o
    lse_ref[...] = jnp.zeros_like(lse_ref)
    for g in range(o.shape[0] // 128):
        lse_ref[g : g + 1, :] = lse[:, g * 128 : (g + 1) * 128]


def pair_body(o_ref, lse_ref, in_ref, out_ref):
    ring, block, _ = out_ref.shape
    share = block - STAT
    rows = o_ref.shape[0]
    per = 128 // share
    for g in range(rows // 128):
        three = in_ref[g * per, share:block, :].astype(F32)
        other = (three[0:1] + three[1:2]) + three[2:3]
        here = lse_ref[g : g + 1, :]
        top = jnp.maximum(other, here)
        wo, wh = jnp.exp(other - top), jnp.exp(here - top)
        total = wo + wh
        lines = packed3(top + jnp.log(total))
        share_of = column(wh / total)
        for j in range(g * per, (g + 1) * per):
            w = share_of[(j % per) * share : (j % per + 1) * share, :]
            a = in_ref[j, :share, :].astype(F32)
            h = o_ref[j * share : (j + 1) * share, :]
            out_ref[j, :share, :] = (a + w * (h - a)).astype(BF16)
            out_ref[j, share:block, :] = lines


def settle_body(in_ref, out_ref, w_ref):
    ring, block, _ = in_ref.shape
    share = block - STAT
    _, z = place(ring)
    lines = in_ref[:, share:block, :].astype(F32)
    lse = (lines[:, 0, :] + lines[:, 1, :]) + lines[:, 2, :]
    top = jnp.max(lse, axis=0, keepdims=True)
    w = jnp.exp(lse - top)
    total = jnp.sum(w, axis=0, keepdims=True)
    w = w / total
    w_ref[...] = jnp.concatenate([w, jnp.zeros((128 - ring, 128), F32)], axis=0).T
    mine = w_ref[pl.ds(pl.multiple_of((z % (128 // share)) * share, share), share), :]
    acc = jnp.zeros((share, 128), F32)
    for b in range(ring):
        acc = acc + mine[:, b : b + 1] * in_ref[b, :share, :].astype(F32)
    y = (acc * lax.rsqrt(jnp.mean(acc * acc, axis=1, keepdims=True) + eps)).astype(BF16)
    three = packed3(top + jnp.log(total))
    for p in range(ring):
        out_ref[p, :share, :] = y
        out_ref[p, share:, :] = three


def features_body(rt, q_ref, mine_ref, other_ref, own_ref, stat_ref, keep_ref, send_ref, c_ref, f_ref, g_ref):
    rows, width = q_ref.shape
    peers, half, _ = mine_ref.shape
    count = 2 * half
    sel = peers * count
    ring = peers // 2
    c = LOG2E * width**-0.5
    pb = lax.axis_index("pb")
    x, z = place(ring)
    for j in range(peers):
        for ref, core in ((mine_ref, pb), (other_ref, 1 - pb)):
            c_ref[pl.ds(pl.multiple_of(j * count + core * half, half), half), :] = ref[j]
    for t in range(rows // rt):
        s = lax.dot_general(c_ref[...], q_ref[t * rt : (t + 1) * rt, :], NT, preferred_element_type=F32)
        mx = jnp.max(s, axis=0, keepdims=True) * c
        e = jnp.exp2(s * c - mx)
        total = jnp.sum(e, axis=0, keepdims=True)
        f_ref[:, t * rt : (t + 1) * rt] = (e * (sel / total)).astype(BF16)
        stat = (mx + jnp.log2(total)) * (1.0 / LOG2E)
        for g in range(rt // 128):
            r = t * (rt // 128) + g
            stat_ref[r : r + 1, :] = stat[:, g * 128 : (g + 1) * 128]
    there = rows // 2
    lanes = pl.ds(pl.multiple_of(x * there, there), there)
    for k, side in ((0, x), (1, 1 - x)):
        at = pl.multiple_of((side * ring + z) * count, count)
        own_ref[k * count : (k + 1) * count, :] = f_ref[pl.ds(at, count), lanes]
    at = lax.axis_index("ctx") * count
    g_ref[:half, :] = f_ref[pl.ds(pl.multiple_of(at + pb * half, half), half), :]
    g_ref[half:, :] = f_ref[pl.ds(pl.multiple_of(at + (1 - pb) * half, half), half), :]
    step = 512
    for k in range(0, sel, step):
        g = lax.dot_general(g_ref[...], f_ref[k : k + step, :], NT, preferred_element_type=F32)
        g = g * (1.0 / (2 * rows))
        keep_ref[:, k : k + step] = g[:half]
        send_ref[:, k : k + step] = g[half:]


def rhs_body(total_rows, in_ref, own_ref, keep_ref, send_ref, y_ref):
    ring, block, _ = in_ref.shape
    share = block - STAT
    count = keep_ref.shape[0]
    rows = ring * share
    for p in range(ring):
        y_ref[p * share : (p + 1) * share, :] = in_ref[p, :share, :]
    g = jnp.dot(own_ref[...], y_ref[...], preferred_element_type=F32) * (1.0 / total_rows)
    keep_ref[...] = g[:count]
    send_ref[:count, :] = g[count:]
    send_ref[count:, :] = jnp.zeros((8, 128), F32)
    per = 128 // share
    lane = lax.broadcasted_iota(jnp.int32, (1, 128), 1)
    for h in range(rows // 128):
        line = jnp.zeros((1, 128), F32)
        for j in range(per):
            v = in_ref[h * per + j, share:block, :].astype(F32)
            v = (v[0:1] + v[1:2]) + v[2:3]
            line = jnp.where((lane >= j * share) & (lane < (j + 1) * share), v, line)
        send_ref[count + h : count + h + 1, :] = line


def sides_body(ring, keep_ref, sent_ref, got_ref, stat_ref, gsend_ref, mine_ref, out_ref, gap_ref, sum_ref):
    count = keep_ref.shape[0]
    half = count // 2
    sel = gsend_ref.shape[1]
    pb = lax.axis_index("pb")
    x, _ = place(ring)
    sum_ref[...] = keep_ref[...] + got_ref[:count, :]
    mine_ref[...] = sum_ref[pl.ds(pl.multiple_of(pb * half, half), half), :]
    out_ref[:, :sel] = gsend_ref[...]
    out_ref[:, sel:] = sum_ref[pl.ds(pl.multiple_of((1 - pb) * half, half), half), :]
    lines = gap_ref.shape[0] // 2
    here, there = sent_ref[count : count + lines, :], got_ref[count : count + lines, :]
    low = jnp.where(x == 0, here, there)
    high = jnp.where(x == 0, there, here)
    gap_ref[:lines, :] = low - stat_ref[:lines, :]
    gap_ref[lines:, :] = high - stat_ref[lines:, :]


def last_body(g_ref, r_ref, in_ref, gram_ref, rhs_ref):
    sel = g_ref.shape[1]
    gram_ref[...] = g_ref[...] + in_ref[:, :sel]
    rhs_ref[...] = r_ref[...] + in_ref[:, sel:]


def shards(queries, cache_keys, cache_values, sel_index):
    heads, rows_dev, width = queries.shape[1:]
    q = queries[0].reshape(-1, width)
    keys, values = cache_keys[0], cache_values[0]
    rows, tokens = q.shape[0], keys.shape[0]
    blocks = lax.axis_size("ctx")
    ring = blocks // 2
    part = rows // 2
    share = part // ring
    block = share + STAT
    count = sel_index.shape[1]
    half = count // 2
    sel = count * blocks
    total_rows = 2 * rows
    swap = [(0, 1), (1, 0)]
    across = [(i, (i + ring) % blocks) for i in range(blocks)]
    rings = [list(range(ring)), list(range(ring, blocks))]

    def exchange(x):
        return lax.all_to_all(x, "ctx", 0, 0, axis_index_groups=rings, tiled=True)

    (picked,) = call(
        "pick", pick_body, [((blocks, half, width), BF16)], (sel_index, keys), flops=2 * half * tokens * width, moved=tokens * width * 2
    )
    mine = lax.all_to_all(picked, "ctx", 0, 0, tiled=True)
    work = dict(flops=4 * part * tokens * width, exps=part * tokens, moved=tokens * width * 4, scratch=[pltpu.VMEM((tokens, part), F32)])
    (away,) = call(
        "away", functools.partial(away_body, ring), [((ring, block, width), BF16)], (q, keys, values), after=(picked,), **work
    )
    came = lax.ppermute(away, "ctx", across)
    home, lse = call(
        "home",
        functools.partial(home_body, ring),
        [((part, width), F32), ((8, 128), F32)],
        (q, keys, values),
        after=(away,),
        **work,
    )
    (parts,) = call("pair", pair_body, [((ring, block, width), BF16)], (home, lse, came), moved=part * width * 12)
    other = lax.ppermute(mine, "pb", swap)
    (told,) = call(
        "settle",
        settle_body,
        [((ring, block, width), BF16)],
        (exchange(parts),),
        after=(other,),
        scratch=[pltpu.VMEM((128, 128), F32)],
        moved=part * width * 8,
    )
    heard = exchange(told)
    own, stat, gkeep, gsend = call(
        "features",
        functools.partial(features_body, 256),
        [((2 * count, part), BF16), ((rows // 128, 128), F32), ((half, sel), F32), ((half, sel), F32)],
        (q, mine, other),
        after=(told,),
        scratch=[pltpu.VMEM((sel, width), BF16), pltpu.VMEM((sel, rows), BF16), pltpu.VMEM((count, rows), BF16)],
        flops=2 * rows * sel * (width + count),
        exps=rows * sel,
        moved=sel * width * 4,
    )
    rkeep, rsend = call(
        "rhs",
        functools.partial(rhs_body, total_rows),
        [((count, width), F32), ((count + 8, width), F32)],
        (heard, own),
        scratch=[pltpu.VMEM((part, width), BF16)],
        flops=4 * count * part * width,
        moved=part * width * 2,
    )
    rmine, send, gap = call(
        "sides",
        functools.partial(sides_body, ring),
        [((half, width), F32), ((half, sel + width), F32), ((rows // 128, 128), F32)],
        (rkeep, rsend, lax.ppermute(rsend, "ctx", across), stat, gsend),
        scratch=[pltpu.VMEM((count, width), F32)],
        moved=half * sel * 8,
    )
    gram, rhs = call(
        "last",
        last_body,
        [((half, sel), F32), ((half, width), F32)],
        (gkeep, rmine, lax.ppermute(send, "pb", swap)),
        moved=half * sel * 12,
    )
    return (gram[None], rhs[None], gap.reshape(1, heads, rows_dev))


def solution(mesh):
    in_specs = (
        P("kv", None, "pb", None),
        P("kv", "ctx", None),
        P("kv", "ctx", None),
        P("kv", "ctx"),
    )
    out_specs = (P("kv", ("ctx", "pb"), None), P("kv", ("ctx", "pb"), None), P("kv", None, "pb"))
    return jax.shard_map(shards, mesh=mesh, in_specs=in_specs, out_specs=out_specs, check_vma=False)
```

time: 97.8 us -> 96.8 us (0.990)
  blocking collectives: 35.6 us -> 0 us
  waiting for transfers between devices: 6.61 us -> 26.3 us
  starting transfers between devices: 31.1 us -> 48.8 us
  Pallas kernels: 21.6 us -> 17.2 us
  local copies, waits for them, and re-layouts: 1.65 us -> 3.1 us
    all_to_all x1 -> x0, blocking collectives: 35.6 us -> none  [exchange(): return lax.all_to_all(x, 'ctx', 0, 0, axis_index_groups=rings, tiled=True)]
    all_to_all x0 -> x1, starting transfers between devices: none -> 17.1 us  [shards(): mine = lax.all_to_all(picked, 'ctx', 0, 0, tiled=True)]
    all_to_all x1 -> x2, waiting for transfers between devices: 2.42 us -> 15.5 us  [exchange(): return lax.all_to_all(x, 'ctx', 0, 0, axis_index_groups=rings, tiled=True)]
    all_to_all x0 -> x1, waiting for transfers between devices: none -> 5.24 us  [shards(): mine = lax.all_to_all(picked, 'ctx', 0, 0, tiled=True)]
    pallas_call x8 -> x9, Pallas kernels: 21.6 us -> 17.2 us  [call(): pl.pallas_call(ordered, name=name, out_shape=[jax.ShapeDtypeStruct(s, d)...]
    all_to_all x1 -> x2, starting transfers between devices: 11.5 us -> 13.7 us  [exchange(): return lax.all_to_all(x, 'ctx', 0, 0, axis_index_groups=rings, tiled=True)]
    ppermute x1, waiting for transfers between devices: 0.01 us -> 2.24 us  [shards(): came = lax.ppermute(away, 'ctx', across)]
    ppermute x2 -> x1, starting transfers between devices: 10.1 us -> 8.35 us  [shards(): lax.ppermute(send, 'pb', swap)]
  transfers between devices with their start and end apart: 6 -> 7, of which waited for: 4 -> 6; matrix products, arithmetic and copies ran while one was open for 0% -> 0% of each run, Pallas kernels for 13% -> 14%
where the time goes in v3:
time: 96.8 us; the launch traced here: 96.2 us
  starting transfers between devices  48.8 us (50%)
  waiting for transfers between devices  26.3 us (27%)
  Pallas kernels  17.2 us (18%)
  local copies, waits for them, and re-layouts  3.1 us (3%)
    pallas_call x9, Pallas kernels, call(): pl.pallas_call(ordered, name=name, out_shape=[jax.ShapeDtypeStruct(s, d)...  17.2 us
    all_to_all x1, starting transfers between devices, shards(): mine = lax.all_to_all(picked, 'ctx', 0, 0, tiled=True)  17.1 us
    all_to_all x2, waiting for transfers between devices, exchange(): return lax.all_to_all(x, 'ctx', 0, 0, axis_index_groups=rings, tiled=True)  15.5 us
    all_to_all x2, starting transfers between devices, exchange(): return lax.all_to_all(x, 'ctx', 0, 0, axis_index_groups=rings, tiled=True)  13.7 us
    ppermute x1, starting transfers between devices, shards(): lax.ppermute(send, 'pb', swap)  8.35 us
    all_to_all x1, waiting for transfers between devices, shards(): mine = lax.all_to_all(picked, 'ctx', 0, 0, tiled=True)  5.24 us
    ppermute x1, starting transfers between devices, shards(): other = lax.ppermute(mine, 'pb', swap)  3.72 us
    ppermute x1, starting transfers between devices, shards(): came = lax.ppermute(away, 'ctx', across)  3.15 us
  transfers between devices with their start and end apart: 7, of which 6 were waited for; matrix products, arithmetic and copies ran while one was open for 0% of the time, Pallas kernels for 14%

profile of v3, /device:TPU:1, one launch (start us, length us, event | category | flops | bytes accessed | tf_op | source)
XLA Modules:
  0.0 96.2 jit_solution(12283196909185375103)
XLA Ops:
  0.6 0.6 copy-done.2
  1.3 1.2 %copy-done = bf16[1,4096,128]{2,1,0:T(8,128)(2,1)S(1)} copy-done((bf16[1,4096,128]{2,1,0:T(8,128)(2,1)S(1)}, bf16[1,4096,128]{2,1,0:T(8,128)(2,1)}, u32[]{:S(2)}) %copy-start) | copy-done | bytes 1048600
  2.5 1.1 %pick.1.refs_3_ = bf16[32,32,128]{2,1,0:T(8,128)(2,1)} custom-call(s32[1,64]{1,0:T(1,128)S(1)} %copy-done.2, bf16[4096,128]{1,0:T(8,128)(2,1)S(1)} %bitcast.6), custom_call_target="tpu_custom_call" | custom-call | flops 33554432 | bytes 1048576 | tf_op jit(solution)/shard_map/pick/pallas_call | solution.py:27
  3.6 17.1 %all-to-all-start = ((bf16[32,32,128]{2,1,0:T(8,128)(2,1)}), bf16[32,32,128]{2,1,0:T(8,128)(2,1)S(1)}, u32[]{:S(2)}, u32[]{:S(2)}) async-start(bf16[32,32,128]{2,1,0:T(8,128)(2,1)} %pick.1.refs_3_), calls=%async_computation | async-start | bytes 524288 | tf_op jit(solution)/shard_map/all_to_all | solution.py:285
  20.7 1.2 %copy-done.3 = bf16[1,4096,128]{2,1,0:T(8,128)(2,1)S(1)} copy-done((bf16[1,4096,128]{2,1,0:T(8,128)(2,1)S(1)}, bf16[1,4096,128]{2,1,0:T(8,128)(2,1)}, u32[]{:S(2)}) %copy-start.3) | copy-done | bytes 1048600
  21.9 3.8 %away.1.refs_3_ = bf16[16,48,128]{2,1,0:T(8,128)(2,1)S(1)} custom-call(bf16[1024,128]{1,0:T(8,128)(2,1)S(1)} %bitcast.11, bf16[4096,128]{1,0:T(8,128)(2,1)S(1)} %bitcast.7, bf16[4096,128]{1,0:T(8,128)(2,1)S(1)} %bitcast.9, bf16[32,32,128]{2,1,0:T(8,128)(2,1)} %pick.1.refs_3_), custom_call_target="tpu_custom_call" | custom-call | flops 1073741824 | bytes 2097152 | tf_op jit(solution)/shard_map/away/pallas_call | solution.py:27
  25.7 3.1 %collective-permute-start.1 = (bf16[16,48,128]{2,1,0:T(8,128)(2,1)S(1)}, bf16[16,48,128]{2,1,0:T(8,128)(2,1)S(1)}, u32[]{:S(2)}, u32[]{:S(2)}) collective-permute-start(bf16[16,48,128]{2,1,0:T(8,128)(2,1)S(1)} %away.1.refs_3_), channel_id=1, source_target_pairs={{0,256},{16,272},{32,288},{48,304},{64,320},{80,336},{96,352},{112... | collective-permute-start | bytes 589832 | tf_op jit(solution)/shard_map/ppermute | solution.py:290
  28.9 3.5 %home.1 = (f32[512,128]{1,0:T(8,128)S(1)}, f32[8,128]{1,0:T(8,128)S(1)}) custom-call(bf16[1024,128]{1,0:T(8,128)(2,1)S(1)} %bitcast.12, bf16[4096,128]{1,0:T(8,128)(2,1)S(1)} %bitcast.8, bf16[4096,128]{1,0:T(8,128)(2,1)S(1)} %bitcast.10, bf16[16,48,128]{2,1,0:T(8,128)(2,1)S(1)} %away.1.refs_3_), custom_call_target="tpu_custom_call" | custom-call | flops 1073741824 | bytes 2097152 | tf_op jit(solution)/shard_map/home/pallas_call | solution.py:27
  32.4 2.2 %collective-permute-done.1.refs_2_ = bf16[16,48,128]{2,1,0:T(8,128)(2,1)S(1)} collective-permute-done((bf16[16,48,128]{2,1,0:T(8,128)(2,1)S(1)}, bf16[16,48,128]{2,1,0:T(8,128)(2,1)S(1)}, u32[]{:S(2)}, u32[]{:S(2)}) %collective-permute-start.1) | collective-permute-done | bytes 196640 | tf_op jit(solution)/shard_map/ppermute | solution.py:290
  34.6 0.8 pair.1
  35.4 5.2 %all-to-all-done.refs_1_ = bf16[32,32,128]{2,1,0:T(8,128)(2,1)S(1)} async-done(((bf16[32,32,128]{2,1,0:T(8,128)(2,1)}), bf16[32,32,128]{2,1,0:T(8,128)(2,1)S(1)}, u32[]{:S(2)}, u32[]{:S(2)}) %all-to-all-start) | async-done | bytes 262176 | tf_op jit(solution)/shard_map/all_to_all | solution.py:285
  40.7 5.9 %all-to-all-start.1 = ((bf16[16,48,128]{2,1,0:T(8,128)(2,1)}), bf16[16,48,128]{2,1,0:T(8,128)(2,1)S(1)}, u32[]{:S(2)}, u32[]{:S(2)}) async-start(bf16[16,48,128]{2,1,0:T(8,128)(2,1)} %pair.1), calls=%async_computation.1 | async-start | bytes 393216 | tf_op jit(solution)/shard_map/all_to_all | solution.py:280
  46.6 3.7 %collective-permute-start = (bf16[32,32,128]{2,1,0:T(8,128)(2,1)S(1)}, bf16[32,32,128]{2,1,0:T(8,128)(2,1)S(1)}, u32[]{:S(2)}, u32[]{:S(2)}) collective-permute-start(bf16[32,32,128]{2,1,0:T(8,128)(2,1)S(1)} %all-to-all-done.refs_1_), channel_id=1, source_target_pairs={{0,1},{1,0},{2,3},{3,2},{4,5},{5,4},{6,7},{7,6},{8,9},{9,8},{10,11... | collective-permute-start | bytes 786440 | tf_op jit(solution)/shard_map/ppermute | solution.py:300
  50.3 8.6 %all-to-all-done.1.refs_0_ = bf16[16,48,128]{2,1,0:T(8,128)(2,1)S(1)} async-done(((bf16[16,48,128]{2,1,0:T(8,128)(2,1)}), bf16[16,48,128]{2,1,0:T(8,128)(2,1)S(1)}, u32[]{:S(2)}, u32[]{:S(2)}) %all-to-all-start.1) | async-done | bytes 196640 | tf_op jit(solution)/shard_map/all_to_all | solution.py:280
  58.9 1.1 %settle.1.refs_3_ = bf16[16,48,128]{2,1,0:T(8,128)(2,1)} custom-call(bf16[16,48,128]{2,1,0:T(8,128)(2,1)S(1)} %all-to-all-done.1.refs_0_, bf16[32,32,128]{2,1,0:T(8,128)(2,1)S(1)} %collective-permute-done.refs_1_.refs_2_), custom_call_target="tpu_custom_call" | custom-call | bytes 524288 | tf_op jit(solution)/shard_map/settle/pallas_call | solution.py:27
  60.0 7.8 %all-to-all-start.2 = ((bf16[16,48,128]{2,1,0:T(8,128)(2,1)}), bf16[16,48,128]{2,1,0:T(8,128)(2,1)S(1)}, u32[]{:S(2)}, u32[]{:S(2)}) async-start(bf16[16,48,128]{2,1,0:T(8,128)(2,1)} %settle.1.refs_3_), calls=%async_computation.2 | async-start | bytes 393216 | tf_op jit(solution)/shard_map/all_to_all | solution.py:280
  67.8 5.4 %features.1 = (bf16[128,512]{1,0:T(8,128)(2,1)S(1)}, f32[8,128]{1,0:T(8,128)S(1)}, f32[32,2048]{1,0:T(8,128)S(1)}, f32[32,2048]{1,0:T(8,128)S(1)}) custom-call(bf16[1024,128]{1,0:T(8,128)(2,1)S(1)} %bitcast.13, bf16[32,32,128]{2,1,0:T(8,128)(2,1)S(1)} %all-to-all-done.refs_1_, bf16[32,32,128]{2,1,0:T(8,128)(2,1)S(1)} %collective-permute-done.refs_1_.refs_2_, ...), custom_call_target="tpu_custom_call" | custom-call | flops 805306368 | bytes 1048576 | tf_op jit(solution)/shard_map/features/pallas_call | solution.py:27
  73.3 6.9 %all-to-all-done.2.refs_0_ = bf16[16,48,128]{2,1,0:T(8,128)(2,1)S(1)} async-done(((bf16[16,48,128]{2,1,0:T(8,128)(2,1)}), bf16[16,48,128]{2,1,0:T(8,128)(2,1)S(1)}, u32[]{:S(2)}, u32[]{:S(2)}) %all-to-all-start.2) | async-done | bytes 196640 | tf_op jit(solution)/shard_map/all_to_all | solution.py:280
  80.4 2.8 %collective-permute-start.2 = (f32[72,128]{1,0:T(8,128)S(1)}, f32[72,128]{1,0:T(8,128)S(1)}, u32[]{:S(2)}, u32[]{:S(2)}) collective-permute-start(f32[72,128]{1,0:T(8,128)S(1)} %get-tuple-element.21.refs_1_), channel_id=1, source_target_pairs={{0,256},{16,272},{32,288},{48,304},{64,320},{80,336},{96,352},{112... | collective-permute-start | bytes 110600 | tf_op jit(solution)/shard_map/ppermute | solution.py:335
  83.2 2.2 %collective-permute-done.2.refs_2_ = f32[72,128]{1,0:T(8,128)S(1)} collective-permute-done((f32[72,128]{1,0:T(8,128)S(1)}, f32[72,128]{1,0:T(8,128)S(1)}, u32[]{:S(2)}, u32[]{:S(2)}) %collective-permute-start.2) | collective-permute-done | bytes 36896 | tf_op jit(solution)/shard_map/ppermute | solution.py:335
  85.4 0.6 sides.1
  86.0 8.3 %collective-permute-start.3 = (f32[32,2176]{1,0:T(8,128)S(1)}, f32[32,2176]{1,0:T(8,128)S(1)}, u32[]{:S(2)}, u32[]{:S(2)}) collective-permute-start(f32[32,2176]{1,0:T(8,128)S(1)} %get-tuple-element.25), channel_id=1, source_target_pairs={{0,1},{1,0},{2,3},{3,2},{4,5},{5,4},{6,7},{7,6},{8,9},{9,8},{10,11... | collective-permute-start | bytes 835592 | tf_op jit(solution)/shard_map/ppermute | solution.py:343
  94.3 1.2 %collective-permute-done.3.refs_2_ = f32[32,2176]{1,0:T(8,128)S(1)} collective-permute-done((f32[32,2176]{1,0:T(8,128)S(1)}, f32[32,2176]{1,0:T(8,128)S(1)}, u32[]{:S(2)}, u32[]{:S(2)}) %collective-permute-start.3) | collective-permute-done | bytes 278560 | tf_op jit(solution)/shard_map/ppermute | solution.py:343
  95.5 0.7 last.1
  (11 shorter events, 0.2 us)
Async XLA Ops:
  0.6 0.7 copy-start.2
  1.3 1.2 %copy-start = (bf16[1,4096,128]{2,1,0:T(8,128)(2,1)S(1)}, bf16[1,4096,128]{2,1,0:T(8,128)(2,1)}, u32[]{:S(2)}) copy-start(bf16[1,4096,128]{2,1,0:T(8,128)(2,1)} %param.5) | copy-start | bytes 3145732
  2.5 18.2 %copy-start.1 = (bf16[1,4096,128]{2,1,0:T(8,128)(2,1)S(1)}, bf16[1,4096,128]{2,1,0:T(8,128)(2,1)}, u32[]{:S(2)}) copy-start(bf16[1,4096,128]{2,1,0:T(8,128)(2,1)} %param.5) | copy-start | bytes 3145732
  3.6 17.1 %copy-start.5 = (bf16[1,8,128,128]{3,2,1,0:T(8,128)(2,1)S(1)}, bf16[1,8,128,128]{3,2,1,0:T(8,128)(2,1)}, u32[]{:S(2)}) copy-start(bf16[1,8,128,128]{3,2,1,0:T(8,128)(2,1)} %param.4) | copy-start | bytes 786436
  3.6 37.1 %all-to-all-start = ((bf16[32,32,128]{2,1,0:T(8,128)(2,1)}), bf16[32,32,128]{2,1,0:T(8,128)(2,1)S(1)}, u32[]{:S(2)}, u32[]{:S(2)}) async-start(bf16[32,32,128]{2,1,0:T(8,128)(2,1)} %pick.1.refs_3_), calls=%async_computation | async-start | bytes 524288 | tf_op jit(solution)/shard_map/all_to_all | solution.py:285
  20.7 1.2 %copy-start.3 = (bf16[1,4096,128]{2,1,0:T(8,128)(2,1)S(1)}, bf16[1,4096,128]{2,1,0:T(8,128)(2,1)}, u32[]{:S(2)}) copy-start(bf16[1,4096,128]{2,1,0:T(8,128)(2,1)} %param.6) | copy-start | bytes 3145732
  21.9 6.9 %copy-start.4 = (bf16[1,4096,128]{2,1,0:T(8,128)(2,1)S(1)}, bf16[1,4096,128]{2,1,0:T(8,128)(2,1)}, u32[]{:S(2)}) copy-start(bf16[1,4096,128]{2,1,0:T(8,128)(2,1)} %param.6) | copy-start | bytes 3145732
  25.7 8.9 %collective-permute-start.1 = (bf16[16,48,128]{2,1,0:T(8,128)(2,1)S(1)}, bf16[16,48,128]{2,1,0:T(8,128)(2,1)S(1)}, u32[]{:S(2)}, u32[]{:S(2)}) collective-permute-start(bf16[16,48,128]{2,1,0:T(8,128)(2,1)S(1)} %away.1.refs_3_), channel_id=1, source_target_pairs={{0,256},{16,272},{32,288},{48,304},{64,320},{80,336},{96,352},{112... | collective-permute-start | bytes 589832 | tf_op jit(solution)/shard_map/ppermute | solution.py:290
  40.7 18.2 %all-to-all-start.1 = ((bf16[16,48,128]{2,1,0:T(8,128)(2,1)}), bf16[16,48,128]{2,1,0:T(8,128)(2,1)S(1)}, u32[]{:S(2)}, u32[]{:S(2)}) async-start(bf16[16,48,128]{2,1,0:T(8,128)(2,1)} %pair.1), calls=%async_computation.1 | async-start | bytes 393216 | tf_op jit(solution)/shard_map/all_to_all | solution.py:280
  46.6 12.3 %collective-permute-start = (bf16[32,32,128]{2,1,0:T(8,128)(2,1)S(1)}, bf16[32,32,128]{2,1,0:T(8,128)(2,1)S(1)}, u32[]{:S(2)}, u32[]{:S(2)}) collective-permute-start(bf16[32,32,128]{2,1,0:T(8,128)(2,1)S(1)} %all-to-all-done.refs_1_), channel_id=1, source_target_pairs={{0,1},{1,0},{2,3},{3,2},{4,5},{5,4},{6,7},{7,6},{8,9},{9,8},{10,11... | collective-permute-start | bytes 786440 | tf_op jit(solution)/shard_map/ppermute | solution.py:300
  60.0 20.2 %all-to-all-start.2 = ((bf16[16,48,128]{2,1,0:T(8,128)(2,1)}), bf16[16,48,128]{2,1,0:T(8,128)(2,1)S(1)}, u32[]{:S(2)}, u32[]{:S(2)}) async-start(bf16[16,48,128]{2,1,0:T(8,128)(2,1)} %settle.1.refs_3_), calls=%async_computation.2 | async-start | bytes 393216 | tf_op jit(solution)/shard_map/all_to_all | solution.py:280
  80.4 5.0 %collective-permute-start.2 = (f32[72,128]{1,0:T(8,128)S(1)}, f32[72,128]{1,0:T(8,128)S(1)}, u32[]{:S(2)}, u32[]{:S(2)}) collective-permute-start(f32[72,128]{1,0:T(8,128)S(1)} %get-tuple-element.21.refs_1_), channel_id=1, source_target_pairs={{0,256},{16,272},{32,288},{48,304},{64,320},{80,336},{96,352},{112... | collective-permute-start | bytes 110600 | tf_op jit(solution)/shard_map/ppermute | solution.py:335
  86.0 9.5 %collective-permute-start.3 = (f32[32,2176]{1,0:T(8,128)S(1)}, f32[32,2176]{1,0:T(8,128)S(1)}, u32[]{:S(2)}, u32[]{:S(2)}) collective-permute-start(f32[32,2176]{1,0:T(8,128)S(1)} %get-tuple-element.25), channel_id=1, source_target_pairs={{0,1},{1,0},{2,3},{3,2},{4,5},{5,4},{6,7},{7,6},{8,9},{9,8},{10,11... | collective-permute-start | bytes 835592 | tf_op jit(solution)/shard_map/ppermute | solution.py:343

commit v4 on v2

--- a/solution.py
+++ b/solution.py
@@ -18,24 +18,22 @@
 STAT = 16
 
 
-def call(name, body, outs, ins, scratch=(), after=(), held=None, specs=(), flops=0, exps=0, moved=0, limit=20):
-    count, skip, here = len(ins), len(after) + (held is not None), len(outs)
-    more = [held] if held is not None else []
+def call(name, body, outs, ins, scratch=(), after=(), specs=(), flops=0, exps=0, moved=0, limit=20):
+    count, skip = len(ins), len(after)
 
     def ordered(*refs):
-        body(*refs[:count], *refs[count + skip : count + skip + here], *refs[count + skip + here + len(more) :])
+        body(*refs[:count], *refs[count + skip :])
 
     return pl.pallas_call(
         ordered,
         name=name,
-        out_shape=[jax.ShapeDtypeStruct(s, d) for s, d in outs] + [jax.ShapeDtypeStruct(m.shape, m.dtype) for m in more],
+        out_shape=[jax.ShapeDtypeStruct(s, d) for s, d in outs],
         in_specs=(list(specs) or [VMEM] * count) + [ANY] * skip,
-        out_specs=[VMEM] * here + [ANY] * len(more),
-        input_output_aliases={count + skip - 1: here} if more else {},
+        out_specs=[VMEM] * len(outs),
         scratch_shapes=list(scratch),
-        compiler_params=pltpu.CompilerParams(vmem_limit_bytes=limit << 20),
+        compiler_params=pltpu.CompilerParams(vmem_limit_bytes=int(limit * 2**20)),
         cost_estimate=pl.CostEstimate(flops=flops, transcendentals=exps, bytes_accessed=moved),
-    )(*ins, *after, *more)
+    )(*ins, *after)
 
 
 def split3(x):
@@ -73,28 +71,22 @@
     x, _ = place(ring)
     part = 1 - x if away else x
     copies = [pltpu.make_async_copy(q_hbm.at[pl.ds(pl.multiple_of(part * rows, rows), rows)], q_ref, sem.at[0])]
-    for ref, hbm in ((k_ref, k_hbm), (v_ref, v_hbm)):
-        for a in range(0, tokens, step):
-            cut = pl.ds(a, step)
-            copies.append(pltpu.make_async_copy(hbm.at[cut], ref.at[cut], sem.at[len(copies)]))
+    copies += [pltpu.make_async_copy(k_hbm, k_ref, sem.at[1]), pltpu.make_async_copy(v_hbm, v_ref, sem.at[2])]
     for copy in copies:
         copy.start()
     copies[0].wait()
+    copies[1].wait()
     q = q_ref[...]
-    chunks = tokens // step
     mx = None
-    for n in range(chunks):
-        copies[1 + n].wait()
-        a = n * step
+    for a in range(0, tokens, step):
         s = lax.dot_general(k_ref[a : a + step, :], q, NT, preferred_element_type=F32)
         s_ref[a : a + step, :] = s
         top = jnp.max(s.reshape(step // 8, 8, rows), axis=0)
         mx = top if mx is None else jnp.maximum(mx, top)
     mc = jnp.max(mx, axis=0, keepdims=True) * c
     total, out = jnp.zeros((8, rows), F32), jnp.zeros((width, rows), F32)
-    for n in range(chunks):
-        copies[1 + chunks + n].wait()
-        a = n * step
+    copies[2].wait()
+    for a in range(0, tokens, step):
         p = jnp.exp2(s_ref[a : a + step, :] * c - mc)
         total = total + jnp.sum(p.reshape(step // 8, 8, rows), axis=0)
         out = out + lax.dot_general(v_ref[a : a + step, :], p.astype(BF16), TT, preferred_element_type=F32)
@@ -257,14 +249,16 @@
         send_ref[count + h : count + h + 1, :] = line
 
 
-def sides_body(ring, keep_ref, sent_ref, got_ref, stat_ref, mine_ref, other_ref, gap_ref, sum_ref):
+def sides_body(ring, keep_ref, sent_ref, got_ref, stat_ref, gsend_ref, mine_ref, out_ref, gap_ref, sum_ref):
     count = keep_ref.shape[0]
     half = count // 2
+    sel = gsend_ref.shape[1]
     pb = lax.axis_index("pb")
     x, _ = place(ring)
     sum_ref[...] = keep_ref[...] + got_ref[:count, :]
     mine_ref[...] = sum_ref[pl.ds(pl.multiple_of(pb * half, half), half), :]
-    other_ref[...] = sum_ref[pl.ds(pl.multiple_of((1 - pb) * half, half), half), :]
+    out_ref[:, :sel] = gsend_ref[...]
+    out_ref[:, sel:] = sum_ref[pl.ds(pl.multiple_of((1 - pb) * half, half), half), :]
     lines = gap_ref.shape[0] // 2
     here, there = sent_ref[count : count + lines, :], got_ref[count : count + lines, :]
     low = jnp.where(x == 0, here, there)
@@ -273,8 +267,10 @@
     gap_ref[lines:, :] = high - stat_ref[lines:, :]
 
 
-def last_body(a_ref, b_ref, out_ref):
-    out_ref[...] = a_ref[...] + b_ref[...]
+def last_body(g_ref, r_ref, in_ref, gram_ref, rhs_ref):
+    sel = g_ref.shape[1]
+    gram_ref[...] = g_ref[...] + in_ref[:, :sel]
+    rhs_ref[...] = r_ref[...] + in_ref[:, sel:]
 
 
 def shards(queries, cache_keys, cache_values, sel_index):
@@ -303,9 +299,9 @@
         pltpu.VMEM((tokens, width), BF16),
         pltpu.VMEM((tokens, width), BF16),
         pltpu.VMEM((tokens, part), F32),
-        pltpu.SemaphoreType.DMA((1 + 2 * (tokens // 512),)),
+        pltpu.SemaphoreType.DMA((3,)),
     ]
-    work = dict(flops=4 * part * tokens * width, exps=part * tokens, moved=tokens * width * 4, limit=60)
+    work = dict(flops=4 * part * tokens * width, exps=part * tokens, moved=tokens * width * 4, limit=60.0)
     away, picked = call(
         "away",
         functools.partial(away_body, ring),
@@ -324,7 +320,7 @@
         specs=[ANY] * 3,
         after=(picked,),
         scratch=held,
-        **work,
+        **(work | dict(limit=53.5)),
     )
     (parts,) = call("pair", pair_body, [((ring, block + count, width), BF16)], (home, lse, came, picked), moved=part * width * 12)
     told, mine = call(
@@ -348,27 +344,30 @@
         exps=rows * sel,
         moved=sel * width * 4,
     )
-    rkeep, rsend, gsend = call(
+    rkeep, rsend = call(
         "rhs",
         functools.partial(rhs_body, total_rows),
         [((count, width), F32), ((count + 8, width), F32)],
         (heard, own),
-        held=gsend,
         scratch=[pltpu.VMEM((part, width), BF16)],
         flops=4 * count * part * width,
         moved=part * width * 2,
     )
-    rmine, rother, gap = call(
+    rmine, send, gap = call(
         "sides",
         functools.partial(sides_body, ring),
-        [((half, width), F32), ((half, width), F32), ((rows // 128, 128), F32)],
-        (rkeep, rsend, lax.ppermute(rsend, "ctx", across), stat),
+        [((half, width), F32), ((half, sel + width), F32), ((rows // 128, 128), F32)],
+        (rkeep, rsend, lax.ppermute(rsend, "ctx", across), stat, gsend),
         scratch=[pltpu.VMEM((count, width), F32)],
-        moved=count * width * 16,
-    )
-    gram = gkeep + lax.ppermute(gsend, "pb", swap)
-    rgot = lax.ppermute(rother, "pb", swap)
-    (rhs,) = call("last", last_body, [((half, width), F32)], (rmine, rgot), after=(gram,), moved=half * width * 12)
+        moved=half * sel * 8,
+    )
+    gram, rhs = call(
+        "last",
+        last_body,
+        [((half, sel), F32), ((half, width), F32)],
+        (gkeep, rmine, lax.ppermute(send, "pb", swap)),
+        moved=half * sel * 12,
+    )
     return (gram[None], rhs[None], gap.reshape(1, heads, rows_dev))
 
 

time: 97.8 us -> 91.8 us (0.939)
  Pallas kernels: 21.6 us -> 18.1 us
  starting transfers between devices: 31.1 us -> 29.8 us
    pallas_call x8, Pallas kernels: 21.6 us -> 18.1 us  [call(): pl.pallas_call(ordered, name=name, out_shape=[jax.ShapeDtypeStruct(s, d)...]
    ppermute x2 -> x1, starting transfers between devices: 10.1 us -> 8.03 us  [shards(): lax.ppermute(send, 'pb', swap)]
  transfers between devices with their start and end apart: 6 -> 5, of which waited for: 4 -> 4; matrix products, arithmetic and copies ran while one was open for 0% -> 0% of each run, Pallas kernels for 13% -> 11%
where the time goes in v4:
time: 91.8 us; the launch traced here: 91.4 us
  blocking collectives  34.9 us (38%)
  starting transfers between devices  29.8 us (32%)
  Pallas kernels  18.1 us (20%)
  waiting for transfers between devices  7.13 us (8%)
    all_to_all x1, blocking collectives, exchange(): return lax.all_to_all(x, 'ctx', 0, 0, axis_index_groups=rings, tiled=True)  34.9 us
    pallas_call x8, Pallas kernels, call(): pl.pallas_call(ordered, name=name, out_shape=[jax.ShapeDtypeStruct(s, d)...  18.1 us
    all_to_all x1, starting transfers between devices, exchange(): return lax.all_to_all(x, 'ctx', 0, 0, axis_index_groups=rings, tiled=True)  12.3 us
    ppermute x1, starting transfers between devices, shards(): lax.ppermute(send, 'pb', swap)  8.03 us
    ppermute x1, starting transfers between devices, shards(): came = lax.ppermute(away, 'ctx', across)  3.94 us
    ppermute x1, starting transfers between devices, shards(): other = lax.ppermute(mine, 'pb', swap)  3.08 us
    all_to_all x1, waiting for transfers between devices, exchange(): return lax.all_to_all(x, 'ctx', 0, 0, axis_index_groups=rings, tiled=True)  2.64 us
    ppermute x1, starting transfers between devices, shards(): lax.ppermute(rsend, 'ctx', across)  2.52 us
  transfers between devices with their start and end apart: 5, of which 4 were waited for; matrix products, arithmetic and copies ran while one was open for 0% of the time, Pallas kernels for 11%

profile of v4, /device:TPU:1, one launch (start us, length us, event | category | flops | bytes accessed | tf_op | source)
XLA Modules:
  0.0 91.4 jit_solution(7469870770997055947)
XLA Ops:
  0.6 5.4 %away.1 = (bf16[800,128]{1,0:T(8,128)(2,1)}, bf16[32,128]{1,0:T(8,128)(2,1)}) custom-call(s32[1,64]{1,0:T(1,128)} %refs_0_.1, bf16[1024,128]{1,0:T(8,128)(2,1)} %bitcast.6, bf16[4096,128]{1,0:T(8,128)(2,1)} %bitcast.9, bf16[4096,128]{1,0:T(8,128)(2,1)} %bitcast.11), custom_call_target="tpu_custom_call" | custom-call | flops 1073741824 | bytes 2097152 | tf_op jit(solution)/shard_map/away/pallas_call | solution.py:27
  6.0 3.9 %collective-permute-start = (bf16[800,128]{1,0:T(8,128)(2,1)}, bf16[800,128]{1,0:T(8,128)(2,1)S(1)}, u32[]{:S(2)}, u32[]{:S(2)}) collective-permute-start(bf16[800,128]{1,0:T(8,128)(2,1)} %get-tuple-element.23), channel_id=1, source_target_pairs={{0,256},{16,272},{32,288},{48,304},{64,320},{80,336},{96,352},{112... | collective-permute-start | bytes 614408 | tf_op jit(solution)/shard_map/ppermute | solution.py:314
  10.0 0.0 copy-start
  10.0 0.7 copy-done
  10.7 4.4 %home.1 = (f32[512,128]{1,0:T(8,128)S(1)}, f32[8,128]{1,0:T(8,128)S(1)}) custom-call(bf16[1024,128]{1,0:T(8,128)(2,1)} %bitcast.7, bf16[4096,128]{1,0:T(8,128)(2,1)} %bitcast.10, bf16[4096,128]{1,0:T(8,128)(2,1)} %bitcast.12, bf16[32,128]{1,0:T(8,128)(2,1)S(1)} %copy-done), custom_call_target="tpu_custom_call" | custom-call | flops 1073741824 | bytes 2097152 | tf_op jit(solution)/shard_map/home/pallas_call | solution.py:27
  15.1 0.0 collective-permute-done.refs_2_
  15.1 0.2 pair.1
  15.3 34.9 %all_to_all.10.refs_0_ = bf16[16,112,128]{2,1,0:T(8,128)(2,1)S(1)} all-to-all(bf16[16,112,128]{2,1,0:T(8,128)(2,1)S(1)} %pair.1), channel_id=1, replica_groups={{0,16,32,48,64,80,96,112,128,144,160,176,192,208,224,240},{256,272,288,..., dimensions={0} | all-to-all | bytes 917504 | tf_op jit(solution)/shard_map/all_to_all | solution.py:295
  50.2 1.1 %settle.1 = (bf16[16,48,128]{2,1,0:T(8,128)(2,1)}, bf16[16,64,128]{2,1,0:T(8,128)(2,1)S(1)}) custom-call(bf16[16,112,128]{2,1,0:T(8,128)(2,1)S(1)} %all_to_all.10.refs_0_), custom_call_target="tpu_custom_call" | custom-call | bytes 524288 | tf_op jit(solution)/shard_map/settle/pallas_call | solution.py:27
  51.3 0.0 copy-start.1
  51.3 12.3 %all-to-all-start.1 = ((bf16[16,48,128]{2,1,0:T(8,128)(2,1)}), bf16[16,48,128]{2,1,0:T(8,128)(2,1)S(1)}, u32[]{:S(2)}, u32[]{:S(2)}) async-start(bf16[16,48,128]{2,1,0:T(8,128)(2,1)} %get-tuple-element.25.refs_3_), calls=%async_computation.1 | async-start | bytes 393216 | tf_op jit(solution)/shard_map/all_to_all | solution.py:295
  63.6 3.1 %collective-permute-start.1 = (bf16[16,64,128]{2,1,0:T(8,128)(2,1)S(1)}, bf16[16,64,128]{2,1,0:T(8,128)(2,1)S(1)}, u32[]{:S(2)}, u32[]{:S(2)}) collective-permute-start(bf16[16,64,128]{2,1,0:T(8,128)(2,1)S(1)} %get-tuple-element.24.refs_1_), channel_id=1, source_target_pairs={{0,1},{1,0},{2,3},{3,2},{4,5},{5,4},{6,7},{7,6},{8,9},{9,8},{10,11... | collective-permute-start | bytes 786440 | tf_op jit(solution)/shard_map/ppermute | solution.py:335
  66.7 1.1 %collective-permute-done.1.refs_2_ = bf16[16,64,128]{2,1,0:T(8,128)(2,1)S(1)} collective-permute-done((bf16[16,64,128]{2,1,0:T(8,128)(2,1)S(1)}, bf16[16,64,128]{2,1,0:T(8,128)(2,1)S(1)}, u32[]{:S(2)}, u32[]{:S(2)}) %collective-permute-start.1) | collective-permute-done | bytes 262176 | tf_op jit(solution)/shard_map/ppermute | solution.py:335
  67.8 0.0 copy-done.1
  67.8 5.5 %features.1 = (bf16[128,512]{1,0:T(8,128)(2,1)S(1)}, f32[8,128]{1,0:T(8,128)S(1)}, f32[32,2048]{1,0:T(8,128)S(1)}, f32[32,2048]{1,0:T(8,128)S(1)}) custom-call(bf16[1024,128]{1,0:T(8,128)(2,1)S(1)} %bitcast.8, bf16[16,64,128]{2,1,0:T(8,128)(2,1)S(1)} %get-tuple-element.24.refs_1_, bf16[16,64,128]{2,1,0:T(8,128)(2,1)S(1)} %collective-permute-done.1.refs_2_, ...), custom_call_target="tpu_custom_call" | custom-call | flops 805306368 | bytes 1048576 | tf_op jit(solution)/shard_map/features/pallas_call | solution.py:27
  73.3 2.6 %all-to-all-done.1.refs_0_ = bf16[16,48,128]{2,1,0:T(8,128)(2,1)S(1)} async-done(((bf16[16,48,128]{2,1,0:T(8,128)(2,1)}), bf16[16,48,128]{2,1,0:T(8,128)(2,1)S(1)}, u32[]{:S(2)}, u32[]{:S(2)}) %all-to-all-start.1) | async-done | bytes 196640 | tf_op jit(solution)/shard_map/all_to_all | solution.py:295
  75.9 0.2 rhs.1
  76.1 2.5 %collective-permute-start.2 = (f32[72,128]{1,0:T(8,128)S(1)}, f32[72,128]{1,0:T(8,128)S(1)}, u32[]{:S(2)}, u32[]{:S(2)}) collective-permute-start(f32[72,128]{1,0:T(8,128)S(1)} %get-tuple-element.29.refs_1_), channel_id=1, source_target_pairs={{0,256},{16,272},{32,288},{48,304},{64,320},{80,336},{96,352},{112... | collective-permute-start | bytes 110600 | tf_op jit(solution)/shard_map/ppermute | solution.py:360
  78.7 2.2 %collective-permute-done.2.refs_2_ = f32[72,128]{1,0:T(8,128)S(1)} collective-permute-done((f32[72,128]{1,0:T(8,128)S(1)}, f32[72,128]{1,0:T(8,128)S(1)}, u32[]{:S(2)}, u32[]{:S(2)}) %collective-permute-start.2) | collective-permute-done | bytes 36896 | tf_op jit(solution)/shard_map/ppermute | solution.py:360
  80.8 0.6 sides.1
  81.5 8.0 %collective-permute-start.3 = (f32[32,2176]{1,0:T(8,128)S(1)}, f32[32,2176]{1,0:T(8,128)S(1)}, u32[]{:S(2)}, u32[]{:S(2)}) collective-permute-start(f32[32,2176]{1,0:T(8,128)S(1)} %get-tuple-element.33), channel_id=1, source_target_pairs={{0,1},{1,0},{2,3},{3,2},{4,5},{5,4},{6,7},{7,6},{8,9},{9,8},{10,11... | collective-permute-start | bytes 835592 | tf_op jit(solution)/shard_map/ppermute | solution.py:368
  89.5 1.2 %collective-permute-done.3.refs_2_ = f32[32,2176]{1,0:T(8,128)S(1)} collective-permute-done((f32[32,2176]{1,0:T(8,128)S(1)}, f32[32,2176]{1,0:T(8,128)S(1)}, u32[]{:S(2)}, u32[]{:S(2)}) %collective-permute-start.3) | collective-permute-done | bytes 278560 | tf_op jit(solution)/shard_map/ppermute | solution.py:368
  90.7 0.7 last.1
Async XLA Ops:
  6.0 9.0 %collective-permute-start = (bf16[800,128]{1,0:T(8,128)(2,1)}, bf16[800,128]{1,0:T(8,128)(2,1)S(1)}, u32[]{:S(2)}, u32[]{:S(2)}) collective-permute-start(bf16[800,128]{1,0:T(8,128)(2,1)} %get-tuple-element.23), channel_id=1, source_target_pairs={{0,256},{16,272},{32,288},{48,304},{64,320},{80,336},{96,352},{112... | collective-permute-start | bytes 614408 | tf_op jit(solution)/shard_map/ppermute | solution.py:314
  10.0 0.7 copy-start
  51.3 16.5 %copy-start.1 = (bf16[1,8,128,128]{3,2,1,0:T(8,128)(2,1)S(1)}, bf16[1,8,128,128]{3,2,1,0:T(8,128)(2,1)}, u32[]{:S(2)}) copy-start(bf16[1,8,128,128]{3,2,1,0:T(8,128)(2,1)} %param.4) | copy-start | bytes 786436
  51.3 24.7 %all-to-all-start.1 = ((bf16[16,48,128]{2,1,0:T(8,128)(2,1)}), bf16[16,48,128]{2,1,0:T(8,128)(2,1)S(1)}, u32[]{:S(2)}, u32[]{:S(2)}) async-start(bf16[16,48,128]{2,1,0:T(8,128)(2,1)} %get-tuple-element.25.refs_3_), calls=%async_computation.1 | async-start | bytes 393216 | tf_op jit(solution)/shard_map/all_to_all | solution.py:295
  63.6 4.2 %collective-permute-start.1 = (bf16[16,64,128]{2,1,0:T(8,128)(2,1)S(1)}, bf16[16,64,128]{2,1,0:T(8,128)(2,1)S(1)}, u32[]{:S(2)}, u32[]{:S(2)}) collective-permute-start(bf16[16,64,128]{2,1,0:T(8,128)(2,1)S(1)} %get-tuple-element.24.refs_1_), channel_id=1, source_target_pairs={{0,1},{1,0},{2,3},{3,2},{4,5},{5,4},{6,7},{7,6},{8,9},{9,8},{10,11... | collective-permute-start | bytes 786440 | tf_op jit(solution)/shard_map/ppermute | solution.py:335
  76.1 4.7 %collective-permute-start.2 = (f32[72,128]{1,0:T(8,128)S(1)}, f32[72,128]{1,0:T(8,128)S(1)}, u32[]{:S(2)}, u32[]{:S(2)}) collective-permute-start(f32[72,128]{1,0:T(8,128)S(1)} %get-tuple-element.29.refs_1_), channel_id=1, source_target_pairs={{0,256},{16,272},{32,288},{48,304},{64,320},{80,336},{96,352},{112... | collective-permute-start | bytes 110600 | tf_op jit(solution)/shard_map/ppermute | solution.py:360
  81.5 9.2 %collective-permute-start.3 = (f32[32,2176]{1,0:T(8,128)S(1)}, f32[32,2176]{1,0:T(8,128)S(1)}, u32[]{:S(2)}, u32[]{:S(2)}) collective-permute-start(f32[32,2176]{1,0:T(8,128)S(1)} %get-tuple-element.33), channel_id=1, source_target_pairs={{0,1},{1,0},{2,3},{3,2},{4,5},{5,4},{6,7},{7,6},{8,9},{9,8},{10,11... | collective-permute-start | bytes 835592 | tf_op jit(solution)/shard_map/ppermute | solution.py:368

commit v5 on v4

--- a/solution.py
+++ b/solution.py
@@ -15,7 +15,8 @@
 ANY = pl.BlockSpec(memory_space=pl.ANY)
 NT = (((1,), (1,)), ((), ()))
 TT = (((0,), (0,)), ((), ()))
-STAT = 16
+STAT = 8
+FIRST = 12
 
 
 def call(name, body, outs, ins, scratch=(), after=(), specs=(), flops=0, exps=0, moved=0, limit=20):
@@ -58,6 +59,10 @@
     return jnp.broadcast_to(line, (128, 128)).T
 
 
+def slot(z, ring):
+    return (z - FIRST) % ring
+
+
 def place(ring):
     at = lax.axis_index("ctx")
     return at // ring, at % ring
@@ -71,7 +76,9 @@
     x, _ = place(ring)
     part = 1 - x if away else x
     copies = [pltpu.make_async_copy(q_hbm.at[pl.ds(pl.multiple_of(part * rows, rows), rows)], q_ref, sem.at[0])]
-    copies += [pltpu.make_async_copy(k_hbm, k_ref, sem.at[1]), pltpu.make_async_copy(v_hbm, v_ref, sem.at[2])]
+    cuts = [pl.ds(0, tokens // 4), pl.ds(tokens // 4, tokens - tokens // 4)]
+    copies += [pltpu.make_async_copy(k_hbm.at[cut], k_ref.at[cut], sem.at[1 + n]) for n, cut in enumerate(cuts)]
+    copies.append(pltpu.make_async_copy(v_hbm, v_ref, sem.at[3]))
     for copy in copies:
         copy.start()
     copies[0].wait()
@@ -79,13 +86,15 @@
     q = q_ref[...]
     mx = None
     for a in range(0, tokens, step):
+        if a == tokens // 4:
+            copies[2].wait()
         s = lax.dot_general(k_ref[a : a + step, :], q, NT, preferred_element_type=F32)
         s_ref[a : a + step, :] = s
         top = jnp.max(s.reshape(step // 8, 8, rows), axis=0)
         mx = top if mx is None else jnp.maximum(mx, top)
     mc = jnp.max(mx, axis=0, keepdims=True) * c
     total, out = jnp.zeros((8, rows), F32), jnp.zeros((width, rows), F32)
-    copies[2].wait()
+    copies[3].wait()
     for a in range(0, tokens, step):
         p = jnp.exp2(s_ref[a : a + step, :] * c - mc)
         total = total + jnp.sum(p.reshape(step // 8, 8, rows), axis=0)
@@ -103,12 +112,11 @@
     share = rows // ring
     per = 128 // share
     o = o.astype(BF16)
-    block = share + STAT
     for g in range(rows // 128):
         three = packed3(lse[:, g * 128 : (g + 1) * 128])
         for j in range(g * per, (g + 1) * per):
-            out_ref[j * block : j * block + share, :] = o[j * share : (j + 1) * share, :]
-            out_ref[j * block + share : (j + 1) * block, :] = three
+            out_ref[j, :share, :] = o[j * share : (j + 1) * share, :]
+            out_ref[j, share:, :] = three
     fetch.wait()
     half = pick_ref.shape[0]
     count = sel_ref.shape[1]
@@ -126,7 +134,7 @@
         acc += jnp.dot(hot, k_ref[k : k + step, :], preferred_element_type=F32)
     mine = acc.astype(BF16)
     pick_ref[...] = mine
-    out_ref[ring * block : ring * block + half, :] = mine
+    out_ref[ring, :half, :] = mine
 
 
 def home_body(ring, q_hbm, k_hbm, v_hbm, out_ref, lse_ref, q_ref, k_ref, v_ref, s_ref, sem):
@@ -138,16 +146,14 @@
 
 
 def pair_body(o_ref, lse_ref, in_ref, pick_ref, out_ref):
-    ring = out_ref.shape[0]
+    ring, length, _ = out_ref.shape
     rows = o_ref.shape[0]
     half = pick_ref.shape[0]
     share = rows // ring
     per = 128 // share
-    block = share + STAT
-    mine, theirs = pick_ref[...], in_ref[ring * block : ring * block + half, :]
+    mine, theirs = pick_ref[...], in_ref[ring, :half, :]
     for g in range(rows // 128):
-        at = g * per * block
-        three = in_ref[at + share : at + block, :].astype(F32)
+        three = in_ref[g * per, share:, :].astype(F32)
         other = (three[0:1] + three[1:2]) + three[2:3]
         here = lse_ref[g : g + 1, :]
         top = jnp.maximum(other, here)
@@ -157,19 +163,19 @@
         share_of = column(wh / total)
         for j in range(g * per, (g + 1) * per):
             w = share_of[(j % per) * share : (j % per + 1) * share, :]
-            a = in_ref[j * block : j * block + share, :].astype(F32)
+            a = in_ref[j, :share, :].astype(F32)
             h = o_ref[j * share : (j + 1) * share, :]
-            out_ref[j, :share, :] = (a + w * (h - a)).astype(BF16)
-            out_ref[j, share:block, :] = lines
-            out_ref[j, block : block + half, :] = mine
-            out_ref[j, block + half :, :] = theirs
+            to = slot(j, ring)
+            out_ref[to, :share, :] = (a + w * (h - a)).astype(BF16)
+            out_ref[to, share : share + half, :] = mine
+            out_ref[to, share + half : length - STAT, :] = theirs
+            out_ref[to, length - STAT :, :] = lines
 
 
 def settle_body(share, in_ref, out_ref, keys_ref, w_ref):
-    ring = in_ref.shape[0]
-    block = share + STAT
+    ring, length, _ = in_ref.shape
     _, z = place(ring)
-    lines = in_ref[:, share:block, :].astype(F32)
+    lines = in_ref[:, length - STAT :, :].astype(F32)
     lse = (lines[:, 0, :] + lines[:, 1, :]) + lines[:, 2, :]
     top = jnp.max(lse, axis=0, keepdims=True)
     w = jnp.exp(lse - top)
@@ -185,7 +191,7 @@
     for p in range(ring):
         out_ref[p, :share, :] = y
         out_ref[p, share:, :] = three
-        keys_ref[p] = in_ref[p, block:, :]
+        keys_ref[p] = in_ref[p, share : length - STAT, :]
 
 
 def features_body(rt, q_ref, mine_ref, other_ref, own_ref, stat_ref, keep_ref, send_ref, c_ref, f_ref, g_ref):
@@ -200,7 +206,7 @@
         for ref, core in ((mine_ref, pb), (other_ref, 1 - pb)):
             for k, side in ((0, x), (1, 1 - x)):
                 at = pl.multiple_of((side * ring + j) * count + core * half, half)
-                c_ref[pl.ds(at, half), :] = ref[j, k * half : (k + 1) * half, :]
+                c_ref[pl.ds(at, half), :] = ref[slot(j, ring), k * half : (k + 1) * half, :]
     for t in range(rows // rt):
         s = lax.dot_general(c_ref[...], q_ref[t * rt : (t + 1) * rt, :], NT, preferred_element_type=F32)
         mx = jnp.max(s, axis=0, keepdims=True) * c
@@ -233,7 +239,7 @@
     count = keep_ref.shape[0]
     rows = ring * share
     for p in range(ring):
-        y_ref[p * share : (p + 1) * share, :] = in_ref[p, :share, :]
+        y_ref[p * share : (p + 1) * share, :] = in_ref[slot(p, ring), :share, :]
     g = jnp.dot(own_ref[...], y_ref[...], preferred_element_type=F32) * (1.0 / total_rows)
     keep_ref[...] = g[:count]
     send_ref[:count, :] = g[count:]
@@ -243,7 +249,7 @@
     for h in range(rows // 128):
         line = jnp.zeros((1, 128), F32)
         for j in range(per):
-            v = in_ref[h * per + j, share:block, :].astype(F32)
+            v = in_ref[slot(h * per + j, ring), share:, :].astype(F32)
             v = (v[0:1] + v[1:2]) + v[2:3]
             line = jnp.where((lane >= j * share) & (lane < (j + 1) * share), v, line)
         send_ref[count + h : count + h + 1, :] = line
@@ -289,7 +295,7 @@
     total_rows = 2 * rows
     swap = [(0, 1), (1, 0)]
     across = [(i, (i + ring) % blocks) for i in range(blocks)]
-    rings = [list(range(ring)), list(range(ring, blocks))]
+    rings = [[side + (j + FIRST) % ring for j in range(ring)] for side in (0, ring)]
 
     def exchange(x):
         return lax.all_to_all(x, "ctx", 0, 0, axis_index_groups=rings, tiled=True)
@@ -299,13 +305,13 @@
         pltpu.VMEM((tokens, width), BF16),
         pltpu.VMEM((tokens, width), BF16),
         pltpu.VMEM((tokens, part), F32),
-        pltpu.SemaphoreType.DMA((3,)),
+        pltpu.SemaphoreType.DMA((4,)),
     ]
     work = dict(flops=4 * part * tokens * width, exps=part * tokens, moved=tokens * width * 4, limit=60.0)
     away, picked = call(
         "away",
         functools.partial(away_body, ring),
-        [((ring * block + half, width), BF16), ((half, width), BF16)],
+        [((ring + 1, block, width), BF16), ((half, width), BF16)],
         (sel_index, q, keys, values),
         specs=[ANY] * 4,
         scratch=[pltpu.VMEM((1, count), jnp.int32), *held, pltpu.SemaphoreType.DMA],
@@ -318,7 +324,6 @@
         [((part, width), F32), ((8, 128), F32)],
         (q, keys, values),
         specs=[ANY] * 3,
-        after=(picked,),
         scratch=held,
         **(work | dict(limit=53.5)),
     )

time: 91.8 us -> 85.9 us (0.936)
  waiting for transfers between devices: 7.13 us -> 4.75 us
  starting transfers between devices: 29.8 us -> 28.1 us
  blocking collectives: 34.9 us -> 33.6 us
    all_to_all x1, waiting for transfers between devices: 2.64 us -> 0.38 us  [exchange(): return lax.all_to_all(x, 'ctx', 0, 0, axis_index_groups=rings, tiled=True)]
    ppermute x1, starting transfers between devices: 8.03 us -> 5.79 us  [shards(): lax.ppermute(send, 'pb', swap)]
    all_to_all x1, blocking collectives: 34.9 us -> 33.6 us  [exchange(): return lax.all_to_all(x, 'ctx', 0, 0, axis_index_groups=rings, tiled=True)]
  transfers between devices with their start and end apart: 5 -> 5, of which waited for: 4 -> 4; matrix products, arithmetic and copies ran while one was open for 0% -> 0% of each run, Pallas kernels for 11% -> 12%
where the time goes in v5:
time: 85.9 us; the launch traced here: 85.5 us
  blocking collectives  33.6 us (39%)
  starting transfers between devices  28.1 us (33%)
  Pallas kernels  18.3 us (21%)
  waiting for transfers between devices  4.75 us (6%)
    all_to_all x1, blocking collectives, exchange(): return lax.all_to_all(x, 'ctx', 0, 0, axis_index_groups=rings, tiled=True)  33.6 us
    pallas_call x8, Pallas kernels, call(): pl.pallas_call(ordered, name=name, out_shape=[jax.ShapeDtypeStruct(s, d)...  18.3 us
    all_to_all x1, starting transfers between devices, exchange(): return lax.all_to_all(x, 'ctx', 0, 0, axis_index_groups=rings, tiled=True)  12.3 us
    ppermute x1, starting transfers between devices, shards(): lax.ppermute(send, 'pb', swap)  5.79 us
    ppermute x1, starting transfers between devices, shards(): came = lax.ppermute(away, 'ctx', across)  3.95 us
    ppermute x1, starting transfers between devices, shards(): other = lax.ppermute(mine, 'pb', swap)  3.44 us
    ppermute x1, starting transfers between devices, shards(): lax.ppermute(rsend, 'ctx', across)  2.63 us
    ppermute x1, waiting for transfers between devices, shards(): lax.ppermute(rsend, 'ctx', across)  2.07 us
  transfers between devices with their start and end apart: 5, of which 4 were waited for; matrix products, arithmetic and copies ran while one was open for 0% of the time, Pallas kernels for 12%

profile of v5, /device:TPU:1, one launch (start us, length us, event | category | flops | bytes accessed | tf_op | source)
XLA Modules:
  0.0 85.5 jit_solution(7994814226606628952)
XLA Ops:
  0.6 5.5 %away.1 = (bf16[17,40,128]{2,1,0:T(8,128)(2,1)}, bf16[32,128]{1,0:T(8,128)(2,1)}) custom-call(s32[1,64]{1,0:T(1,128)} %refs_0_.1, bf16[1024,128]{1,0:T(8,128)(2,1)} %bitcast.6, bf16[4096,128]{1,0:T(8,128)(2,1)} %bitcast.9, bf16[4096,128]{1,0:T(8,128)(2,1)} %bitcast.11), custom_call_target="tpu_custom_call" | custom-call | flops 1073741824 | bytes 2097152 | tf_op jit(solution)/shard_map/away/pallas_call | solution.py:28
  6.2 4.0 %collective-permute-start = (bf16[17,40,128]{2,1,0:T(8,128)(2,1)}, bf16[17,40,128]{2,1,0:T(8,128)(2,1)S(1)}, u32[]{:S(2)}, u32[]{:S(2)}) collective-permute-start(bf16[17,40,128]{2,1,0:T(8,128)(2,1)} %get-tuple-element.22), channel_id=1, source_target_pairs={{0,256},{16,272},{32,288},{48,304},{64,320},{80,336},{96,352},{112... | collective-permute-start | bytes 522248 | tf_op jit(solution)/shard_map/ppermute | solution.py:320
  10.1 0.0 copy-start
  10.1 4.5 %home.1 = (f32[512,128]{1,0:T(8,128)S(1)}, f32[8,128]{1,0:T(8,128)S(1)}) custom-call(bf16[1024,128]{1,0:T(8,128)(2,1)} %bitcast.7, bf16[4096,128]{1,0:T(8,128)(2,1)} %bitcast.10, bf16[4096,128]{1,0:T(8,128)(2,1)} %bitcast.12), custom_call_target="tpu_custom_call" | custom-call | flops 1073741824 | bytes 2097152 | tf_op jit(solution)/shard_map/home/pallas_call | solution.py:28
  14.6 0.0 collective-permute-done.refs_2_
  14.7 0.0 copy-done
  14.7 0.2 pair.1
  14.8 33.6 %all_to_all.10.refs_0_ = bf16[16,104,128]{2,1,0:T(8,128)(2,1)S(1)} all-to-all(bf16[16,104,128]{2,1,0:T(8,128)(2,1)S(1)} %pair.1), channel_id=1, replica_groups={{192,208,224,240,0,16,32,48,64,80,96,112,128,144,160,176},{448,464,480,..., dimensions={0} | all-to-all | bytes 851968 | tf_op jit(solution)/shard_map/all_to_all | solution.py:301
  48.4 1.1 %settle.1 = (bf16[16,40,128]{2,1,0:T(8,128)(2,1)}, bf16[16,64,128]{2,1,0:T(8,128)(2,1)S(1)}) custom-call(bf16[16,104,128]{2,1,0:T(8,128)(2,1)S(1)} %all_to_all.10.refs_0_), custom_call_target="tpu_custom_call" | custom-call | bytes 524288 | tf_op jit(solution)/shard_map/settle/pallas_call | solution.py:28
  49.5 0.0 copy-start.1
  49.5 12.3 %all-to-all-start.1 = ((bf16[16,40,128]{2,1,0:T(8,128)(2,1)}), bf16[16,40,128]{2,1,0:T(8,128)(2,1)S(1)}, u32[]{:S(2)}, u32[]{:S(2)}) async-start(bf16[16,40,128]{2,1,0:T(8,128)(2,1)} %get-tuple-element.25.refs_3_), calls=%async_computation.1 | async-start | bytes 327680 | tf_op jit(solution)/shard_map/all_to_all | solution.py:301
  61.8 3.4 %collective-permute-start.1 = (bf16[16,64,128]{2,1,0:T(8,128)(2,1)S(1)}, bf16[16,64,128]{2,1,0:T(8,128)(2,1)S(1)}, u32[]{:S(2)}, u32[]{:S(2)}) collective-permute-start(bf16[16,64,128]{2,1,0:T(8,128)(2,1)S(1)} %get-tuple-element.24.refs_1_), channel_id=1, source_target_pairs={{0,1},{1,0},{2,3},{3,2},{4,5},{5,4},{6,7},{7,6},{8,9},{9,8},{10,11... | collective-permute-start | bytes 786440 | tf_op jit(solution)/shard_map/ppermute | solution.py:340
  65.3 1.1 %collective-permute-done.1.refs_2_ = bf16[16,64,128]{2,1,0:T(8,128)(2,1)S(1)} collective-permute-done((bf16[16,64,128]{2,1,0:T(8,128)(2,1)S(1)}, bf16[16,64,128]{2,1,0:T(8,128)(2,1)S(1)}, u32[]{:S(2)}, u32[]{:S(2)}) %collective-permute-start.1) | collective-permute-done | bytes 262176 | tf_op jit(solution)/shard_map/ppermute | solution.py:340
  66.4 0.0 copy-done.1
  66.4 5.5 %features.1 = (bf16[128,512]{1,0:T(8,128)(2,1)S(1)}, f32[8,128]{1,0:T(8,128)S(1)}, f32[32,2048]{1,0:T(8,128)S(1)}, f32[32,2048]{1,0:T(8,128)S(1)}) custom-call(bf16[1024,128]{1,0:T(8,128)(2,1)S(1)} %bitcast.8, bf16[16,64,128]{2,1,0:T(8,128)(2,1)S(1)} %get-tuple-element.24.refs_1_, bf16[16,64,128]{2,1,0:T(8,128)(2,1)S(1)} %collective-permute-done.1.refs_2_, ...), custom_call_target="tpu_custom_call" | custom-call | flops 805306368 | bytes 1048576 | tf_op jit(solution)/shard_map/features/pallas_call | solution.py:28
  71.9 0.4 all-to-all-done.1.refs_0_
  72.3 0.2 rhs.1
  72.5 2.6 %collective-permute-start.2 = (f32[72,128]{1,0:T(8,128)S(1)}, f32[72,128]{1,0:T(8,128)S(1)}, u32[]{:S(2)}, u32[]{:S(2)}) collective-permute-start(f32[72,128]{1,0:T(8,128)S(1)} %get-tuple-element.29.refs_1_), channel_id=1, source_target_pairs={{0,256},{16,272},{32,288},{48,304},{64,320},{80,336},{96,352},{112... | collective-permute-start | bytes 110600 | tf_op jit(solution)/shard_map/ppermute | solution.py:365
  75.1 2.1 %collective-permute-done.2.refs_2_ = f32[72,128]{1,0:T(8,128)S(1)} collective-permute-done((f32[72,128]{1,0:T(8,128)S(1)}, f32[72,128]{1,0:T(8,128)S(1)}, u32[]{:S(2)}, u32[]{:S(2)}) %collective-permute-start.2) | collective-permute-done | bytes 36896 | tf_op jit(solution)/shard_map/ppermute | solution.py:365
  77.2 0.6 sides.1
  77.8 5.8 %collective-permute-start.3 = (f32[32,2176]{1,0:T(8,128)S(1)}, f32[32,2176]{1,0:T(8,128)S(1)}, u32[]{:S(2)}, u32[]{:S(2)}) collective-permute-start(f32[32,2176]{1,0:T(8,128)S(1)} %get-tuple-element.33), channel_id=1, source_target_pairs={{0,1},{1,0},{2,3},{3,2},{4,5},{5,4},{6,7},{7,6},{8,9},{9,8},{10,11... | collective-permute-start | bytes 835592 | tf_op jit(solution)/shard_map/ppermute | solution.py:373
  83.6 1.2 %collective-permute-done.3.refs_2_ = f32[32,2176]{1,0:T(8,128)S(1)} collective-permute-done((f32[32,2176]{1,0:T(8,128)S(1)}, f32[32,2176]{1,0:T(8,128)S(1)}, u32[]{:S(2)}, u32[]{:S(2)}) %collective-permute-start.3) | collective-permute-done | bytes 278560 | tf_op jit(solution)/shard_map/ppermute | solution.py:373
  84.8 0.7 last.1
Async XLA Ops:
  6.2 8.5 %collective-permute-start = (bf16[17,40,128]{2,1,0:T(8,128)(2,1)}, bf16[17,40,128]{2,1,0:T(8,128)(2,1)S(1)}, u32[]{:S(2)}, u32[]{:S(2)}) collective-permute-start(bf16[17,40,128]{2,1,0:T(8,128)(2,1)} %get-tuple-element.22), channel_id=1, source_target_pairs={{0,256},{16,272},{32,288},{48,304},{64,320},{80,336},{96,352},{112... | collective-permute-start | bytes 522248 | tf_op jit(solution)/shard_map/ppermute | solution.py:320
  10.1 4.5 %copy-start = (bf16[32,128]{1,0:T(8,128)(2,1)S(1)}, bf16[32,128]{1,0:T(8,128)(2,1)}, u32[]{:S(2)}) copy-start(bf16[32,128]{1,0:T(8,128)(2,1)} %get-tuple-element.23.refs_3_) | copy-start | bytes 24580
  49.5 16.9 %copy-start.1 = (bf16[1,8,128,128]{3,2,1,0:T(8,128)(2,1)S(1)}, bf16[1,8,128,128]{3,2,1,0:T(8,128)(2,1)}, u32[]{:S(2)}) copy-start(bf16[1,8,128,128]{3,2,1,0:T(8,128)(2,1)} %param.4) | copy-start | bytes 786436
  49.5 22.8 %all-to-all-start.1 = ((bf16[16,40,128]{2,1,0:T(8,128)(2,1)}), bf16[16,40,128]{2,1,0:T(8,128)(2,1)S(1)}, u32[]{:S(2)}, u32[]{:S(2)}) async-start(bf16[16,40,128]{2,1,0:T(8,128)(2,1)} %get-tuple-element.25.refs_3_), calls=%async_computation.1 | async-start | bytes 327680 | tf_op jit(solution)/shard_map/all_to_all | solution.py:301
  61.8 4.6 %collective-permute-start.1 = (bf16[16,64,128]{2,1,0:T(8,128)(2,1)S(1)}, bf16[16,64,128]{2,1,0:T(8,128)(2,1)S(1)}, u32[]{:S(2)}, u32[]{:S(2)}) collective-permute-start(bf16[16,64,128]{2,1,0:T(8,128)(2,1)S(1)} %get-tuple-element.24.refs_1_), channel_id=1, source_target_pairs={{0,1},{1,0},{2,3},{3,2},{4,5},{5,4},{6,7},{7,6},{8,9},{9,8},{10,11... | collective-permute-start | bytes 786440 | tf_op jit(solution)/shard_map/ppermute | solution.py:340
  72.5 4.7 %collective-permute-start.2 = (f32[72,128]{1,0:T(8,128)S(1)}, f32[72,128]{1,0:T(8,128)S(1)}, u32[]{:S(2)}, u32[]{:S(2)}) collective-permute-start(f32[72,128]{1,0:T(8,128)S(1)} %get-tuple-element.29.refs_1_), channel_id=1, source_target_pairs={{0,256},{16,272},{32,288},{48,304},{64,320},{80,336},{96,352},{112... | collective-permute-start | bytes 110600 | tf_op jit(solution)/shard_map/ppermute | solution.py:365
  77.8 7.0 %collective-permute-start.3 = (f32[32,2176]{1,0:T(8,128)S(1)}, f32[32,2176]{1,0:T(8,128)S(1)}, u32[]{:S(2)}, u32[]{:S(2)}) collective-permute-start(f32[32,2176]{1,0:T(8,128)S(1)} %get-tuple-element.33), channel_id=1, source_target_pairs={{0,1},{1,0},{2,3},{3,2},{4,5},{5,4},{6,7},{7,6},{8,9},{9,8},{10,11... | collective-permute-start | bytes 835592 | tf_op jit(solution)/shard_map/ppermute | solution.py:373

commit v6 on v5

--- a/solution.py
+++ b/solution.py
@@ -68,7 +68,26 @@
     return at // ring, at % ring
 
 
-def attend(ring, away, q_hbm, k_hbm, v_hbm, q_ref, k_ref, v_ref, s_ref, sem):
+def select(sel_ref, k_ref, pick_ref):
+    half, width = pick_ref.shape
+    count = sel_ref.shape[1]
+    tokens = k_ref.shape[0]
+    base = lax.axis_index("ctx") * tokens
+    first = lax.axis_index("pb") * half
+    row = lax.broadcasted_iota(jnp.int32, (half, count), 0) + first
+    lane = lax.broadcasted_iota(jnp.int32, (half, count), 1)
+    sel = jnp.broadcast_to((sel_ref[...] - base).astype(F32), (half, count))
+    col = jnp.sum(jnp.where(row == lane, sel, 0.0), axis=1, keepdims=True).astype(jnp.int32)
+    step = 512
+    acc = jnp.zeros((half, width), F32)
+    for k in range(0, tokens, step):
+        at = lax.broadcasted_iota(jnp.int32, (half, step), 1) + k
+        hot = (at == col).astype(F32).astype(BF16)
+        acc += jnp.dot(hot, k_ref[k : k + step, :], preferred_element_type=F32)
+    pick_ref[...] = acc.astype(BF16)
+
+
+def attend(ring, away, q_hbm, k_hbm, v_hbm, q_ref, k_ref, v_ref, s_ref, sem, fetch=None, pick=None):
     rows, width = q_ref.shape
     tokens = k_ref.shape[0]
     step = 512
@@ -88,11 +107,15 @@
     for a in range(0, tokens, step):
         if a == tokens // 4:
             copies[2].wait()
+            if fetch is not None:
+                fetch.wait()
         s = lax.dot_general(k_ref[a : a + step, :], q, NT, preferred_element_type=F32)
         s_ref[a : a + step, :] = s
         top = jnp.max(s.reshape(step // 8, 8, rows), axis=0)
         mx = top if mx is None else jnp.maximum(mx, top)
     mc = jnp.max(mx, axis=0, keepdims=True) * c
+    if pick is not None:
+        pick()
     total, out = jnp.zeros((8, rows), F32), jnp.zeros((width, rows), F32)
     copies[3].wait()
     for a in range(0, tokens, step):
@@ -106,9 +129,13 @@
 def away_body(ring, sel_hbm, q_hbm, k_hbm, v_hbm, out_ref, pick_ref, sel_ref, q_ref, k_ref, v_ref, s_ref, sem, sel_sem):
     fetch = pltpu.make_async_copy(sel_hbm, sel_ref, sel_sem)
     fetch.start()
-    o, lse = attend(ring, True, q_hbm, k_hbm, v_hbm, q_ref, k_ref, v_ref, s_ref, sem)
-    rows, width = q_ref.shape
-    tokens = k_ref.shape[0]
+
+    def pick():
+        select(sel_ref, k_ref, pick_ref)
+        out_ref[ring, : pick_ref.shape[0], :] = pick_ref[...]
+
+    o, lse = attend(ring, True, q_hbm, k_hbm, v_hbm, q_ref, k_ref, v_ref, s_ref, sem, fetch, pick)
+    rows = q_ref.shape[0]
     share = rows // ring
     per = 128 // share
     o = o.astype(BF16)
@@ -117,24 +144,6 @@
         for j in range(g * per, (g + 1) * per):
             out_ref[j, :share, :] = o[j * share : (j + 1) * share, :]
             out_ref[j, share:, :] = three
-    fetch.wait()
-    half = pick_ref.shape[0]
-    count = sel_ref.shape[1]
-    base = lax.axis_index("ctx") * tokens
-    first = lax.axis_index("pb") * half
-    row = lax.broadcasted_iota(jnp.int32, (half, count), 0) + first
-    lane = lax.broadcasted_iota(jnp.int32, (half, count), 1)
-    sel = jnp.broadcast_to((sel_ref[...] - base).astype(F32), (half, count))
-    col = jnp.sum(jnp.where(row == lane, sel, 0.0), axis=1, keepdims=True).astype(jnp.int32)
-    step = 512
-    acc = jnp.zeros((half, width), F32)
-    for k in range(0, tokens, step):
-        at = lax.broadcasted_iota(jnp.int32, (half, step), 1) + k
-        hot = (at == col).astype(F32).astype(BF16)
-        acc += jnp.dot(hot, k_ref[k : k + step, :], preferred_element_type=F32)
-    mine = acc.astype(BF16)
-    pick_ref[...] = mine
-    out_ref[ring, :half, :] = mine
 
 
 def home_body(ring, q_hbm, k_hbm, v_hbm, out_ref, lse_ref, q_ref, k_ref, v_ref, s_ref, sem):
@@ -233,50 +242,40 @@
         send_ref[:, k : k + step] = g[half:]
 
 
-def rhs_body(total_rows, in_ref, own_ref, keep_ref, send_ref, y_ref):
+def rhs_body(total_rows, in_ref, own_ref, send_ref, y_ref, g_ref):
     ring, block, _ = in_ref.shape
     share = block - STAT
-    count = keep_ref.shape[0]
+    half = send_ref.shape[1] - 8
     rows = ring * share
+    x, _ = place(ring)
     for p in range(ring):
         y_ref[p * share : (p + 1) * share, :] = in_ref[slot(p, ring), :share, :]
-    g = jnp.dot(own_ref[...], y_ref[...], preferred_element_type=F32) * (1.0 / total_rows)
-    keep_ref[...] = g[:count]
-    send_ref[:count, :] = g[count:]
-    send_ref[count:, :] = jnp.zeros((8, 128), F32)
+    g_ref[...] = jnp.dot(own_ref[...], y_ref[...], preferred_element_type=F32) * (1.0 / total_rows)
     per = 128 // share
     lane = lax.broadcasted_iota(jnp.int32, (1, 128), 1)
+    lines = []
     for h in range(rows // 128):
         line = jnp.zeros((1, 128), F32)
         for j in range(per):
             v = in_ref[slot(h * per + j, ring), share:, :].astype(F32)
             v = (v[0:1] + v[1:2]) + v[2:3]
             line = jnp.where((lane >= j * share) & (lane < (j + 1) * share), v, line)
-        send_ref[count + h : count + h + 1, :] = line
-
-
-def sides_body(ring, keep_ref, sent_ref, got_ref, stat_ref, gsend_ref, mine_ref, out_ref, gap_ref, sum_ref):
-    count = keep_ref.shape[0]
-    half = count // 2
-    sel = gsend_ref.shape[1]
+        lines.append(line)
+    lines = jnp.concatenate(lines + [jnp.zeros((8 - len(lines), 128), F32)], axis=0)
+    for k in range(4):
+        other = x if k < 2 else 1 - x
+        send_ref[k, :half, :] = g_ref[pl.ds(pl.multiple_of(other * (2 * half) + (k % 2) * half, half), half), :]
+        send_ref[k, half:, :] = lines
+
+
+def last_body(got_ref, stat_ref, keep_ref, in_ref, gram_ref, rhs_ref, gap_ref):
+    half = rhs_ref.shape[0]
+    rhs_ref[...] = (got_ref[0, :half, :] + got_ref[1, :half, :]) + (got_ref[2, :half, :] + got_ref[3, :half, :])
+    gram_ref[...] = keep_ref[...] + in_ref[...]
     pb = lax.axis_index("pb")
-    x, _ = place(ring)
-    sum_ref[...] = keep_ref[...] + got_ref[:count, :]
-    mine_ref[...] = sum_ref[pl.ds(pl.multiple_of(pb * half, half), half), :]
-    out_ref[:, :sel] = gsend_ref[...]
-    out_ref[:, sel:] = sum_ref[pl.ds(pl.multiple_of((1 - pb) * half, half), half), :]
     lines = gap_ref.shape[0] // 2
-    here, there = sent_ref[count : count + lines, :], got_ref[count : count + lines, :]
-    low = jnp.where(x == 0, here, there)
-    high = jnp.where(x == 0, there, here)
-    gap_ref[:lines, :] = low - stat_ref[:lines, :]
-    gap_ref[lines:, :] = high - stat_ref[lines:, :]
-
-
-def last_body(g_ref, r_ref, in_ref, gram_ref, rhs_ref):
-    sel = g_ref.shape[1]
-    gram_ref[...] = g_ref[...] + in_ref[:, :sel]
-    rhs_ref[...] = r_ref[...] + in_ref[:, sel:]
+    gap_ref[:lines, :] = got_ref[pb, half : half + lines, :] - stat_ref[:lines, :]
+    gap_ref[lines:, :] = got_ref[2 + pb, half : half + lines, :] - stat_ref[lines:, :]
 
 
 def shards(queries, cache_keys, cache_values, sel_index):
@@ -349,28 +348,22 @@
         exps=rows * sel,
         moved=sel * width * 4,
     )
-    rkeep, rsend = call(
+    quads = [[2 * (side + z) + core for side in (0, ring) for core in (0, 1)] for z in range(ring)]
+    (send,) = call(
         "rhs",
         functools.partial(rhs_body, total_rows),
-        [((count, width), F32), ((count + 8, width), F32)],
+        [((4, half + 8, width), F32)],
         (heard, own),
-        scratch=[pltpu.VMEM((part, width), BF16)],
+        scratch=[pltpu.VMEM((part, width), BF16), pltpu.VMEM((2 * count, width), F32)],
         flops=4 * count * part * width,
         moved=part * width * 2,
     )
-    rmine, send, gap = call(
-        "sides",
-        functools.partial(sides_body, ring),
-        [((half, width), F32), ((half, sel + width), F32), ((rows // 128, 128), F32)],
-        (rkeep, rsend, lax.ppermute(rsend, "ctx", across), stat, gsend),
-        scratch=[pltpu.VMEM((count, width), F32)],
-        moved=half * sel * 8,
-    )
-    gram, rhs = call(
+    got = lax.all_to_all(send, ("ctx", "pb"), 0, 0, axis_index_groups=quads, tiled=True)
+    gram, rhs, gap = call(
         "last",
         last_body,
-        [((half, sel), F32), ((half, width), F32)],
-        (gkeep, rmine, lax.ppermute(send, "pb", swap)),
+        [((half, sel), F32), ((half, width), F32), ((rows // 128, 128), F32)],
+        (got, stat, gkeep, lax.ppermute(gsend, "pb", swap)),
         moved=half * sel * 12,
     )
     return (gram[None], rhs[None], gap.reshape(1, heads, rows_dev))

time: 85.9 us -> 83.4 us (0.971)
  starting transfers between devices: 28.1 us -> 26.1 us
    ppermute x2 -> x1, starting transfers between devices: 8.42 us -> 2.27 us  [shards(): lax.ppermute(gsend, 'pb', swap)]
    all_to_all x0 -> x1, starting transfers between devices: none -> 4.1 us  [shards(): lax.all_to_all(send, ('ctx', 'pb'), 0, 0, axis_index_groups=quads, tiled=...]
    all_to_all x0 -> x1, waiting for transfers between devices: none -> 3.3 us  [shards(): lax.all_to_all(send, ('ctx', 'pb'), 0, 0, axis_index_groups=quads, tiled=...]
    ppermute x2 -> x1, waiting for transfers between devices: 3.23 us -> 0.01 us  [shards(): lax.ppermute(gsend, 'pb', swap)]
    pallas_call x8 -> x7, Pallas kernels: 18.3 us -> 18.2 us  [call(): pl.pallas_call(ordered, name=name, out_shape=[jax.ShapeDtypeStruct(s, d)...]
  transfers between devices with their start and end apart: 5 -> 5, of which waited for: 4 -> 2; matrix products, arithmetic and copies ran while one was open for 0% -> 0% of each run, Pallas kernels for 12% -> 13%
where the time goes in v6:
time: 83.4 us; the launch traced here: 83 us
  blocking collectives  33.6 us (40%)
  starting transfers between devices  26.1 us (31%)
  Pallas kernels  18.2 us (22%)
  waiting for transfers between devices  4.45 us (5%)
    all_to_all x1, blocking collectives, exchange(): return lax.all_to_all(x, 'ctx', 0, 0, axis_index_groups=rings, tiled=True)  33.6 us
    pallas_call x7, Pallas kernels, call(): pl.pallas_call(ordered, name=name, out_shape=[jax.ShapeDtypeStruct(s, d)...  18.2 us
    all_to_all x1, starting transfers between devices, exchange(): return lax.all_to_all(x, 'ctx', 0, 0, axis_index_groups=rings, tiled=True)  12.3 us
    all_to_all x1, starting transfers between devices, shards(): lax.all_to_all(send, ('ctx', 'pb'), 0, 0, axis_index_groups=quads, tiled=...  4.1 us
    ppermute x1, starting transfers between devices, shards(): came = lax.ppermute(away, 'ctx', across)  3.95 us
    ppermute x1, starting transfers between devices, shards(): other = lax.ppermute(mine, 'pb', swap)  3.44 us
    all_to_all x1, waiting for transfers between devices, shards(): lax.all_to_all(send, ('ctx', 'pb'), 0, 0, axis_index_groups=quads, tiled=...  3.3 us
    ppermute x1, starting transfers between devices, shards(): lax.ppermute(gsend, 'pb', swap)  2.27 us
  transfers between devices with their start and end apart: 5, of which 2 were waited for; matrix products, arithmetic and copies ran while one was open for 0% of the time, Pallas kernels for 13%

profile of v6, /device:TPU:1, one launch (start us, length us, event | category | flops | bytes accessed | tf_op | source)
XLA Modules:
  0.0 83.0 jit_solution(14510768442784425938)
XLA Ops:
  0.6 5.3 %away.1 = (bf16[17,40,128]{2,1,0:T(8,128)(2,1)}, bf16[32,128]{1,0:T(8,128)(2,1)}) custom-call(s32[1,64]{1,0:T(1,128)} %refs_0_.1, bf16[1024,128]{1,0:T(8,128)(2,1)} %bitcast.6, bf16[4096,128]{1,0:T(8,128)(2,1)} %bitcast.9, bf16[4096,128]{1,0:T(8,128)(2,1)} %bitcast.11), custom_call_target="tpu_custom_call" | custom-call | flops 1073741824 | bytes 2097152 | tf_op jit(solution)/shard_map/away/pallas_call | solution.py:28
  6.0 4.0 %collective-permute-start = (bf16[17,40,128]{2,1,0:T(8,128)(2,1)}, bf16[17,40,128]{2,1,0:T(8,128)(2,1)S(1)}, u32[]{:S(2)}, u32[]{:S(2)}) collective-permute-start(bf16[17,40,128]{2,1,0:T(8,128)(2,1)} %get-tuple-element.18), channel_id=1, source_target_pairs={{0,256},{16,272},{32,288},{48,304},{64,320},{80,336},{96,352},{112... | collective-permute-start | bytes 522248 | tf_op jit(solution)/shard_map/ppermute | solution.py:319
  9.9 0.0 copy-start
  9.9 4.5 %home.1 = (f32[512,128]{1,0:T(8,128)S(1)}, f32[8,128]{1,0:T(8,128)S(1)}) custom-call(bf16[1024,128]{1,0:T(8,128)(2,1)} %bitcast.7, bf16[4096,128]{1,0:T(8,128)(2,1)} %bitcast.10, bf16[4096,128]{1,0:T(8,128)(2,1)} %bitcast.12), custom_call_target="tpu_custom_call" | custom-call | flops 1073741824 | bytes 2097152 | tf_op jit(solution)/shard_map/home/pallas_call | solution.py:28
  14.5 0.0 collective-permute-done.refs_2_
  14.5 0.0 copy-done
  14.5 0.2 pair.1
  14.6 33.6 %all_to_all.15.refs_0_ = bf16[16,104,128]{2,1,0:T(8,128)(2,1)S(1)} all-to-all(bf16[16,104,128]{2,1,0:T(8,128)(2,1)S(1)} %pair.1), channel_id=1, replica_groups={{192,208,224,240,0,16,32,48,64,80,96,112,128,144,160,176},{448,464,480,..., dimensions={0} | all-to-all | bytes 851968 | tf_op jit(solution)/shard_map/all_to_all | solution.py:300
  48.2 1.1 %settle.1 = (bf16[16,40,128]{2,1,0:T(8,128)(2,1)}, bf16[16,64,128]{2,1,0:T(8,128)(2,1)S(1)}) custom-call(bf16[16,104,128]{2,1,0:T(8,128)(2,1)S(1)} %all_to_all.15.refs_0_), custom_call_target="tpu_custom_call" | custom-call | bytes 524288 | tf_op jit(solution)/shard_map/settle/pallas_call | solution.py:28
  49.3 0.0 copy-start.1
  49.3 12.3 %all-to-all-start.1 = ((bf16[16,40,128]{2,1,0:T(8,128)(2,1)}), bf16[16,40,128]{2,1,0:T(8,128)(2,1)S(1)}, u32[]{:S(2)}, u32[]{:S(2)}) async-start(bf16[16,40,128]{2,1,0:T(8,128)(2,1)} %get-tuple-element.20.refs_3_), calls=%async_computation.1 | async-start | bytes 327680 | tf_op jit(solution)/shard_map/all_to_all | solution.py:300
  61.6 3.4 %collective-permute-start.1 = (bf16[16,64,128]{2,1,0:T(8,128)(2,1)S(1)}, bf16[16,64,128]{2,1,0:T(8,128)(2,1)S(1)}, u32[]{:S(2)}, u32[]{:S(2)}) collective-permute-start(bf16[16,64,128]{2,1,0:T(8,128)(2,1)S(1)} %get-tuple-element.21.refs_1_), channel_id=1, source_target_pairs={{0,1},{1,0},{2,3},{3,2},{4,5},{5,4},{6,7},{7,6},{8,9},{9,8},{10,11... | collective-permute-start | bytes 786440 | tf_op jit(solution)/shard_map/ppermute | solution.py:339
  65.1 1.1 %collective-permute-done.1.refs_2_ = bf16[16,64,128]{2,1,0:T(8,128)(2,1)S(1)} collective-permute-done((bf16[16,64,128]{2,1,0:T(8,128)(2,1)S(1)}, bf16[16,64,128]{2,1,0:T(8,128)(2,1)S(1)}, u32[]{:S(2)}, u32[]{:S(2)}) %collective-permute-start.1) | collective-permute-done | bytes 262176 | tf_op jit(solution)/shard_map/ppermute | solution.py:339
  66.2 0.0 copy-done.1
  66.2 5.5 %features.1 = (bf16[128,512]{1,0:T(8,128)(2,1)S(1)}, f32[8,128]{1,0:T(8,128)S(1)}, f32[32,2048]{1,0:T(8,128)S(1)}, f32[32,2048]{1,0:T(8,128)S(1)}) custom-call(bf16[1024,128]{1,0:T(8,128)(2,1)S(1)} %bitcast.8, bf16[16,64,128]{2,1,0:T(8,128)(2,1)S(1)} %get-tuple-element.21.refs_1_, bf16[16,64,128]{2,1,0:T(8,128)(2,1)S(1)} %collective-permute-done.1.refs_2_, ...), custom_call_target="tpu_custom_call" | custom-call | flops 805306368 | bytes 1048576 | tf_op jit(solution)/shard_map/features/pallas_call | solution.py:28
  71.7 2.3 %collective-permute-start.2 = (f32[32,2048]{1,0:T(8,128)S(1)}, f32[32,2048]{1,0:T(8,128)S(1)}, u32[]{:S(2)}, u32[]{:S(2)}) collective-permute-start(f32[32,2048]{1,0:T(8,128)S(1)} %get-tuple-element.25), channel_id=1, source_target_pairs={{0,1},{1,0},{2,3},{3,2},{4,5},{5,4},{6,7},{7,6},{8,9},{9,8},{10,11... | collective-permute-start | bytes 786440 | tf_op jit(solution)/shard_map/ppermute | solution.py:366
  74.0 0.0 all-to-all-done.1.refs_0_
  74.0 0.8 %rhs.1 = f32[4,40,128]{2,1,0:T(8,128)} custom-call(bf16[16,40,128]{2,1,0:T(8,128)(2,1)S(1)} %all-to-all-done.1.refs_0_, bf16[128,512]{1,0:T(8,128)(2,1)S(1)} %get-tuple-element.22.refs_1_), custom_call_target="tpu_custom_call" | custom-call | flops 16777216 | bytes 131072 | tf_op jit(solution)/shard_map/rhs/pallas_call | solution.py:28
  74.8 4.1 %all-to-all-start.2 = ((f32[4,40,128]{2,1,0:T(8,128)}), f32[4,40,128]{2,1,0:T(8,128)S(1)}, u32[]{:S(2)}, u32[]{:S(2)}) async-start(f32[4,40,128]{2,1,0:T(8,128)} %rhs.1), calls=%async_computation.2 | async-start | bytes 163840 | tf_op jit(solution)/shard_map/all_to_all | solution.py:361
  78.9 0.0 collective-permute-done.2.refs_3_
  78.9 3.3 %all-to-all-done.2.refs_0_ = f32[4,40,128]{2,1,0:T(8,128)S(1)} async-done(((f32[4,40,128]{2,1,0:T(8,128)}), f32[4,40,128]{2,1,0:T(8,128)S(1)}, u32[]{:S(2)}, u32[]{:S(2)}) %all-to-all-start.2) | async-done | bytes 81952 | tf_op jit(solution)/shard_map/all_to_all | solution.py:361
  82.2 0.7 last.1
Async XLA Ops:
  6.0 8.5 %collective-permute-start = (bf16[17,40,128]{2,1,0:T(8,128)(2,1)}, bf16[17,40,128]{2,1,0:T(8,128)(2,1)S(1)}, u32[]{:S(2)}, u32[]{:S(2)}) collective-permute-start(bf16[17,40,128]{2,1,0:T(8,128)(2,1)} %get-tuple-element.18), channel_id=1, source_target_pairs={{0,256},{16,272},{32,288},{48,304},{64,320},{80,336},{96,352},{112... | collective-permute-start | bytes 522248 | tf_op jit(solution)/shard_map/ppermute | solution.py:319
  9.9 4.6 %copy-start = (bf16[32,128]{1,0:T(8,128)(2,1)S(1)}, bf16[32,128]{1,0:T(8,128)(2,1)}, u32[]{:S(2)}) copy-start(bf16[32,128]{1,0:T(8,128)(2,1)} %get-tuple-element.19.refs_3_) | copy-start | bytes 24580
  49.3 16.9 %copy-start.1 = (bf16[1,8,128,128]{3,2,1,0:T(8,128)(2,1)S(1)}, bf16[1,8,128,128]{3,2,1,0:T(8,128)(2,1)}, u32[]{:S(2)}) copy-start(bf16[1,8,128,128]{3,2,1,0:T(8,128)(2,1)} %param.4) | copy-start | bytes 786436
  49.3 24.7 %all-to-all-start.1 = ((bf16[16,40,128]{2,1,0:T(8,128)(2,1)}), bf16[16,40,128]{2,1,0:T(8,128)(2,1)S(1)}, u32[]{:S(2)}, u32[]{:S(2)}) async-start(bf16[16,40,128]{2,1,0:T(8,128)(2,1)} %get-tuple-element.20.refs_3_), calls=%async_computation.1 | async-start | bytes 327680 | tf_op jit(solution)/shard_map/all_to_all | solution.py:300
  61.6 4.6 %collective-permute-start.1 = (bf16[16,64,128]{2,1,0:T(8,128)(2,1)S(1)}, bf16[16,64,128]{2,1,0:T(8,128)(2,1)S(1)}, u32[]{:S(2)}, u32[]{:S(2)}) collective-permute-start(bf16[16,64,128]{2,1,0:T(8,128)(2,1)S(1)} %get-tuple-element.21.refs_1_), channel_id=1, source_target_pairs={{0,1},{1,0},{2,3},{3,2},{4,5},{5,4},{6,7},{7,6},{8,9},{9,8},{10,11... | collective-permute-start | bytes 786440 | tf_op jit(solution)/shard_map/ppermute | solution.py:339
  71.7 7.2 %collective-permute-start.2 = (f32[32,2048]{1,0:T(8,128)S(1)}, f32[32,2048]{1,0:T(8,128)S(1)}, u32[]{:S(2)}, u32[]{:S(2)}) collective-permute-start(f32[32,2048]{1,0:T(8,128)S(1)} %get-tuple-element.25), channel_id=1, source_target_pairs={{0,1},{1,0},{2,3},{3,2},{4,5},{5,4},{6,7},{7,6},{8,9},{9,8},{10,11... | collective-permute-start | bytes 786440 | tf_op jit(solution)/shard_map/ppermute | solution.py:366
  74.8 7.4 %all-to-all-start.2 = ((f32[4,40,128]{2,1,0:T(8,128)}), f32[4,40,128]{2,1,0:T(8,128)S(1)}, u32[]{:S(2)}, u32[]{:S(2)}) async-start(f32[4,40,128]{2,1,0:T(8,128)} %rhs.1), calls=%async_computation.2 | async-start | bytes 163840 | tf_op jit(solution)/shard_map/all_to_all | solution.py:361

commit v7 on v6

--- a/solution.py
+++ b/solution.py
@@ -10,7 +10,7 @@
 
 eps = 1e-06
 LOG2E = math.log2(math.e)
-F32, BF16 = jnp.float32, jnp.bfloat16
+F32, F16, BF16 = jnp.float32, jnp.float16, jnp.bfloat16
 VMEM = pl.BlockSpec(memory_space=pltpu.VMEM)
 ANY = pl.BlockSpec(memory_space=pl.ANY)
 NT = (((1,), (1,)), ((), ()))
@@ -84,7 +84,7 @@
         at = lax.broadcasted_iota(jnp.int32, (half, step), 1) + k
         hot = (at == col).astype(F32).astype(BF16)
         acc += jnp.dot(hot, k_ref[k : k + step, :], preferred_element_type=F32)
-    pick_ref[...] = acc.astype(BF16)
+    pick_ref[...] = acc
 
 
 def attend(ring, away, q_hbm, k_hbm, v_hbm, q_ref, k_ref, v_ref, s_ref, sem, fetch=None, pick=None):
@@ -138,12 +138,11 @@
     rows = q_ref.shape[0]
     share = rows // ring
     per = 128 // share
-    o = o.astype(BF16)
     for g in range(rows // 128):
-        three = packed3(lse[:, g * 128 : (g + 1) * 128])
+        line = jnp.broadcast_to(lse[:, g * 128 : (g + 1) * 128], (STAT, 128))
         for j in range(g * per, (g + 1) * per):
             out_ref[j, :share, :] = o[j * share : (j + 1) * share, :]
-            out_ref[j, share:, :] = three
+            out_ref[j, share:, :] = line
 
 
 def home_body(ring, q_hbm, k_hbm, v_hbm, out_ref, lse_ref, q_ref, k_ref, v_ref, s_ref, sem):
@@ -162,8 +161,7 @@
     per = 128 // share
     mine, theirs = pick_ref[...], in_ref[ring, :half, :]
     for g in range(rows // 128):
-        three = in_ref[g * per, share:, :].astype(F32)
-        other = (three[0:1] + three[1:2]) + three[2:3]
+        other = in_ref[g * per, share : share + 1, :]
         here = lse_ref[g : g + 1, :]
         top = jnp.maximum(other, here)
         wo, wh = jnp.exp(other - top), jnp.exp(here - top)
@@ -172,19 +170,19 @@
         share_of = column(wh / total)
         for j in range(g * per, (g + 1) * per):
             w = share_of[(j % per) * share : (j % per + 1) * share, :]
-            a = in_ref[j, :share, :].astype(F32)
+            a = in_ref[j, :share, :]
             h = o_ref[j * share : (j + 1) * share, :]
             to = slot(j, ring)
-            out_ref[to, :share, :] = (a + w * (h - a)).astype(BF16)
+            out_ref[to, :share, :] = a + w * (h - a)
             out_ref[to, share : share + half, :] = mine
             out_ref[to, share + half : length - STAT, :] = theirs
-            out_ref[to, length - STAT :, :] = lines
+            out_ref[to, length - STAT :, :] = lines.astype(F32)
 
 
 def settle_body(share, in_ref, out_ref, keys_ref, w_ref):
     ring, length, _ = in_ref.shape
     _, z = place(ring)
-    lines = in_ref[:, length - STAT :, :].astype(F32)
+    lines = in_ref[:, length - STAT :, :]
     lse = (lines[:, 0, :] + lines[:, 1, :]) + lines[:, 2, :]
     top = jnp.max(lse, axis=0, keepdims=True)
     w = jnp.exp(lse - top)
@@ -194,13 +192,13 @@
     mine = w_ref[pl.ds(pl.multiple_of((z % (128 // share)) * share, share), share), :]
     acc = jnp.zeros((share, 128), F32)
     for b in range(ring):
-        acc = acc + mine[:, b : b + 1] * in_ref[b, :share, :].astype(F32)
+        acc = acc + mine[:, b : b + 1] * in_ref[b, :share, :]
     y = (acc * lax.rsqrt(jnp.mean(acc * acc, axis=1, keepdims=True) + eps)).astype(BF16)
     three = packed3(top + jnp.log(total))
     for p in range(ring):
         out_ref[p, :share, :] = y
         out_ref[p, share:, :] = three
-        keys_ref[p] = in_ref[p, share : length - STAT, :]
+        keys_ref[p] = in_ref[p, share : length - STAT, :].astype(BF16)
 
 
 def features_body(rt, q_ref, mine_ref, other_ref, own_ref, stat_ref, keep_ref, send_ref, c_ref, f_ref, g_ref):
@@ -310,7 +308,7 @@
     away, picked = call(
         "away",
         functools.partial(away_body, ring),
-        [((ring + 1, block, width), BF16), ((half, width), BF16)],
+        [((ring + 1, block, width), F32), ((half, width), F32)],
         (sel_index, q, keys, values),
         specs=[ANY] * 4,
         scratch=[pltpu.VMEM((1, count), jnp.int32), *held, pltpu.SemaphoreType.DMA],
@@ -326,12 +324,12 @@
         scratch=held,
         **(work | dict(limit=53.5)),
     )
-    (parts,) = call("pair", pair_body, [((ring, block + count, width), BF16)], (home, lse, came, picked), moved=part * width * 12)
+    (parts,) = call("pair", pair_body, [((ring, block + count, width), F32)], (home, lse, came, picked), moved=part * width * 12)
     told, mine = call(
         "settle",
         functools.partial(settle_body, share),
         [((ring, block, width), BF16), ((ring, count, width), BF16)],
-        (exchange(parts),),
+        (exchange(parts.astype(F16)).astype(F32),),
         scratch=[pltpu.VMEM((128, 128), F32)],
         moved=part * width * 8,
     )

time: 83.4 us -> 86.9 us (1.042)
  blocking collectives: 33.6 us -> 36.5 us
    all_to_all x1, blocking collectives: 33.6 us -> 36.5 us  [exchange(): return lax.all_to_all(x, 'ctx', 0, 0, axis_index_groups=rings, tiled=True)]
  transfers between devices with their start and end apart: 5 -> 5, of which waited for: 2 -> 3; matrix products, arithmetic and copies ran while one was open for 0% -> 0% of each run, Pallas kernels for 13% -> 13%
where the time goes in v7:
time: 86.9 us; the launch traced here: 86.5 us
  blocking collectives  36.5 us (42%)
  starting transfers between devices  26.2 us (30%)
  Pallas kernels  18.2 us (21%)
  waiting for transfers between devices  4.79 us (6%)
    all_to_all x1, blocking collectives, exchange(): return lax.all_to_all(x, 'ctx', 0, 0, axis_index_groups=rings, tiled=True)  36.5 us
    pallas_call x7, Pallas kernels, call(): pl.pallas_call(ordered, name=name, out_shape=[jax.ShapeDtypeStruct(s, d)...  18.2 us
    all_to_all x1, starting transfers between devices, exchange(): return lax.all_to_all(x, 'ctx', 0, 0, axis_index_groups=rings, tiled=True)  12.4 us
    all_to_all x1, starting transfers between devices, shards(): lax.all_to_all(send, ('ctx', 'pb'), 0, 0, axis_index_groups=quads, tiled=...  3.97 us
    ppermute x1, starting transfers between devices, shards(): came = lax.ppermute(away, 'ctx', across)  3.95 us
    ppermute x1, starting transfers between devices, shards(): other = lax.ppermute(mine, 'pb', swap)  3.6 us
    all_to_all x1, waiting for transfers between devices, shards(): lax.all_to_all(send, ('ctx', 'pb'), 0, 0, axis_index_groups=quads, tiled=...  3.3 us
    ppermute x1, starting transfers between devices, shards(): lax.ppermute(gsend, 'pb', swap)  2.29 us
  transfers between devices with their start and end apart: 5, of which 3 were waited for; matrix products, arithmetic and copies ran while one was open for 0% of the time, Pallas kernels for 13%

profile of v7, /device:TPU:1, one launch (start us, length us, event | category | flops | bytes accessed | tf_op | source)
XLA Modules:
  0.0 86.5 jit_solution(435407070761373723)
XLA Ops:
  0.6 5.4 %away.1 = (f32[17,40,128]{2,1,0:T(8,128)}, f32[32,128]{1,0:T(8,128)}) custom-call(s32[1,64]{1,0:T(1,128)} %refs_0_.1, bf16[1024,128]{1,0:T(8,128)(2,1)} %bitcast.6, bf16[4096,128]{1,0:T(8,128)(2,1)} %bitcast.9, bf16[4096,128]{1,0:T(8,128)(2,1)} %bitcast.11), custom_call_target="tpu_custom_call" | custom-call | flops 1073741824 | bytes 2097152 | tf_op jit(solution)/shard_map/away/pallas_call | solution.py:28
  6.0 4.0 %collective-permute-start = (f32[17,40,128]{2,1,0:T(8,128)}, f32[17,40,128]{2,1,0:T(8,128)S(1)}, u32[]{:S(2)}, u32[]{:S(2)}) collective-permute-start(f32[17,40,128]{2,1,0:T(8,128)} %get-tuple-element.18), channel_id=1, source_target_pairs={{0,256},{16,272},{32,288},{48,304},{64,320},{80,336},{96,352},{112... | collective-permute-start | bytes 1044488 | tf_op jit(solution)/shard_map/ppermute | solution.py:317
  10.0 0.0 copy-start
  10.0 4.5 %home.1 = (f32[512,128]{1,0:T(8,128)S(1)}, f32[8,128]{1,0:T(8,128)S(1)}) custom-call(bf16[1024,128]{1,0:T(8,128)(2,1)} %bitcast.7, bf16[4096,128]{1,0:T(8,128)(2,1)} %bitcast.10, bf16[4096,128]{1,0:T(8,128)(2,1)} %bitcast.12), custom_call_target="tpu_custom_call" | custom-call | flops 1073741824 | bytes 2097152 | tf_op jit(solution)/shard_map/home/pallas_call | solution.py:28
  14.5 0.3 collective-permute-done.refs_2_
  14.9 0.0 copy-done
  14.9 0.2 pair.1
  15.0 0.1 convert_element_type.6
  15.1 36.5 %all_to_all.15 = f16[16,104,128]{2,1,0:T(8,128)(2,1)S(1)} all-to-all(f16[16,104,128]{2,1,0:T(8,128)(2,1)S(1)} %convert_element_type.6), channel_id=1, replica_groups={{192,208,224,240,0,16,32,48,64,80,96,112,128,144,160,176},{448,464,480,..., dimensions={0} | all-to-all | bytes 851968 | tf_op jit(solution)/shard_map/all_to_all | solution.py:298
  51.6 0.1 convert_element_type.7.refs_0_
  51.6 1.1 %settle.1 = (bf16[16,40,128]{2,1,0:T(8,128)(2,1)}, bf16[16,64,128]{2,1,0:T(8,128)(2,1)S(1)}) custom-call(f32[16,104,128]{2,1,0:T(8,128)S(1)} %convert_element_type.7.refs_0_), custom_call_target="tpu_custom_call" | custom-call | bytes 524288 | tf_op jit(solution)/shard_map/settle/pallas_call | solution.py:28
  52.7 0.0 copy-start.1
  52.7 12.4 %all-to-all-start.1 = ((bf16[16,40,128]{2,1,0:T(8,128)(2,1)}), bf16[16,40,128]{2,1,0:T(8,128)(2,1)S(1)}, u32[]{:S(2)}, u32[]{:S(2)}) async-start(bf16[16,40,128]{2,1,0:T(8,128)(2,1)} %get-tuple-element.20.refs_3_), calls=%async_computation.1 | async-start | bytes 327680 | tf_op jit(solution)/shard_map/all_to_all | solution.py:298
  65.1 3.6 %collective-permute-start.1 = (bf16[16,64,128]{2,1,0:T(8,128)(2,1)S(1)}, bf16[16,64,128]{2,1,0:T(8,128)(2,1)S(1)}, u32[]{:S(2)}, u32[]{:S(2)}) collective-permute-start(bf16[16,64,128]{2,1,0:T(8,128)(2,1)S(1)} %get-tuple-element.21.refs_1_), channel_id=1, source_target_pairs={{0,1},{1,0},{2,3},{3,2},{4,5},{5,4},{6,7},{7,6},{8,9},{9,8},{10,11... | collective-permute-start | bytes 786440 | tf_op jit(solution)/shard_map/ppermute | solution.py:337
  68.7 1.1 %collective-permute-done.1.refs_2_ = bf16[16,64,128]{2,1,0:T(8,128)(2,1)S(1)} collective-permute-done((bf16[16,64,128]{2,1,0:T(8,128)(2,1)S(1)}, bf16[16,64,128]{2,1,0:T(8,128)(2,1)S(1)}, u32[]{:S(2)}, u32[]{:S(2)}) %collective-permute-start.1) | collective-permute-done | bytes 262176 | tf_op jit(solution)/shard_map/ppermute | solution.py:337
  69.8 0.0 copy-done.1
  69.8 5.5 %features.1 = (bf16[128,512]{1,0:T(8,128)(2,1)S(1)}, f32[8,128]{1,0:T(8,128)S(1)}, f32[32,2048]{1,0:T(8,128)S(1)}, f32[32,2048]{1,0:T(8,128)S(1)}) custom-call(bf16[1024,128]{1,0:T(8,128)(2,1)S(1)} %bitcast.8, bf16[16,64,128]{2,1,0:T(8,128)(2,1)S(1)} %get-tuple-element.21.refs_1_, bf16[16,64,128]{2,1,0:T(8,128)(2,1)S(1)} %collective-permute-done.1.refs_2_, ...), custom_call_target="tpu_custom_call" | custom-call | flops 805306368 | bytes 1048576 | tf_op jit(solution)/shard_map/features/pallas_call | solution.py:28
  75.3 2.3 %collective-permute-start.2 = (f32[32,2048]{1,0:T(8,128)S(1)}, f32[32,2048]{1,0:T(8,128)S(1)}, u32[]{:S(2)}, u32[]{:S(2)}) collective-permute-start(f32[32,2048]{1,0:T(8,128)S(1)} %get-tuple-element.25), channel_id=1, source_target_pairs={{0,1},{1,0},{2,3},{3,2},{4,5},{5,4},{6,7},{7,6},{8,9},{9,8},{10,11... | collective-permute-start | bytes 786440 | tf_op jit(solution)/shard_map/ppermute | solution.py:364
  77.6 0.0 all-to-all-done.1.refs_0_
  77.6 0.8 rhs.1
  78.5 4.0 %all-to-all-start.2 = ((f32[4,40,128]{2,1,0:T(8,128)}), f32[4,40,128]{2,1,0:T(8,128)S(1)}, u32[]{:S(2)}, u32[]{:S(2)}) async-start(f32[4,40,128]{2,1,0:T(8,128)} %rhs.1), calls=%async_computation.2 | async-start | bytes 163840 | tf_op jit(solution)/shard_map/all_to_all | solution.py:359
  82.4 0.0 collective-permute-done.2.refs_3_
  82.4 3.3 %all-to-all-done.2.refs_0_ = f32[4,40,128]{2,1,0:T(8,128)S(1)} async-done(((f32[4,40,128]{2,1,0:T(8,128)}), f32[4,40,128]{2,1,0:T(8,128)S(1)}, u32[]{:S(2)}, u32[]{:S(2)}) %all-to-all-start.2) | async-done | bytes 81952 | tf_op jit(solution)/shard_map/all_to_all | solution.py:359
  85.8 0.7 last.1
Async XLA Ops:
  6.0 8.8 %collective-permute-start = (f32[17,40,128]{2,1,0:T(8,128)}, f32[17,40,128]{2,1,0:T(8,128)S(1)}, u32[]{:S(2)}, u32[]{:S(2)}) collective-permute-start(f32[17,40,128]{2,1,0:T(8,128)} %get-tuple-element.18), channel_id=1, source_target_pairs={{0,256},{16,272},{32,288},{48,304},{64,320},{80,336},{96,352},{112... | collective-permute-start | bytes 1044488 | tf_op jit(solution)/shard_map/ppermute | solution.py:317
  10.0 4.9 %copy-start = (f32[32,128]{1,0:T(8,128)S(1)}, f32[32,128]{1,0:T(8,128)}, u32[]{:S(2)}) copy-start(f32[32,128]{1,0:T(8,128)} %get-tuple-element.19.refs_3_) | copy-start | bytes 49156
  52.7 17.1 %copy-start.1 = (bf16[1,8,128,128]{3,2,1,0:T(8,128)(2,1)S(1)}, bf16[1,8,128,128]{3,2,1,0:T(8,128)(2,1)}, u32[]{:S(2)}) copy-start(bf16[1,8,128,128]{3,2,1,0:T(8,128)(2,1)} %param.4) | copy-start | bytes 786436
  52.7 24.9 %all-to-all-start.1 = ((bf16[16,40,128]{2,1,0:T(8,128)(2,1)}), bf16[16,40,128]{2,1,0:T(8,128)(2,1)S(1)}, u32[]{:S(2)}, u32[]{:S(2)}) async-start(bf16[16,40,128]{2,1,0:T(8,128)(2,1)} %get-tuple-element.20.refs_3_), calls=%async_computation.1 | async-start | bytes 327680 | tf_op jit(solution)/shard_map/all_to_all | solution.py:298
  65.1 4.7 %collective-permute-start.1 = (bf16[16,64,128]{2,1,0:T(8,128)(2,1)S(1)}, bf16[16,64,128]{2,1,0:T(8,128)(2,1)S(1)}, u32[]{:S(2)}, u32[]{:S(2)}) collective-permute-start(bf16[16,64,128]{2,1,0:T(8,128)(2,1)S(1)} %get-tuple-element.21.refs_1_), channel_id=1, source_target_pairs={{0,1},{1,0},{2,3},{3,2},{4,5},{5,4},{6,7},{7,6},{8,9},{9,8},{10,11... | collective-permute-start | bytes 786440 | tf_op jit(solution)/shard_map/ppermute | solution.py:337
  75.3 7.1 %collective-permute-start.2 = (f32[32,2048]{1,0:T(8,128)S(1)}, f32[32,2048]{1,0:T(8,128)S(1)}, u32[]{:S(2)}, u32[]{:S(2)}) collective-permute-start(f32[32,2048]{1,0:T(8,128)S(1)} %get-tuple-element.25), channel_id=1, source_target_pairs={{0,1},{1,0},{2,3},{3,2},{4,5},{5,4},{6,7},{7,6},{8,9},{9,8},{10,11... | collective-permute-start | bytes 786440 | tf_op jit(solution)/shard_map/ppermute | solution.py:364
  78.5 7.3 %all-to-all-start.2 = ((f32[4,40,128]{2,1,0:T(8,128)}), f32[4,40,128]{2,1,0:T(8,128)S(1)}, u32[]{:S(2)}, u32[]{:S(2)}) async-start(f32[4,40,128]{2,1,0:T(8,128)} %rhs.1), calls=%async_computation.2 | async-start | bytes 163840 | tf_op jit(solution)/shard_map/all_to_all | solution.py:359

commit v8 on v7

--- a/solution.py
+++ b/solution.py
@@ -139,10 +139,10 @@
     share = rows // ring
     per = 128 // share
     for g in range(rows // 128):
-        line = jnp.broadcast_to(lse[:, g * 128 : (g + 1) * 128], (STAT, 128))
+        three = packed3(lse[:, g * 128 : (g + 1) * 128]).astype(F32)
         for j in range(g * per, (g + 1) * per):
             out_ref[j, :share, :] = o[j * share : (j + 1) * share, :]
-            out_ref[j, share:, :] = line
+            out_ref[j, share:, :] = three
 
 
 def home_body(ring, q_hbm, k_hbm, v_hbm, out_ref, lse_ref, q_ref, k_ref, v_ref, s_ref, sem):
@@ -161,7 +161,8 @@
     per = 128 // share
     mine, theirs = pick_ref[...], in_ref[ring, :half, :]
     for g in range(rows // 128):
-        other = in_ref[g * per, share : share + 1, :]
+        three = in_ref[g * per, share:, :]
+        other = (three[0:1] + three[1:2]) + three[2:3]
         here = lse_ref[g : g + 1, :]
         top = jnp.maximum(other, here)
         wo, wh = jnp.exp(other - top), jnp.exp(here - top)
@@ -314,7 +315,7 @@
         scratch=[pltpu.VMEM((1, count), jnp.int32), *held, pltpu.SemaphoreType.DMA],
         **work,
     )
-    came = lax.ppermute(away, "ctx", across)
+    came = lax.ppermute(away.astype(F16), "ctx", across).astype(F32)
     home, lse = call(
         "home",
         functools.partial(home_body, ring),

time: 86.9 us -> 85.5 us (0.984)
  blocking collectives: 36.5 us -> 33.6 us
  other arithmetic: 0.12 us -> 1.15 us
    all_to_all x1, blocking collectives: 36.5 us -> 33.6 us  [exchange(): return lax.all_to_all(x, 'ctx', 0, 0, axis_index_groups=rings, tiled=True)]
    convert_element_type x0 -> x2, other arithmetic: none -> 1.03 us  [shards(): came = lax.ppermute(away.astype(F16), 'ctx', across).astype(F32)]
  transfers between devices with their start and end apart: 5 -> 5, of which waited for: 3 -> 2; matrix products, arithmetic and copies ran while one was open for 0% -> 0% of each run, Pallas kernels for 13% -> 13%
where the time goes in v8:
time: 85.5 us; the launch traced here: 84.9 us
  blocking collectives  33.6 us (39%)
  starting transfers between devices  26.1 us (31%)
  Pallas kernels  18.2 us (21%)
  waiting for transfers between devices  4.45 us (5%)
  other arithmetic  1.15 us (1%)
    all_to_all x1, blocking collectives, exchange(): return lax.all_to_all(x, 'ctx', 0, 0, axis_index_groups=rings, tiled=True)  33.6 us
    pallas_call x7, Pallas kernels, call(): pl.pallas_call(ordered, name=name, out_shape=[jax.ShapeDtypeStruct(s, d)...  18.2 us
    all_to_all x1, starting transfers between devices, exchange(): return lax.all_to_all(x, 'ctx', 0, 0, axis_index_groups=rings, tiled=True)  12.4 us
    all_to_all x1, starting transfers between devices, shards(): lax.all_to_all(send, ('ctx', 'pb'), 0, 0, axis_index_groups=quads, tiled=...  4.13 us
    ppermute x1, starting transfers between devices, shards(): came = lax.ppermute(away.astype(F16), 'ctx', across).astype(F32)  3.95 us
    ppermute x1, starting transfers between devices, shards(): other = lax.ppermute(mine, 'pb', swap)  3.4 us
    all_to_all x1, waiting for transfers between devices, shards(): lax.all_to_all(send, ('ctx', 'pb'), 0, 0, axis_index_groups=quads, tiled=...  3.3 us
    ppermute x1, starting transfers between devices, shards(): lax.ppermute(gsend, 'pb', swap)  2.29 us
  transfers between devices with their start and end apart: 5, of which 2 were waited for; matrix products, arithmetic and copies ran while one was open for 0% of the time, Pallas kernels for 13%

profile of v8, /device:TPU:1, one launch (start us, length us, event | category | flops | bytes accessed | tf_op | source)
XLA Modules:
  0.0 84.9 jit_solution(7466750578758040598)
XLA Ops:
  0.6 5.4 %away.1 = (f32[17,40,128]{2,1,0:T(8,128)}, f32[32,128]{1,0:T(8,128)}) custom-call(s32[1,64]{1,0:T(1,128)} %refs_0_.1, bf16[1024,128]{1,0:T(8,128)(2,1)} %bitcast.6, bf16[4096,128]{1,0:T(8,128)(2,1)} %bitcast.9, bf16[4096,128]{1,0:T(8,128)(2,1)} %bitcast.11), custom_call_target="tpu_custom_call" | custom-call | flops 1073741824 | bytes 2097152 | tf_op jit(solution)/shard_map/away/pallas_call | solution.py:28
  6.0 1.0 %convert_element_type.12 = f16[17,40,128]{2,1,0:T(8,128)(2,1)S(1)} convert(f32[17,40,128]{2,1,0:T(8,128)} %get-tuple-element.18) | non-fusion elementwise | flops 87040 | bytes 522240 | tf_op jit(solution)/shard_map/convert_element_type | solution.py:318
  7.0 4.0 %collective-permute-start = (f16[17,40,128]{2,1,0:T(8,128)(2,1)S(1)}, f16[17,40,128]{2,1,0:T(8,128)(2,1)S(1)}, u32[]{:S(2)}, u32[]{:S(2)}) collective-permute-start(f16[17,40,128]{2,1,0:T(8,128)(2,1)S(1)} %convert_element_type.12), channel_id=1, source_target_pairs={{0,256},{16,272},{32,288},{48,304},{64,320},{80,336},{96,352},{112... | collective-permute-start | bytes 522248 | tf_op jit(solution)/shard_map/ppermute | solution.py:318
  11.0 4.5 %home.1 = (f32[512,128]{1,0:T(8,128)S(1)}, f32[8,128]{1,0:T(8,128)S(1)}) custom-call(bf16[1024,128]{1,0:T(8,128)(2,1)} %bitcast.7, bf16[4096,128]{1,0:T(8,128)(2,1)} %bitcast.10, bf16[4096,128]{1,0:T(8,128)(2,1)} %bitcast.12), custom_call_target="tpu_custom_call" | custom-call | flops 1073741824 | bytes 2097152 | tf_op jit(solution)/shard_map/home/pallas_call | solution.py:28
  15.5 0.0 collective-permute-done
  15.5 0.0 copy-start
  15.6 0.7 copy-done
  16.2 0.2 pair.1
  16.4 0.1 convert_element_type.14
  16.5 33.6 %all_to_all.15 = f16[16,104,128]{2,1,0:T(8,128)(2,1)S(1)} all-to-all(f16[16,104,128]{2,1,0:T(8,128)(2,1)S(1)} %convert_element_type.14), channel_id=1, replica_groups={{192,208,224,240,0,16,32,48,64,80,96,112,128,144,160,176},{448,464,480,..., dimensions={0} | all-to-all | bytes 851968 | tf_op jit(solution)/shard_map/all_to_all | solution.py:299
  50.1 0.1 convert_element_type.15.refs_0_
  50.1 1.1 %settle.1 = (bf16[16,40,128]{2,1,0:T(8,128)(2,1)}, bf16[16,64,128]{2,1,0:T(8,128)(2,1)S(1)}) custom-call(f32[16,104,128]{2,1,0:T(8,128)S(1)} %convert_element_type.15.refs_0_), custom_call_target="tpu_custom_call" | custom-call | bytes 524288 | tf_op jit(solution)/shard_map/settle/pallas_call | solution.py:28
  51.2 12.4 %all-to-all-start.1 = ((bf16[16,40,128]{2,1,0:T(8,128)(2,1)}), bf16[16,40,128]{2,1,0:T(8,128)(2,1)S(1)}, u32[]{:S(2)}, u32[]{:S(2)}) async-start(bf16[16,40,128]{2,1,0:T(8,128)(2,1)} %get-tuple-element.20.refs_3_), calls=%async_computation.1 | async-start | bytes 327680 | tf_op jit(solution)/shard_map/all_to_all | solution.py:299
  63.6 3.4 %collective-permute-start.1 = (bf16[16,64,128]{2,1,0:T(8,128)(2,1)S(1)}, bf16[16,64,128]{2,1,0:T(8,128)(2,1)S(1)}, u32[]{:S(2)}, u32[]{:S(2)}) collective-permute-start(bf16[16,64,128]{2,1,0:T(8,128)(2,1)S(1)} %get-tuple-element.21.refs_1_), channel_id=1, source_target_pairs={{0,1},{1,0},{2,3},{3,2},{4,5},{5,4},{6,7},{7,6},{8,9},{9,8},{10,11... | collective-permute-start | bytes 786440 | tf_op jit(solution)/shard_map/ppermute | solution.py:338
  67.0 1.1 %collective-permute-done.1.refs_2_ = bf16[16,64,128]{2,1,0:T(8,128)(2,1)S(1)} collective-permute-done((bf16[16,64,128]{2,1,0:T(8,128)(2,1)S(1)}, bf16[16,64,128]{2,1,0:T(8,128)(2,1)S(1)}, u32[]{:S(2)}, u32[]{:S(2)}) %collective-permute-start.1) | collective-permute-done | bytes 262176 | tf_op jit(solution)/shard_map/ppermute | solution.py:338
  68.1 0.0 copy-done.1
  68.1 5.5 %features.1 = (bf16[128,512]{1,0:T(8,128)(2,1)S(1)}, f32[8,128]{1,0:T(8,128)S(1)}, f32[32,2048]{1,0:T(8,128)S(1)}, f32[32,2048]{1,0:T(8,128)S(1)}) custom-call(bf16[1024,128]{1,0:T(8,128)(2,1)S(1)} %bitcast.8, bf16[16,64,128]{2,1,0:T(8,128)(2,1)S(1)} %get-tuple-element.21.refs_1_, bf16[16,64,128]{2,1,0:T(8,128)(2,1)S(1)} %collective-permute-done.1.refs_2_, ...), custom_call_target="tpu_custom_call" | custom-call | flops 805306368 | bytes 1048576 | tf_op jit(solution)/shard_map/features/pallas_call | solution.py:28
  73.6 2.3 %collective-permute-start.2 = (f32[32,2048]{1,0:T(8,128)S(1)}, f32[32,2048]{1,0:T(8,128)S(1)}, u32[]{:S(2)}, u32[]{:S(2)}) collective-permute-start(f32[32,2048]{1,0:T(8,128)S(1)} %get-tuple-element.25), channel_id=1, source_target_pairs={{0,1},{1,0},{2,3},{3,2},{4,5},{5,4},{6,7},{7,6},{8,9},{9,8},{10,11... | collective-permute-start | bytes 786440 | tf_op jit(solution)/shard_map/ppermute | solution.py:365
  75.9 0.0 all-to-all-done.1.refs_0_
  75.9 0.8 rhs.1
  76.8 4.1 %all-to-all-start.2 = ((f32[4,40,128]{2,1,0:T(8,128)}), f32[4,40,128]{2,1,0:T(8,128)S(1)}, u32[]{:S(2)}, u32[]{:S(2)}) async-start(f32[4,40,128]{2,1,0:T(8,128)} %rhs.1), calls=%async_computation.2 | async-start | bytes 163840 | tf_op jit(solution)/shard_map/all_to_all | solution.py:360
  80.9 0.0 collective-permute-done.2.refs_3_
  80.9 3.3 %all-to-all-done.2.refs_0_ = f32[4,40,128]{2,1,0:T(8,128)S(1)} async-done(((f32[4,40,128]{2,1,0:T(8,128)}), f32[4,40,128]{2,1,0:T(8,128)S(1)}, u32[]{:S(2)}, u32[]{:S(2)}) %all-to-all-start.2) | async-done | bytes 81952 | tf_op jit(solution)/shard_map/all_to_all | solution.py:360
  84.2 0.7 last.1
  (2 shorter events, 0.0 us)
Async XLA Ops:
  7.0 8.5 %collective-permute-start = (f16[17,40,128]{2,1,0:T(8,128)(2,1)S(1)}, f16[17,40,128]{2,1,0:T(8,128)(2,1)S(1)}, u32[]{:S(2)}, u32[]{:S(2)}) collective-permute-start(f16[17,40,128]{2,1,0:T(8,128)(2,1)S(1)} %convert_element_type.12), channel_id=1, source_target_pairs={{0,256},{16,272},{32,288},{48,304},{64,320},{80,336},{96,352},{112... | collective-permute-start | bytes 522248 | tf_op jit(solution)/shard_map/ppermute | solution.py:318
  15.5 0.7 copy-start
  51.2 16.9 %copy-start.1 = (bf16[1,8,128,128]{3,2,1,0:T(8,128)(2,1)S(1)}, bf16[1,8,128,128]{3,2,1,0:T(8,128)(2,1)}, u32[]{:S(2)}) copy-start(bf16[1,8,128,128]{3,2,1,0:T(8,128)(2,1)} %param.4) | copy-start | bytes 786436
  51.2 24.7 %all-to-all-start.1 = ((bf16[16,40,128]{2,1,0:T(8,128)(2,1)}), bf16[16,40,128]{2,1,0:T(8,128)(2,1)S(1)}, u32[]{:S(2)}, u32[]{:S(2)}) async-start(bf16[16,40,128]{2,1,0:T(8,128)(2,1)} %get-tuple-element.20.refs_3_), calls=%async_computation.1 | async-start | bytes 327680 | tf_op jit(solution)/shard_map/all_to_all | solution.py:299
  63.6 4.5 %collective-permute-start.1 = (bf16[16,64,128]{2,1,0:T(8,128)(2,1)S(1)}, bf16[16,64,128]{2,1,0:T(8,128)(2,1)S(1)}, u32[]{:S(2)}, u32[]{:S(2)}) collective-permute-start(bf16[16,64,128]{2,1,0:T(8,128)(2,1)S(1)} %get-tuple-element.21.refs_1_), channel_id=1, source_target_pairs={{0,1},{1,0},{2,3},{3,2},{4,5},{5,4},{6,7},{7,6},{8,9},{9,8},{10,11... | collective-permute-start | bytes 786440 | tf_op jit(solution)/shard_map/ppermute | solution.py:338
  73.6 7.3 %collective-permute-start.2 = (f32[32,2048]{1,0:T(8,128)S(1)}, f32[32,2048]{1,0:T(8,128)S(1)}, u32[]{:S(2)}, u32[]{:S(2)}) collective-permute-start(f32[32,2048]{1,0:T(8,128)S(1)} %get-tuple-element.25), channel_id=1, source_target_pairs={{0,1},{1,0},{2,3},{3,2},{4,5},{5,4},{6,7},{7,6},{8,9},{9,8},{10,11... | collective-permute-start | bytes 786440 | tf_op jit(solution)/shard_map/ppermute | solution.py:365
  76.8 7.4 %all-to-all-start.2 = ((f32[4,40,128]{2,1,0:T(8,128)}), f32[4,40,128]{2,1,0:T(8,128)S(1)}, u32[]{:S(2)}, u32[]{:S(2)}) async-start(f32[4,40,128]{2,1,0:T(8,128)} %rhs.1), calls=%async_computation.2 | async-start | bytes 163840 | tf_op jit(solution)/shard_map/all_to_all | solution.py:360

commit v9 on v8

--- a/solution.py
+++ b/solution.py
@@ -95,20 +95,16 @@
     x, _ = place(ring)
     part = 1 - x if away else x
     copies = [pltpu.make_async_copy(q_hbm.at[pl.ds(pl.multiple_of(part * rows, rows), rows)], q_ref, sem.at[0])]
-    cuts = [pl.ds(0, tokens // 4), pl.ds(tokens // 4, tokens - tokens // 4)]
-    copies += [pltpu.make_async_copy(k_hbm.at[cut], k_ref.at[cut], sem.at[1 + n]) for n, cut in enumerate(cuts)]
-    copies.append(pltpu.make_async_copy(v_hbm, v_ref, sem.at[3]))
+    copies += [pltpu.make_async_copy(k_hbm, k_ref, sem.at[1]), pltpu.make_async_copy(v_hbm, v_ref, sem.at[2])]
     for copy in copies:
         copy.start()
     copies[0].wait()
     copies[1].wait()
+    if fetch is not None:
+        fetch.wait()
     q = q_ref[...]
     mx = None
     for a in range(0, tokens, step):
-        if a == tokens // 4:
-            copies[2].wait()
-            if fetch is not None:
-                fetch.wait()
         s = lax.dot_general(k_ref[a : a + step, :], q, NT, preferred_element_type=F32)
         s_ref[a : a + step, :] = s
         top = jnp.max(s.reshape(step // 8, 8, rows), axis=0)
@@ -117,7 +113,7 @@
     if pick is not None:
         pick()
     total, out = jnp.zeros((8, rows), F32), jnp.zeros((width, rows), F32)
-    copies[3].wait()
+    copies[2].wait()
     for a in range(0, tokens, step):
         p = jnp.exp2(s_ref[a : a + step, :] * c - mc)
         total = total + jnp.sum(p.reshape(step // 8, 8, rows), axis=0)
@@ -303,7 +299,7 @@
         pltpu.VMEM((tokens, width), BF16),
         pltpu.VMEM((tokens, width), BF16),
         pltpu.VMEM((tokens, part), F32),
-        pltpu.SemaphoreType.DMA((4,)),
+        pltpu.SemaphoreType.DMA((3,)),
     ]
     work = dict(flops=4 * part * tokens * width, exps=part * tokens, moved=tokens * width * 4, limit=60.0)
     away, picked = call(
@@ -338,7 +334,7 @@
     other = lax.ppermute(mine, "pb", swap)
     own, stat, gkeep, gsend = call(
         "features",
-        functools.partial(features_body, 256),
+        functools.partial(features_body, 512),
         [((2 * count, part), BF16), ((rows // 128, 128), F32), ((half, sel), F32), ((half, sel), F32)],
         (q, mine, other),
         after=(told,),

time: 85.5 us -> 85.5 us (level)
  no operation moved by 1% of the time
where the time goes in v9:
time: 85.5 us; the launch traced here: 84.9 us
  blocking collectives  33.6 us (39%)
  starting transfers between devices  26.1 us (31%)
  Pallas kernels  18.2 us (21%)
  waiting for transfers between devices  4.45 us (5%)
  other arithmetic  1.15 us (1%)
    all_to_all x1, blocking collectives, exchange(): return lax.all_to_all(x, 'ctx', 0, 0, axis_index_groups=rings, tiled=True)  33.6 us
    pallas_call x7, Pallas kernels, call(): pl.pallas_call(ordered, name=name, out_shape=[jax.ShapeDtypeStruct(s, d)...  18.2 us
    all_to_all x1, starting transfers between devices, exchange(): return lax.all_to_all(x, 'ctx', 0, 0, axis_index_groups=rings, tiled=True)  12.3 us
    all_to_all x1, starting transfers between devices, shards(): lax.all_to_all(send, ('ctx', 'pb'), 0, 0, axis_index_groups=quads, tiled=...  4.12 us
    ppermute x1, starting transfers between devices, shards(): came = lax.ppermute(away.astype(F16), 'ctx', across).astype(F32)  3.95 us
    ppermute x1, starting transfers between devices, shards(): other = lax.ppermute(mine, 'pb', swap)  3.4 us
    all_to_all x1, waiting for transfers between devices, shards(): lax.all_to_all(send, ('ctx', 'pb'), 0, 0, axis_index_groups=quads, tiled=...  3.3 us
    ppermute x1, starting transfers between devices, shards(): lax.ppermute(gsend, 'pb', swap)  2.28 us
  transfers between devices with their start and end apart: 5, of which 2 were waited for; matrix products, arithmetic and copies ran while one was open for 0% of the time, Pallas kernels for 13%

profile of v9, /device:TPU:1, one launch (start us, length us, event | category | flops | bytes accessed | tf_op | source)
XLA Modules:
  0.0 84.9 jit_solution(14266014436083163695)
XLA Ops:
  0.6 5.5 %away.1 = (f32[17,40,128]{2,1,0:T(8,128)}, f32[32,128]{1,0:T(8,128)}) custom-call(s32[1,64]{1,0:T(1,128)} %refs_0_.1, bf16[1024,128]{1,0:T(8,128)(2,1)} %bitcast.6, bf16[4096,128]{1,0:T(8,128)(2,1)} %bitcast.9, bf16[4096,128]{1,0:T(8,128)(2,1)} %bitcast.11), custom_call_target="tpu_custom_call" | custom-call | flops 1073741824 | bytes 2097152 | tf_op jit(solution)/shard_map/away/pallas_call | solution.py:28
  6.1 1.0 %convert_element_type.12 = f16[17,40,128]{2,1,0:T(8,128)(2,1)S(1)} convert(f32[17,40,128]{2,1,0:T(8,128)} %get-tuple-element.18) | non-fusion elementwise | flops 87040 | bytes 522240 | tf_op jit(solution)/shard_map/convert_element_type | solution.py:314
  7.1 4.0 %collective-permute-start = (f16[17,40,128]{2,1,0:T(8,128)(2,1)S(1)}, f16[17,40,128]{2,1,0:T(8,128)(2,1)S(1)}, u32[]{:S(2)}, u32[]{:S(2)}) collective-permute-start(f16[17,40,128]{2,1,0:T(8,128)(2,1)S(1)} %convert_element_type.12), channel_id=1, source_target_pairs={{0,256},{16,272},{32,288},{48,304},{64,320},{80,336},{96,352},{112... | collective-permute-start | bytes 522248 | tf_op jit(solution)/shard_map/ppermute | solution.py:314
  11.1 4.4 %home.1 = (f32[512,128]{1,0:T(8,128)S(1)}, f32[8,128]{1,0:T(8,128)S(1)}) custom-call(bf16[1024,128]{1,0:T(8,128)(2,1)} %bitcast.7, bf16[4096,128]{1,0:T(8,128)(2,1)} %bitcast.10, bf16[4096,128]{1,0:T(8,128)(2,1)} %bitcast.12), custom_call_target="tpu_custom_call" | custom-call | flops 1073741824 | bytes 2097152 | tf_op jit(solution)/shard_map/home/pallas_call | solution.py:28
  15.5 0.0 collective-permute-done
  15.5 0.0 copy-start
  15.5 0.7 copy-done
  16.2 0.2 pair.1
  16.4 0.1 convert_element_type.14
  16.5 33.6 %all_to_all.15 = f16[16,104,128]{2,1,0:T(8,128)(2,1)S(1)} all-to-all(f16[16,104,128]{2,1,0:T(8,128)(2,1)S(1)} %convert_element_type.14), channel_id=1, replica_groups={{192,208,224,240,0,16,32,48,64,80,96,112,128,144,160,176},{448,464,480,..., dimensions={0} | all-to-all | bytes 851968 | tf_op jit(solution)/shard_map/all_to_all | solution.py:295
  50.1 0.1 convert_element_type.15.refs_0_
  50.2 1.1 %settle.1 = (bf16[16,40,128]{2,1,0:T(8,128)(2,1)}, bf16[16,64,128]{2,1,0:T(8,128)(2,1)S(1)}) custom-call(f32[16,104,128]{2,1,0:T(8,128)S(1)} %convert_element_type.15.refs_0_), custom_call_target="tpu_custom_call" | custom-call | bytes 524288 | tf_op jit(solution)/shard_map/settle/pallas_call | solution.py:28
  51.2 12.3 %all-to-all-start.1 = ((bf16[16,40,128]{2,1,0:T(8,128)(2,1)}), bf16[16,40,128]{2,1,0:T(8,128)(2,1)S(1)}, u32[]{:S(2)}, u32[]{:S(2)}) async-start(bf16[16,40,128]{2,1,0:T(8,128)(2,1)} %get-tuple-element.20.refs_3_), calls=%async_computation.1 | async-start | bytes 327680 | tf_op jit(solution)/shard_map/all_to_all | solution.py:295
  63.6 3.4 %collective-permute-start.1 = (bf16[16,64,128]{2,1,0:T(8,128)(2,1)S(1)}, bf16[16,64,128]{2,1,0:T(8,128)(2,1)S(1)}, u32[]{:S(2)}, u32[]{:S(2)}) collective-permute-start(bf16[16,64,128]{2,1,0:T(8,128)(2,1)S(1)} %get-tuple-element.21.refs_1_), channel_id=1, source_target_pairs={{0,1},{1,0},{2,3},{3,2},{4,5},{5,4},{6,7},{7,6},{8,9},{9,8},{10,11... | collective-permute-start | bytes 786440 | tf_op jit(solution)/shard_map/ppermute | solution.py:334
  67.0 1.1 %collective-permute-done.1.refs_2_ = bf16[16,64,128]{2,1,0:T(8,128)(2,1)S(1)} collective-permute-done((bf16[16,64,128]{2,1,0:T(8,128)(2,1)S(1)}, bf16[16,64,128]{2,1,0:T(8,128)(2,1)S(1)}, u32[]{:S(2)}, u32[]{:S(2)}) %collective-permute-start.1) | collective-permute-done | bytes 262176 | tf_op jit(solution)/shard_map/ppermute | solution.py:334
  68.1 0.0 copy-done.1
  68.1 5.5 %features.1 = (bf16[128,512]{1,0:T(8,128)(2,1)S(1)}, f32[8,128]{1,0:T(8,128)S(1)}, f32[32,2048]{1,0:T(8,128)S(1)}, f32[32,2048]{1,0:T(8,128)S(1)}) custom-call(bf16[1024,128]{1,0:T(8,128)(2,1)S(1)} %bitcast.8, bf16[16,64,128]{2,1,0:T(8,128)(2,1)S(1)} %get-tuple-element.21.refs_1_, bf16[16,64,128]{2,1,0:T(8,128)(2,1)S(1)} %collective-permute-done.1.refs_2_, ...), custom_call_target="tpu_custom_call" | custom-call | flops 805306368 | bytes 1048576 | tf_op jit(solution)/shard_map/features/pallas_call | solution.py:28
  73.6 2.3 %collective-permute-start.2 = (f32[32,2048]{1,0:T(8,128)S(1)}, f32[32,2048]{1,0:T(8,128)S(1)}, u32[]{:S(2)}, u32[]{:S(2)}) collective-permute-start(f32[32,2048]{1,0:T(8,128)S(1)} %get-tuple-element.25), channel_id=1, source_target_pairs={{0,1},{1,0},{2,3},{3,2},{4,5},{5,4},{6,7},{7,6},{8,9},{9,8},{10,11... | collective-permute-start | bytes 786440 | tf_op jit(solution)/shard_map/ppermute | solution.py:361
  75.9 0.0 all-to-all-done.1.refs_0_
  75.9 0.8 rhs.1
  76.8 4.1 %all-to-all-start.2 = ((f32[4,40,128]{2,1,0:T(8,128)}), f32[4,40,128]{2,1,0:T(8,128)S(1)}, u32[]{:S(2)}, u32[]{:S(2)}) async-start(f32[4,40,128]{2,1,0:T(8,128)} %rhs.1), calls=%async_computation.2 | async-start | bytes 163840 | tf_op jit(solution)/shard_map/all_to_all | solution.py:356
  80.9 0.0 collective-permute-done.2.refs_3_
  80.9 3.3 %all-to-all-done.2.refs_0_ = f32[4,40,128]{2,1,0:T(8,128)S(1)} async-done(((f32[4,40,128]{2,1,0:T(8,128)}), f32[4,40,128]{2,1,0:T(8,128)S(1)}, u32[]{:S(2)}, u32[]{:S(2)}) %all-to-all-start.2) | async-done | bytes 81952 | tf_op jit(solution)/shard_map/all_to_all | solution.py:356
  84.2 0.7 last.1
  (2 shorter events, 0.0 us)
Async XLA Ops:
  7.1 8.4 %collective-permute-start = (f16[17,40,128]{2,1,0:T(8,128)(2,1)S(1)}, f16[17,40,128]{2,1,0:T(8,128)(2,1)S(1)}, u32[]{:S(2)}, u32[]{:S(2)}) collective-permute-start(f16[17,40,128]{2,1,0:T(8,128)(2,1)S(1)} %convert_element_type.12), channel_id=1, source_target_pairs={{0,256},{16,272},{32,288},{48,304},{64,320},{80,336},{96,352},{112... | collective-permute-start | bytes 522248 | tf_op jit(solution)/shard_map/ppermute | solution.py:314
  15.5 0.7 copy-start
  51.2 16.9 %copy-start.1 = (bf16[1,8,128,128]{3,2,1,0:T(8,128)(2,1)S(1)}, bf16[1,8,128,128]{3,2,1,0:T(8,128)(2,1)}, u32[]{:S(2)}) copy-start(bf16[1,8,128,128]{3,2,1,0:T(8,128)(2,1)} %param.4) | copy-start | bytes 786436
  51.2 24.7 %all-to-all-start.1 = ((bf16[16,40,128]{2,1,0:T(8,128)(2,1)}), bf16[16,40,128]{2,1,0:T(8,128)(2,1)S(1)}, u32[]{:S(2)}, u32[]{:S(2)}) async-start(bf16[16,40,128]{2,1,0:T(8,128)(2,1)} %get-tuple-element.20.refs_3_), calls=%async_computation.1 | async-start | bytes 327680 | tf_op jit(solution)/shard_map/all_to_all | solution.py:295
  63.6 4.5 %collective-permute-start.1 = (bf16[16,64,128]{2,1,0:T(8,128)(2,1)S(1)}, bf16[16,64,128]{2,1,0:T(8,128)(2,1)S(1)}, u32[]{:S(2)}, u32[]{:S(2)}) collective-permute-start(bf16[16,64,128]{2,1,0:T(8,128)(2,1)S(1)} %get-tuple-element.21.refs_1_), channel_id=1, source_target_pairs={{0,1},{1,0},{2,3},{3,2},{4,5},{5,4},{6,7},{7,6},{8,9},{9,8},{10,11... | collective-permute-start | bytes 786440 | tf_op jit(solution)/shard_map/ppermute | solution.py:334
  73.6 7.3 %collective-permute-start.2 = (f32[32,2048]{1,0:T(8,128)S(1)}, f32[32,2048]{1,0:T(8,128)S(1)}, u32[]{:S(2)}, u32[]{:S(2)}) collective-permute-start(f32[32,2048]{1,0:T(8,128)S(1)} %get-tuple-element.25), channel_id=1, source_target_pairs={{0,1},{1,0},{2,3},{3,2},{4,5},{5,4},{6,7},{7,6},{8,9},{9,8},{10,11... | collective-permute-start | bytes 786440 | tf_op jit(solution)/shard_map/ppermute | solution.py:361
  76.8 7.4 %all-to-all-start.2 = ((f32[4,40,128]{2,1,0:T(8,128)}), f32[4,40,128]{2,1,0:T(8,128)S(1)}, u32[]{:S(2)}, u32[]{:S(2)}) async-start(f32[4,40,128]{2,1,0:T(8,128)} %rhs.1), calls=%async_computation.2 | async-start | bytes 163840 | tf_op jit(solution)/shard_map/all_to_all | solution.py:356
